TPU v7x, 32 devices: a whole 2x2x4 slice. The times are simulated.
32 devices in a mesh: groups: 2 (over y), patch: 4 (over z), ccd: 4 (over x, core).
Axes of the slice: x: 2, y: 2, z: 4, core: 2. Of those that a mesh axis runs over, the one named last changes fastest.
Arguments:
- science: bfloat16 [512, 48, 128], P(('groups', 'patch', 'ccd')), parts along dimension 0
- strip_patch: int32 [512], P(('groups', 'patch', 'ccd')), parts along dimension 0, may hold values from 0 to 3, as said below
- strip_tile: int32 [512], P(('groups', 'patch', 'ccd')), parts along dimension 0, may hold values from 0 to 15
- strip_row: int32 [512], P(('groups', 'patch', 'ccd')), parts along dimension 0, may hold values from 0 to 3952
- row_count: int32 [512], P(('groups', 'patch', 'ccd')), parts along dimension 0, may hold values from 24 to 48
- template: bfloat16 [512, 80, 128], P(('groups', 'patch', 'ccd')), parts along dimension 0
- basis_rows: bfloat16 [14, 21], replicated, may hold values from -1.25 to 1.25
- basis_cols: bfloat16 [14, 21], replicated, may hold values from -1.25 to 1.25
- basis_order: int32 [14], replicated, may hold values from 0 to 2
Outputs:
- difference: bfloat16 [512, 48, 128], P(('groups', 'patch', 'ccd')), parts along dimension 0
There are 2 independent parts, one for each index of `groups`. A program takes and returns all parts, laid end to end along the dimension named above; an argument that names none is the same for every part. Nothing has to cross between parts.
Inputs may be any that keep to these rules, and one draw needn't show every extreme that they name: `strip_patch`: no more than 8 of one device's 16 strips intersect one patch, and in every draw some patch receives exactly 8 strips from every device.
All inputs are finite; a program needn't handle non-finite values.
Results may differ from a plain program's by a relative error of at most 0.0022.
Values may be sent and summed in bfloat16 or wider, within the bound.
No kernel may reach another device: no remote copies, remote signals or barrier semaphores. Data moves between devices by JAX's collectives and lax.ppermute only.
A program may use at most 128 MiB of HBM per device.

v0:
```python
import jax
import jax.numpy as jnp
import numpy as np
from jax import lax
from jax.sharding import PartitionSpec as P

PATCH_ROWS = 4000


term_powers = ((0, 0), (1, 0), (0, 1), (2, 0), (1, 1), (0, 2))
ridge_weight = 0.01
strip_block = 4
highest = lax.Precision.HIGHEST


def kernel_tables(basis_rows, basis_cols, strip_rows, tile_rows, columns):
    kernels, kernel_taps = basis_rows.shape
    middle = kernel_taps // 2
    margin = (tile_rows - strip_rows) // 2
    row_lag = jnp.arange(tile_rows)[None, :] - jnp.arange(strip_rows)[:, None] - margin + middle
    col_lag = jnp.arange(columns)[:, None] - jnp.arange(columns)[None, :] + middle
    row_table = jnp.zeros((kernels, strip_rows, tile_rows), jnp.float32)
    col_table = jnp.zeros((kernels, columns, columns), jnp.float32)
    for tap_index in range(kernel_taps):
        row_table = row_table + jnp.where(
            (row_lag == tap_index)[None],
            basis_rows[:, tap_index].astype(jnp.float32)[:, None, None],
            0.0,
        )
        col_table = col_table + jnp.where(
            (col_lag == tap_index)[None],
            basis_cols[:, tap_index].astype(jnp.float32)[:, None, None],
            0.0,
        )
    return (
        row_table.astype(jnp.bfloat16).reshape(kernels * strip_rows, tile_rows),
        col_table.astype(jnp.bfloat16),
    )


def convolve(tile_stack, row_table, col_table):
    kernels = col_table.shape[0]
    columns = col_table.shape[1]
    strip_rows = row_table.shape[0] // kernels
    smoothed = jnp.einsum(
        "ht,btc->bhc", row_table, tile_stack, preferred_element_type=jnp.float32
    ).astype(jnp.bfloat16)
    smoothed = smoothed.reshape(tile_stack.shape[0], kernels, strip_rows, columns)
    return jnp.einsum(
        "bnrc,ncd->bnrd", smoothed, col_table, preferred_element_type=jnp.float32
    ).astype(jnp.bfloat16)


def with_ones(convolved):
    ones_plane = jnp.ones(convolved.shape[:1] + (1,) + convolved.shape[2:], jnp.bfloat16)
    return jnp.concatenate([convolved, ones_plane], axis=1)


def positions(offsets, row_totals, occupied, strip_rows, columns):
    row_steps = jnp.arange(strip_rows, dtype=jnp.int32)
    vertical = (2 * (offsets[:, None] + row_steps[None, :]) + 1).astype(
        jnp.float32
    ) / PATCH_ROWS - 1.0
    across = (2 * jnp.arange(columns, dtype=jnp.int32) + 1).astype(jnp.float32) / columns - 1.0
    usable = ((row_steps[None, :] < row_totals[:, None]) & (occupied[:, None] > 0)).astype(
        jnp.float32
    )
    return (vertical, across, usable)


def strip_stats(image_stack, science, vertical, across, usable):
    row_mask = usable.astype(jnp.bfloat16)
    weighted = jnp.concatenate(
        [image_stack * row_mask[:, None, :, None], (science * row_mask[:, :, None])[:, None]],
        axis=1,
    )
    pieces = []
    for degree in range(5):
        scaled = ((across**degree)[None, None, None, :] * image_stack.astype(jnp.float32)).astype(
            jnp.bfloat16
        )
        pieces.append(
            jnp.einsum("bnrc,bkrc->brnk", scaled, weighted, preferred_element_type=jnp.float32)
        )
    products = jnp.concatenate(pieces, axis=2)
    vertical_powers = jnp.stack([vertical**degree for degree in range(5)], axis=1)
    return jnp.einsum("bar,brxk->baxk", vertical_powers, products, precision=highest)


def solve_patch(moments, basis_order):
    plane_count = moments.shape[2] - 1
    kernels = plane_count - 1
    term_count = len(term_powers)
    unknowns = term_count * plane_count
    term_of = np.arange(unknowns) // plane_count
    plane_of = np.arange(unknowns) % plane_count
    first_power = np.array([term_powers[entry][0] for entry in term_of])
    second_power = np.array([term_powers[entry][1] for entry in term_of])
    pair_up = first_power[:, None] + first_power[None, :]
    pair_side = second_power[:, None] + second_power[None, :]
    row_planes = np.broadcast_to(plane_of[:, None], (unknowns, unknowns))
    col_planes = np.broadcast_to(plane_of[None, :], (unknowns, unknowns))
    paired = moments[pair_up, pair_side * plane_count + row_planes, col_planes]
    normal = 0.5 * (paired + paired.T)
    target = moments[first_power, second_power * plane_count + plane_of, plane_count]
    degree_of = first_power + second_power
    selector = plane_of[:, None] == np.arange(kernels)[None, :]
    order_of = jnp.sum(jnp.where(selector, basis_order[None, :], 0), axis=1)
    active = jnp.where(plane_of == kernels, 1.0, (degree_of <= order_of).astype(jnp.float32))
    system = active[:, None] * active[None, :] * normal + jnp.diag(
        1.0 + ridge_weight * active * jnp.diagonal(normal)
    )
    factor = jnp.linalg.cholesky(system)
    halfway = lax.linalg.triangular_solve(
        factor, (active * target)[:, None], left_side=True, lower=True
    )
    solved = lax.linalg.triangular_solve(
        factor, halfway, left_side=True, lower=True, transpose_a=True
    )
    return solved[:, 0].reshape(term_count, plane_count)


def strip_model(image_stack, science, vertical, across, usable, coefficients):
    term_maps = jnp.stack(
        [
            vertical[:, :, None] ** up_power * across[None, None, :] ** side_power
            for up_power, side_power in term_powers
        ],
        axis=1,
    )
    weights_map = jnp.einsum("bjn,bjrc->bnrc", coefficients, term_maps, precision=highest)
    fitted = jnp.sum(weights_map * image_stack.astype(jnp.float32), axis=1)
    return (usable[:, :, None] * (science.astype(jnp.float32) - fitted)).astype(jnp.bfloat16)


def stats_and_planes(tile_stack, science, offsets, row_totals, occupied, tables):
    convolved = convolve(tile_stack, tables[0], tables[1])
    vertical, across, usable = positions(
        offsets, row_totals, occupied, science.shape[1], science.shape[2]
    )
    return (strip_stats(with_ones(convolved), science, vertical, across, usable), convolved)


def model_from(convolved, science, offsets, row_totals, occupied, coefficients):
    vertical, across, usable = positions(
        offsets, row_totals, occupied, science.shape[1], science.shape[2]
    )
    return strip_model(with_ones(convolved), science, vertical, across, usable, coefficients)


def window(source, start_row):
    return lax.dynamic_slice_in_dim(source, start_row, strip_block, 0)


def body(
    science,
    strip_patch,
    strip_tile,
    strip_row,
    row_count,
    template,
    basis_rows,
    basis_cols,
    basis_order,
):
    patches = lax.axis_size("patch")
    strips_here, strip_rows, columns = science.shape
    tile_rows = template.shape[1]
    kernels = basis_rows.shape[0]
    plane_count = kernels + 1
    capacity = max(2, 2 * strips_here // patches)
    slot_total = patches * capacity
    tables = kernel_tables(basis_rows, basis_cols, strip_rows, tile_rows, columns)
    patch_hot = (strip_patch[:, None] == jnp.arange(patches, dtype=jnp.int32)[None, :]).astype(
        jnp.int32
    )
    before = jnp.cumsum(patch_hot, axis=0) - patch_hot
    slot_index = strip_patch * capacity + jnp.sum(before * patch_hot, axis=1)
    details = jnp.stack([strip_tile, strip_row, row_count, jnp.ones_like(strip_tile)], axis=1)
    sent_details = jnp.zeros((slot_total, 4), jnp.int32).at[slot_index].set(details)
    sent_images = (
        jnp.zeros((slot_total, strip_rows, columns), jnp.bfloat16).at[slot_index].set(science)
    )
    got_images, got_details = (
        lax.all_to_all(
            sent_images.reshape(patches, capacity, strip_rows, columns),
            "patch",
            split_axis=0,
            concat_axis=0,
            tiled=True,
        ),
        lax.all_to_all(
            sent_details.reshape(patches, capacity, 4),
            "patch",
            split_axis=0,
            concat_axis=0,
            tiled=True,
        ),
    )
    got_images = got_images.reshape(slot_total, strip_rows, columns)
    got_details = got_details.reshape(slot_total, 4)
    occupied = got_details[:, 3]
    position = jnp.cumsum(occupied) - 1
    listing = (
        jnp.full((slot_total,), slot_total, jnp.int32)
        .at[jnp.where(occupied > 0, position, slot_total)]
        .set(jnp.arange(slot_total, dtype=jnp.int32), mode="drop")
    )
    block_count = (jnp.sum(occupied) + strip_block - 1) // strip_block

    def fetch_block(block_index):
        picked = window(listing, block_index * strip_block)
        inside = picked < slot_total
        clamped = jnp.minimum(picked, slot_total - 1)
        details_here = got_details[clamped]
        present = jnp.where(inside, details_here[:, 3], 0)
        return (
            picked,
            details_here,
            got_images[clamped],
            details_here[:, 1],
            details_here[:, 2],
            present,
        )

    def add_stats(block_index, carry):
        totals, stored = carry
        picked, details_here, images, offsets, row_totals, present = fetch_block(block_index)
        plates = template[jnp.clip(details_here[:, 0], 0, template.shape[0] - 1)]
        moments, convolved = stats_and_planes(plates, images, offsets, row_totals, present, tables)
        stored = lax.dynamic_update_slice_in_dim(stored, convolved, block_index * strip_block, 0)
        return (totals + jnp.sum(moments, axis=0), stored)

    start = (
        jnp.zeros((5, 5 * plane_count, plane_count + 1), jnp.float32),
        jnp.zeros((slot_total, kernels, strip_rows, columns), jnp.bfloat16),
    )
    totals, stored = lax.fori_loop(0, block_count, add_stats, start)
    summed = lax.psum(totals, "ccd")
    coefficients = solve_patch(summed, basis_order)
    spread = jnp.broadcast_to(coefficients[None], (strip_block,) + coefficients.shape)

    def add_difference(block_index, results):
        picked, details_here, images, offsets, row_totals, present = fetch_block(block_index)
        change = model_from(
            window(stored, block_index * strip_block), images, offsets, row_totals, present, spread
        )
        return results.at[picked].set(change, mode="drop")

    results = lax.fori_loop(
        0, block_count, add_difference, jnp.zeros((slot_total, strip_rows, columns), jnp.bfloat16)
    )
    returned = lax.all_to_all(
        results.reshape(patches, capacity, strip_rows, columns),
        "patch",
        split_axis=0,
        concat_axis=0,
        tiled=True,
    )
    return returned.reshape(slot_total, strip_rows, columns)[slot_index]


def solution(mesh):
    placed = (
        P(("groups", "patch", "ccd"), None, None),
        P(("groups", "patch", "ccd")),
        P(("groups", "patch", "ccd")),
        P(("groups", "patch", "ccd")),
        P(("groups", "patch", "ccd")),
        P(("groups", "patch", "ccd"), None, None),
        P(),
        P(),
        P(),
    )
    return jax.shard_map(
        body,
        mesh=mesh,
        in_specs=placed,
        out_specs=P(("groups", "patch", "ccd"), None, None),
        check_vma=False,
    )
```

profile of v0, /device:TPU:1, one launch (start us, length us, event | category | flops | bytes accessed | tf_op | source)
XLA Modules:
  0.0 852.0 jit_solution(13532093099650800451)
XLA Ops:
  4.5 5.4 all-to-all-start
  9.9 1.9 convert_reduce_fusion.41
  18.0 2.7 scatter_fusion.1
  20.7 4.5 all-to-all-start.1
  28.4 2.2 add_convert_fusion.1
  35.3 3.4 broadcast_in_dim.835
  38.8 228.4 %while.30 = (s32[]{:T(128)}, f32[5,75,16]{1,0,2:T(8,128)S(1)}, bf16[32,14,48,128]{3,2,0,1:T(8,128)(2,1)}, s32[]{:T(128)}, s32[32]{0:T(128)S(1)}, /*index=5*/s32[...) while((s32[]{:T(128)}, f32[5,75,16]{1,0,2:T(8,128)S(1)}, ...), condition=%wide.region_8.9_spmd.clone, body=%wide.region_7.8_spmd.clone.sunk | while | flops 230379360 | bytes 27205380 | solution.py:238
  39.7 1.5 gather_fusion.1
  41.6 4.5 constant_dynamic-update-slice_fusion.12
  47.3 1.6 gather_fusion.2
  51.8 2.2 fusion.199
  53.9 2.2 fusion.198
  56.1 2.1 fusion.195
  58.2 50.0 %concatenate.56 = f32[4,48,75,16]{3,2,1,0:T(8,128)} concatenate(f32[4,48,15,16]{3,2,1,0:T(8,128)} %fusion.195, f32[4,48,15,16]{3,2,1,0:T(8,128)} %fusion.198, f32[4,48,15,16]{3,2,1,0:T(8,128)} %fusion.199, f32[4,48,15,16]{3,2,1,0:T(8,128)S(1)} %fusion.200, f32[4,48,15,16]{3,2,1,0:T(8,128)S(1)} %fusion.201), dimensions={2} | concatenate | bytes 1843200 | tf_op jit(solution)/shard_map/while/body/concatenate | solution.py:85
  108.2 5.4 copy.197
  117.7 4.5 constant_dynamic-update-slice_fusion.12
  123.4 1.6 gather_fusion.2
  127.9 2.2 fusion.199
  130.1 2.2 fusion.198
  132.2 2.1 fusion.195
  134.4 50.0 %concatenate.56 = f32[4,48,75,16]{3,2,1,0:T(8,128)} concatenate(f32[4,48,15,16]{3,2,1,0:T(8,128)} %fusion.195, f32[4,48,15,16]{3,2,1,0:T(8,128)} %fusion.198, f32[4,48,15,16]{3,2,1,0:T(8,128)} %fusion.199, f32[4,48,15,16]{3,2,1,0:T(8,128)S(1)} %fusion.200, f32[4,48,15,16]{3,2,1,0:T(8,128)S(1)} %fusion.201), dimensions={2} | concatenate | bytes 1843200 | tf_op jit(solution)/shard_map/while/body/concatenate | solution.py:85
  184.3 5.4 copy.197
  191.9 1.5 gather_fusion.1
  193.9 4.5 constant_dynamic-update-slice_fusion.12
  199.6 1.6 gather_fusion.2
  204.0 2.2 fusion.199
  206.2 2.2 fusion.198
  208.4 2.1 fusion.195
  210.5 50.0 %concatenate.56 = f32[4,48,75,16]{3,2,1,0:T(8,128)} concatenate(f32[4,48,15,16]{3,2,1,0:T(8,128)} %fusion.195, f32[4,48,15,16]{3,2,1,0:T(8,128)} %fusion.198, f32[4,48,15,16]{3,2,1,0:T(8,128)} %fusion.199, f32[4,48,15,16]{3,2,1,0:T(8,128)S(1)} %fusion.200, f32[4,48,15,16]{3,2,1,0:T(8,128)S(1)} %fusion.201), dimensions={2} | concatenate | bytes 1843200 | tf_op jit(solution)/shard_map/while/body/concatenate | solution.py:85
  260.5 5.4 copy.197
  267.2 88.7 %psum.7 = f32[5,75,16]{1,0,2:T(8,128)S(1)} all-reduce(f32[5,75,16]{1,0,2:T(8,128)S(1)} %get-tuple-element.288), channel_id=1, replica_groups=mesh['groups'=2,'patch'=4,'ccd'=4] {'ccd'}, use_global_device_ids=true, to_apply=%region_10.11 | all-reduce | flops 6000 | bytes 48000 | tf_op jit(solution)/shard_map/psum | solution.py:239
  355.9 73.9 %gather_fusion.5 = f32[8100]{0:T(1024)S(1)} fusion(f32[5,75,16]{1,0,2:T(8,128)S(1)} %psum.7, s32[8100]{0:T(1024)S(1)} %copy-done), kind=kCustom, calls=%fused_computation.5 | custom fusion | bytes 162000 | tf_op jit(solution)/shard_map/gather | solution.py:103
  430.1 1.7 gather_fusion.6
  431.9 8.2 cholesky.16
  441.5 6.9 custom-call.8
  448.4 1.7 gather_fusion.7
  451.6 30.0 %while.31 = (s32[]{:T(128)}, bf16[32,48,128]{2,1,0:T(8,128)(2,1)}, s32[]{:T(128)}, s32[32]{0:T(128)S(1)}, s32[32,4]{1,0:T(8,128)S(1)}, /*index=5*/bf16[32,48,128...) while((s32[]{:T(128)}, bf16[32,48,128]{2,1,0:T(8,128)(2,1)}, ...), condition=%wide.region_16.17_spmd.clone, body=%wide.region_13.16_spmd.clone.sunk | while | flops 27750700 | bytes 6353595 | solution.py:250
  456.1 1.7 fusion.207
  458.0 1.6 gather_fusion.4
  459.6 1.9 scatter_fusion
  466.1 1.7 fusion.207
  468.0 1.6 gather_fusion.4
  469.6 1.9 scatter_fusion
  476.1 1.7 fusion.207
  478.0 1.6 gather_fusion.4
  479.6 1.9 scatter_fusion
  481.6 357.9 %all-to-all-start.2 = ((bf16[4,8,48,128]{3,2,1,0:T(8,128)(2,1)}), bf16[4,8,48,128]{3,2,1,0:T(8,128)(2,1)S(1)}, u32[]{:S(2)}, u32[]{:S(2)}) async-start(bf16[4,8,48,128]{3,2,1,0:T(8,128)(2,1)} %bitcast.36), calls=%async_computation.2 | async-start | bytes 786432 | tf_op jit(solution)/shard_map/all_to_all | solution.py:253
  839.5 11.2 %all-to-all-done.2 = bf16[4,8,48,128]{3,2,1,0:T(8,128)(2,1)S(1)} async-done(((bf16[4,8,48,128]{3,2,1,0:T(8,128)(2,1)}), bf16[4,8,48,128]{3,2,1,0:T(8,128)(2,1)S(1)}, u32[]{:S(2)}, u32[]{:S(2)}) %all-to-all-start.2) | async-done | bytes 393248 | tf_op jit(solution)/shard_map/all_to_all | solution.py:253
  (248 shorter events, 57.7 us)
Async XLA Ops:
  4.5 16.2 %all-to-all-start = ((s32[4,8,4]{1,2,0:T(4,128)}), s32[4,8,4]{1,2,0:T(4,128)S(1)}, u32[]{:S(2)}, u32[]{:S(2)}) async-start(s32[4,8,4]{1,2,0:T(4,128)} %copy.124), calls=%async_computation | async-start | bytes 16384 | tf_op jit(solution)/shard_map/all_to_all | solution.py:192
  13.8 18.2 %copy-start.6 = (pred[90,14]{0,1:T(8,128)(4,1)S(1)}, pred[90,14]{0,1:T(8,128)(4,1)}, u32[]{:S(2)}) copy-start(pred[90,14]{0,1:T(8,128)(4,1)} %constant.365.clone) | copy-start | bytes 3784
  13.8 18.2 %copy-start.7 = (s32[14]{0:T(128)S(1)}, s32[14]{0:T(128)}, u32[]{:S(2)}) copy-start(s32[14]{0:T(128)} %param.34) | copy-start | bytes 172
  13.8 18.3 %copy-start.3 = (bf16[14,21]{1,0:T(8,128)(2,1)S(1)}, bf16[14,21]{1,0:T(8,128)(2,1)}, u32[]{:S(2)}) copy-start(bf16[14,21]{1,0:T(8,128)(2,1)} %param.33) | copy-start | bytes 1768
  20.7 14.6 %all-to-all-start.1 = ((bf16[4,8,48,128]{3,2,1,0:T(8,128)(2,1)}), bf16[4,8,48,128]{3,2,1,0:T(8,128)(2,1)}, u32[]{:S(2)}, u32[]{:S(2)}) async-start(bf16[4,8,48,128]{3,2,1,0:T(8,128)(2,1)} %bitcast.4), calls=%async_computation.1 | async-start | bytes 786432 | tf_op jit(solution)/shard_map/all_to_all | solution.py:185
  53.9 2.2 copy-start.1
  130.1 2.2 copy-start.1
  206.2 2.2 copy-start.1
  267.2 88.7 %copy-start = (s32[8100]{0:T(1024)S(1)}, s32[8100]{0:T(1024)}, u32[]{:S(2)}) copy-start(s32[8100]{0:T(1024)} %constant.447) | copy-start | bytes 97204
  355.9 75.9 %copy-start.4 = (s32[90]{0:T(128)S(1)}, s32[90]{0:T(128)}, u32[]{:S(2)}) copy-start(s32[90]{0:T(128)} %constant.366.clone) | copy-start | bytes 1084
  355.9 75.9 %copy-start.5 = (pred[90]{0:T(512)(128)(4,1)S(1)}, pred[90]{0:T(512)(128)(4,1)}, u32[]{:S(2)}) copy-start(pred[90]{0:T(512)(128)(4,1)} %constant.367.clone) | copy-start | bytes 274
  355.9 92.5 %copy-start.2 = (s32[90]{0:T(128)S(1)}, s32[90]{0:T(128)}, u32[]{:S(2)}) copy-start(s32[90]{0:T(128)} %constant.459) | copy-start | bytes 1084
  481.6 369.2 %all-to-all-start.2 = ((bf16[4,8,48,128]{3,2,1,0:T(8,128)(2,1)}), bf16[4,8,48,128]{3,2,1,0:T(8,128)(2,1)S(1)}, u32[]{:S(2)}, u32[]{:S(2)}) async-start(bf16[4,8,48,128]{3,2,1,0:T(8,128)(2,1)} %bitcast.36), calls=%async_computation.2 | async-start | bytes 786432 | tf_op jit(solution)/shard_map/all_to_all | solution.py:253
where the time goes:
time: 865 us; the launch traced here: 852 us
  starting transfers between devices  368 us (43%)
  local copies, waits for them, and re-layouts  292 us (34%)
  blocking collectives  88.7 us (10%)
  matrix products  48.6 us (6%)
  other arithmetic  42.3 us (5%)
  waiting for transfers between devices  11.2 us (1%)
    all_to_all x1, starting transfers between devices, body(): lax.all_to_all(results.reshape(patches, capacity, strip_rows, columns), '...  358 us
    concatenate x6, local copies, waits for them, and re-layouts, strip_stats(): products = jnp.concatenate(pieces, axis=2)  166 us
    psum x1, blocking collectives, body(): summed = lax.psum(totals, 'ccd')  88.7 us
    gather x3, local copies, waits for them, and re-layouts, solve_patch(): paired = moments[pair_up, pair_side * plane_count + row_planes, col_planes]  74.2 us
    dot_general x15, matrix products, strip_stats(): jnp.einsum('bnrc,bkrc->brnk', scaled, weighted, preferred_element_type=jn...  25.4 us
  transfers between devices with their start and end apart: 3, of which 1 were waited for; matrix products, arithmetic and copies ran while one was open for 2% of the time, Pallas kernels for 0%

commit v1 on v0

v1 whole, which is shorter than its diff:
```python
import functools

import jax
import jax.numpy as jnp
from jax import lax
from jax.experimental import pallas as pl
from jax.experimental.pallas import tpu as pltpu
from jax.sharding import PartitionSpec as P

PATCH_ROWS = 4000
RIDGE = 0.01
TERMS = ((0, 0), (2, 0), (0, 2), (1, 0), (0, 1), (1, 1))
LEFT = 3
BATCH = 4
VMEM = pl.BlockSpec(memory_space=pltpu.VMEM)
SMEM = pl.BlockSpec(memory_space=pltpu.SMEM)
F32, BF16, I32 = jnp.float32, jnp.bfloat16, jnp.int32


def block_of(a, b):
    want = (TERMS[a][0] + TERMS[b][0], TERMS[a][1] + TERMS[b][1])
    for left in range(LEFT):
        for right in range(len(TERMS)):
            if (TERMS[left][0] + TERMS[right][0], TERMS[left][1] + TERMS[right][1]) == want:
                return left, right
    raise ValueError(want)


def params():
    return pltpu.CompilerParams(vmem_limit_bytes=56 * 1024 * 1024)


def tables_kernel(rows_ref, cols_ref, row_out, col_out, *, kernels, taps, rows, tile_rows, columns):
    middle = taps // 2
    lag = (tile_rows - rows) // 2 - middle
    cc = lax.broadcasted_iota(I32, (columns, columns), 0)
    dd = lax.broadcasted_iota(I32, (columns, columns), 1)
    band = (cc - dd <= middle) & (dd - cc <= middle)
    for n in range(kernels):
        taps_n = jnp.broadcast_to(rows_ref[n : n + 1, :], (rows, 128))
        moved = pltpu.roll(taps_n, lag, 1, stride=1, stride_axis=0)
        row_out[n * rows : (n + 1) * rows, :] = moved[:, :tile_rows].astype(BF16)
        taps_n = jnp.broadcast_to(cols_ref[n : n + 1, :], (columns, columns))
        moved = pltpu.roll(taps_n, 0, 1, stride=1, stride_axis=0)
        col_out[n] = jnp.where(band, moved, 0.0).astype(BF16)


def make_tables(basis_rows, basis_cols, rows, tile_rows, columns):
    kernels, taps = basis_rows.shape
    pad = ((0, 0), (0, 128 - taps))
    return pl.pallas_call(
        functools.partial(
            tables_kernel,
            kernels=kernels,
            taps=taps,
            rows=rows,
            tile_rows=tile_rows,
            columns=columns,
        ),
        out_shape=(
            jax.ShapeDtypeStruct((kernels * rows, tile_rows), BF16),
            jax.ShapeDtypeStruct((kernels, columns, columns), BF16),
        ),
        in_specs=[VMEM, VMEM],
        out_specs=(VMEM, VMEM),
        compiler_params=params(),
        name="tables",
    )(
        jnp.pad(basis_rows.astype(F32), pad),
        jnp.roll(jnp.pad(basis_cols.astype(F32)[:, ::-1], pad), -(taps // 2), axis=1),
    )


def select_kernel(me_ref, *refs, shifts, strips, tiles):
    codes, template, outs = refs[:shifts], refs[shifts], refs[shifts + 1 :]
    low = me_ref[0] * tiles
    for code_ref, out in zip(codes, outs):

        def step(s, count, code_ref=code_ref, out=out):
            tile = code_ref[s] - low
            hit = (tile >= 0) & (tile < tiles)

            @pl.when(hit)
            def _():
                out[count] = template[tile]

            return count + hit.astype(I32)

        lax.fori_loop(0, strips, step, jnp.int32(0))


def select_tiles(me, codes, template, capacity):
    shifts = len(codes)
    tiles, tile_rows, columns = template.shape
    return pl.pallas_call(
        functools.partial(select_kernel, shifts=shifts, strips=codes[0].shape[0], tiles=tiles),
        out_shape=[jax.ShapeDtypeStruct((capacity, tile_rows, columns), BF16)] * shifts,
        in_specs=[SMEM] + [SMEM] * shifts + [VMEM],
        out_specs=[VMEM] * shifts,
        compiler_params=params(),
        name="select",
    )(me, *codes, template)


def list_group(code_ref, listing, patch, tiles, strips):
    low = patch * tiles

    def step(s, count):
        tile = code_ref[s] - low
        hit = (tile >= 0) & (tile < tiles)

        @pl.when(hit)
        def _():
            listing[count] = s

        return count + hit.astype(I32)

    return lax.fori_loop(0, strips, step, jnp.int32(0))


def across_rows(columns):
    c = lax.broadcasted_iota(I32, (8, columns), 1)
    return (2 * c + 1).astype(F32) / columns - 1.0


def moments_kernel(
    me_ref,
    code_ref,
    row_ref,
    good_ref,
    plates,
    science,
    row_table,
    col_table,
    *refs,
    first,
    groups,
    capacity,
    own,
    patches,
    ccds,
    share,
    kernels,
    planes,
    earlier,
):
    before = refs[:earlier]
    outs = refs[earlier : len(refs) - 3]
    p32, listing, sums = refs[len(refs) - 3 :]
    last = len(outs) > 2
    planes_out = outs[0]
    strips, rows, columns = science.shape
    tiles = me_ref[2]
    me, ccd = me_ref[0], me_ref[1]
    span = rows * planes
    unknowns = len(TERMS) * planes
    if kernels + 2 < planes:
        p32[...] = jnp.zeros_like(p32)
    for b in range(BATCH):
        p32[pl.ds(b * span + kernels, rows, stride=planes), :] = jnp.ones((rows, columns), F32)
    across = jnp.concatenate([across_rows(columns)] * (planes // 8), axis=0)
    across2 = across * across
    step_rows = 8

    def gram(b, strip, slot):
        offset = row_ref[strip]
        good = good_ref[strip]
        total = jnp.zeros((LEFT * planes, unknowns), F32)
        for chunk in range(rows // step_rows):
            pieces = [[] for _ in TERMS]
            for r in range(chunk * step_rows, (chunk + 1) * step_rows):
                at = r * planes
                rounded = p32[b * span + at : b * span + at + planes, :].astype(BF16)
                planes_out[slot, at : at + planes, :] = rounded
                value = rounded.astype(F32)
                v = (2 * (offset + r) + 1).astype(F32) * (1.0 / PATCH_ROWS) - 1.0
                value = value * jnp.where(r < good, 1.0, 0.0)
                with_u = value * across
                pieces[0].append(value.astype(BF16))
                pieces[1].append((value * (v * v)).astype(BF16))
                pieces[2].append((value * across2).astype(BF16))
                pieces[3].append((value * v).astype(BF16))
                pieces[4].append(with_u.astype(BF16))
                pieces[5].append((with_u * v).astype(BF16))
            wide = [jnp.concatenate(part, axis=1) for part in pieces]
            right = jnp.concatenate(wide, axis=0)
            left = jnp.concatenate(wide[:LEFT], axis=0)
            total = total + lax.dot_general(
                left, right, (((1,), (1,)), ((), ())), preferred_element_type=F32
            )
        return total

    def group(g, carry):
        patch = me + (first + g)
        patch = jnp.where(patch >= patches, patch - patches, patch)
        count = list_group(code_ref, listing, patch, tiles, strips)
        sums[first + g] = jnp.zeros((LEFT * planes, 128), F32)

        def batch(t, carry):
            slots = [t * BATCH + b for b in range(BATCH)]
            chosen = [listing[jnp.minimum(slot, count - 1)] for slot in slots]
            if own:
                stack = [plates[code_ref[s] - patch * tiles] for s in chosen]
            else:
                stack = [plates[g * capacity + jnp.minimum(slot, count - 1)] for slot in slots]
            smoothed = jnp.dot(
                row_table[...], jnp.concatenate(stack, axis=1), preferred_element_type=F32
            ).astype(BF16)
            for n in range(kernels):
                part = smoothed[n * rows : (n + 1) * rows]
                lhs = jnp.concatenate(
                    [part[:, b * columns : (b + 1) * columns] for b in range(BATCH)], axis=0
                )
                convolved = jnp.dot(lhs, col_table[n], preferred_element_type=F32)
                for b in range(BATCH):
                    p32[pl.ds(b * span + n, rows, stride=planes), :] = convolved[
                        b * rows : (b + 1) * rows
                    ]
            for b in range(BATCH):
                p32[pl.ds(b * span + planes - 1, rows, stride=planes), :] = science[
                    chosen[b]
                ].astype(F32)
            for b in range(BATCH):

                @pl.when(slots[b] < count)
                def _(b=b):
                    total = gram(b, chosen[b], g * capacity + slots[b])
                    sums[first + g, :, :unknowns] += total

            return carry

        lax.fori_loop(0, (count + BATCH - 1) // BATCH, batch, 0)
        return carry

    if groups == 1:
        group(0, 0)
    else:
        lax.fori_loop(0, groups, group, 0)
    if not last:
        outs[1][...] = sums[first : first + groups]
    else:
        at = 0
        for ref in before:
            for i in range(ref.shape[0]):
                sums[at] = ref[i]
                at += 1
        for e in range(ccds):
            owner = ccd + e
            owner = jnp.where(owner >= ccds, owner - ccds, owner)
            for k in range(share):
                d = jnp.minimum(k * ccds + owner, patches - 1) - me
                d = jnp.where(d < 0, d + patches, d)
                outs[1 + e][k] = sums[d]


def moments_call(scalars, plates, science, tables, before, first, groups, own, last, sizes):
    capacity, patches, ccds, share, kernels, planes = sizes
    strips, rows, columns = science.shape
    held = groups * capacity
    sum_shape = (LEFT * planes, 128)
    if last:
        sum_outs = [jax.ShapeDtypeStruct((share,) + sum_shape, F32)] * ccds
    else:
        sum_outs = [jax.ShapeDtypeStruct((groups,) + sum_shape, F32)]
    return pl.pallas_call(
        functools.partial(
            moments_kernel,
            first=first,
            groups=groups,
            capacity=capacity,
            own=own,
            patches=patches,
            ccds=ccds,
            share=share,
            kernels=kernels,
            planes=planes,
            earlier=len(before),
        ),
        out_shape=[jax.ShapeDtypeStruct((held, rows * planes, columns), BF16)] + sum_outs,
        in_specs=[SMEM] * 4 + [VMEM] * (4 + len(before)),
        out_specs=[VMEM] * (1 + len(sum_outs)),
        scratch_shapes=[
            pltpu.VMEM((BATCH * rows * planes, columns), F32),
            pltpu.SMEM((strips,), I32),
            pltpu.VMEM((max(patches, ccds),) + sum_shape, F32),
        ],
        compiler_params=params(),
        cost_estimate=pl.CostEstimate(
            flops=int(4e9) * groups // patches, bytes_accessed=1 << 20, transcendentals=0
        ),
        name="moments",
    )(*scalars, plates, science, *tables, *before)


def solve_kernel(order_ref, *refs, kernels, planes, share):
    parts, out = refs[:-1], refs[-1]
    terms = len(TERMS)
    size = terms * planes
    lane = lax.broadcasted_iota(I32, (size, 128), 1)
    sub = lax.broadcasted_iota(I32, (size, 128), 0)

    def activity(index):
        plane, term = index % planes, index // planes
        order = jnp.zeros_like(index)
        for i in range(kernels):
            order = jnp.where(plane == i, order_ref[i], order)
        degree = jnp.zeros_like(index)
        for t, powers in enumerate(TERMS):
            degree = jnp.where(term == t, powers[0] + powers[1], degree)
        wanted = (plane == kernels) | ((plane < kernels) & (degree <= order))
        return jnp.where(wanted & (index < size), 1.0, 0.0)

    active_row = activity(lane[:8])
    active_row = jnp.concatenate([active_row] * (size // 8), axis=0)
    active_col = activity(sub)
    lane16 = lane[:planes]
    row8 = lax.broadcasted_iota(I32, (8, 128), 0)
    for k in range(share):
        moments = parts[0][k]
        for ref in parts[1:]:
            moments = moments + ref[k]
        rows = []
        for a in range(terms):
            row = jnp.zeros((planes, 128), F32)
            for b in range(terms):
                left, right = block_of(a, b)
                piece = moments[left * planes : (left + 1) * planes]
                if b != right:
                    piece = pltpu.roll(piece, ((b - right) * planes) % 128, 1)
                row = jnp.where(lane16 // planes == b, piece, row)
            rows.append(row)
        paired = jnp.concatenate(rows, axis=0)
        target = pltpu.roll(paired, size - (planes - 1), 1)
        masked = active_row * active_col * paired
        system = jnp.where(lane == sub, masked + (1.0 + RIDGE * masked), masked)
        system = jnp.where(lane == size, active_col * target, system)
        blocks = [system[8 * m : 8 * m + 8] for m in range(size // 8)]
        for x in range(size):
            if x % planes > kernels:
                continue
            at, inner = divmod(x, 8)
            row = jnp.broadcast_to(blocks[at][inner : inner + 1], (8, 128))
            pivot = jnp.broadcast_to(row[:, x : x + 1], (8, 128))
            scaled = row * (1.0 / pivot)
            for m in range(size // 8):
                column = jnp.broadcast_to(blocks[m][:, x : x + 1], (8, 128))
                new = blocks[m] - column * scaled
                if m == at:
                    new = jnp.where(row8 == inner, scaled, new)
                blocks[m] = new
        answer = jnp.concatenate(blocks, axis=0)
        answer = jnp.broadcast_to(answer[:, size : size + 1], (size, 128))
        answer = jnp.where(sub % planes == lane % planes, answer, 0.0)
        lines = [
            jnp.sum(answer[t * planes : (t + 1) * planes], axis=0, keepdims=True)
            for t in range(terms)
        ]
        lines.append(jnp.zeros((8 - terms, 128), F32))
        out[k] = jnp.concatenate(lines, axis=0)


def solve(order, parts, kernels, planes):
    share = parts[0].shape[0]
    return pl.pallas_call(
        functools.partial(solve_kernel, kernels=kernels, planes=planes, share=share),
        out_shape=jax.ShapeDtypeStruct((share, 8, 128), F32),
        in_specs=[SMEM] + [VMEM] * len(parts),
        out_specs=VMEM,
        compiler_params=params(),
        name="solve",
    )(order, *parts)


def difference_kernel(
    me_ref,
    code_ref,
    row_ref,
    good_ref,
    *refs,
    calls,
    capacity,
    patches,
    ccds,
    share,
    kernels,
    planes,
    tall,
):
    coefs, stacks = refs[:ccds], refs[ccds : ccds + len(calls)]
    out, table, listing = refs[ccds + len(calls) :]
    strips, rows, columns = out.shape
    me, ccd, tiles = me_ref[0], me_ref[1], me_ref[2]
    for e in range(ccds):
        owner = ccd + e
        owner = jnp.where(owner >= ccds, owner - ccds, owner)
        for k in range(share):
            table[k * ccds + owner] = coefs[e][k]
    across = jnp.concatenate([across_rows(columns)] * (tall // 8), axis=0)
    across2 = across * across
    width = tall * planes
    lane = lax.broadcasted_iota(I32, (tall, width), 1)
    sub = lax.broadcasted_iota(I32, (tall, width), 0)
    diagonal = lane // planes == sub
    is_science = diagonal & (lane % planes == planes - 1)
    sub_out = lax.broadcasted_iota(I32, (tall, columns), 0)

    def pieces(value):
        high = value.astype(BF16)
        rest = value - high.astype(F32)
        middle = rest.astype(BF16)
        return high, middle, (rest - middle.astype(F32)).astype(BF16)

    for (first, groups), stack in zip(calls, stacks):

        def group(g, carry, first=first, stack=stack):
            patch = me + (first + g)
            patch = jnp.where(patch >= patches, patch - patches, patch)
            count = list_group(code_ref, listing, patch, tiles, strips)
            block = table[patch]
            coef = [
                jnp.broadcast_to(
                    jnp.concatenate([block[t : t + 1]] * (width // 128), axis=1), (tall, width)
                )
                for t in range(len(TERMS))
            ]

            def strip_step(j, carry):
                strip = listing[j]
                offset, good = row_ref[strip], good_ref[strip]
                for h in range(rows // tall):
                    v = (2 * (offset + h * tall + sub) + 1).astype(F32) / PATCH_ROWS - 1.0
                    plain = coef[0] + v * (coef[3] + v * coef[1])
                    once = coef[4] + v * coef[5]
                    twice = coef[2]
                    plain = jnp.where(diagonal, -plain, 0.0)
                    plain = jnp.where(is_science, 1.0, plain)
                    once = jnp.where(diagonal, -once, 0.0)
                    twice = jnp.where(diagonal, -twice, 0.0)
                    lhs = jnp.concatenate([*pieces(plain), *pieces(once), *pieces(twice)], axis=0)
                    rhs = stack[g * capacity + j, h * width : (h + 1) * width, :]
                    got = jnp.dot(lhs, rhs, preferred_element_type=F32)
                    part = [got[i * tall : (i + 1) * tall] for i in range(9)]
                    value = (
                        (part[0] + (part[1] + part[2]))
                        + across * (part[3] + (part[4] + part[5]))
                        + across2 * (part[6] + (part[7] + part[8]))
                    )
                    value = jnp.where(h * tall + sub_out < good, value, 0.0)
                    out[strip, h * tall : (h + 1) * tall, :] = value.astype(BF16)
                return carry

            lax.fori_loop(0, count, strip_step, 0)
            return carry

        if groups == 1:
            group(0, 0)
        else:
            lax.fori_loop(0, groups, group, 0)


def difference(scalars, coefs, stacks, calls, shape, sizes):
    capacity, patches, ccds, share, kernels, planes = sizes
    strips, rows, columns = shape
    return pl.pallas_call(
        functools.partial(
            difference_kernel,
            calls=calls,
            capacity=capacity,
            patches=patches,
            ccds=ccds,
            share=share,
            kernels=kernels,
            planes=planes,
            tall=16,
        ),
        out_shape=jax.ShapeDtypeStruct(shape, BF16),
        in_specs=[SMEM] * 4 + [VMEM] * (len(coefs) + len(stacks)),
        out_specs=VMEM,
        scratch_shapes=[
            pltpu.VMEM((share * ccds, 8, 128), F32),
            pltpu.SMEM((strips,), I32),
        ],
        compiler_params=params(),
        name="difference",
    )(*scalars, *coefs, *stacks)


def shifted(value, axis, shift):
    size = lax.axis_size(axis)
    return lax.ppermute(value, axis, [(i, (i + shift) % size) for i in range(size)])


def body(
    science,
    strip_patch,
    strip_tile,
    strip_row,
    row_count,
    template,
    basis_rows,
    basis_cols,
    basis_order,
):
    patches, ccds = lax.axis_size("patch"), lax.axis_size("ccd")
    strips, rows, columns = science.shape
    tiles, tile_rows = template.shape[:2]
    kernels = basis_rows.shape[0]
    planes = -(-(kernels + 2) // 16) * 16
    capacity = max(2, 2 * strips // patches)
    share = -(-patches // ccds)
    sizes = (capacity, patches, ccds, share, kernels, planes)
    me = jnp.stack(
        [lax.axis_index("patch"), lax.axis_index("ccd"), jnp.int32(tiles)]
    ).astype(I32)
    code = strip_patch * tiles + strip_tile
    scalars = (me, code, strip_row, row_count)
    if patches <= 8:
        codes = [shifted(code, "patch", d) for d in range(1, patches)]
    else:
        everyone = lax.all_gather(code, "patch")
        mine = lax.axis_index("patch")
        codes = [
            lax.dynamic_index_in_dim(
                everyone, lax.rem(mine - d + patches, patches), 0, keepdims=False
            )
            for d in range(1, patches)
        ]
    tables = make_tables(basis_rows, basis_cols, rows, tile_rows, columns)
    chosen = select_tiles(me, codes, template, capacity)
    arrived = [shifted(tile, "patch", patches - d) for d, tile in enumerate(chosen, 1)]
    if patches <= 8:
        calls = [(d, 1) for d in range(patches)]
        plates = [template] + arrived
    else:
        calls = [(0, 1), (1, patches - 1)]
        plates = [template, jnp.concatenate(arrived, axis=0)]
    stacks, sums = [], []
    for (first, groups), plate in zip(calls, plates):
        last = first + groups == patches
        got = moments_call(
            scalars, plate, science, tables, sums if last else [], first, groups, first == 0, last,
            sizes,
        )
        stacks.append(got[0])
        if not last:
            sums.append(got[1])
        else:
            scattered = got[1:]
    mine = scattered[0]
    for e in range(1, ccds):
        mine = mine + shifted(scattered[e], "ccd", e)
    parts = [mine] + [shifted(mine, "patch", d) for d in range(1, patches)]
    coefficients = solve(basis_order, parts, kernels, planes)
    coefs = [coefficients] + [shifted(coefficients, "ccd", ccds - e) for e in range(1, ccds)]
    return difference(scalars, coefs, stacks, tuple(calls), science.shape, sizes)


def solution(mesh):
    spread = P(("groups", "patch", "ccd"))
    return jax.shard_map(
        body,
        mesh=mesh,
        in_specs=(spread,) * 6 + (P(), P(), P()),
        out_specs=spread,
        check_vma=False,
    )
```

time: 865 us -> 92 us (0.11); the launches traced: 852 us -> 90.5 us
  starting transfers between devices: 368 us -> 20.3 us
  local copies, waits for them, and re-layouts: 292 us -> 5.79 us
  blocking collectives: 88.7 us -> 0 us
  Pallas kernels: 0 us -> 49.5 us
  matrix products: 48.6 us -> 0 us
  other arithmetic: 42.3 us -> 3.99 us
    all_to_all x3 -> x0, starting transfers between devices: 368 us -> none  [the longest x1 358 us: body(): lax.all_to_all(results.reshape(patches, capacity, strip_rows, columns), '...]
    concatenate x6 -> x0, local copies, waits for them, and re-layouts: 166 us -> none  [strip_stats(): products = jnp.concatenate(pieces, axis=2)]
    gather x21 -> x0, local copies, waits for them, and re-layouts: 96.1 us -> none  [the longest x3 74.2 us: solve_patch(): paired = moments[pair_up, pair_side * plane_count + row_planes, col_planes]]
    psum x1 -> x0, blocking collectives: 88.7 us -> none  [body(): summed = lax.psum(totals, 'ccd')]
    pallas_call x0 -> x8, Pallas kernels: none -> 49.5 us  [the longest x4 23.8 us: moments_call(): pl.pallas_call(functools.partial(moments_kernel, first=first, groups=grou...]
    dot_general x27 -> x0, matrix products: 48 us -> none  [the longest x15 25.4 us: strip_stats(): jnp.einsum('bnrc,bkrc->brnk', scaled, weighted, preferred_element_type=jn...]
    ppermute x0 -> x15, starting transfers between devices: none -> 20.3 us  [shifted(): lax.ppermute(value, axis, [(i, (i + shift) % size) for i in range(size)])]
    another operation x11 -> x1, other arithmetic: 17.6 us -> 0.61 us  [body(): jnp.stack([lax.axis_index('patch'), lax.axis_index('ccd'), jnp.int32(tile...]
  transfers between devices with their start and end apart: 3 -> 15, of which waited for: 1 -> 10; matrix products, arithmetic and copies ran while one was open for 2% -> 5% of each run, Pallas kernels for 0% -> 23%
where the time goes in v1:
time: 92 us; the launch traced here: 90.5 us
  Pallas kernels  49.5 us (54%)
  starting transfers between devices  20.3 us (22%)
  waiting for transfers between devices  10.8 us (12%)
  local copies, waits for them, and re-layouts  5.79 us (6%)
  other arithmetic  3.99 us (4%)
    pallas_call x4, Pallas kernels, moments_call(): pl.pallas_call(functools.partial(moments_kernel, first=first, groups=grou...  23.8 us
    ppermute x15, starting transfers between devices, shifted(): lax.ppermute(value, axis, [(i, (i + shift) % size) for i in range(size)])  20.3 us
    pallas_call x1, Pallas kernels, solve(): pl.pallas_call(functools.partial(solve_kernel, kernels=kernels, planes=pl...  13.7 us
    ppermute x15, waiting for transfers between devices, shifted(): lax.ppermute(value, axis, [(i, (i + shift) % size) for i in range(size)])  10.8 us
    pallas_call x1, Pallas kernels, difference(): pl.pallas_call(functools.partial(difference_kernel, calls=calls, capacity...  7.77 us
    unnamed x30, local copies, waits for them, and re-layouts  4.13 us
    pallas_call x1, Pallas kernels, select_tiles(): pl.pallas_call(functools.partial(select_kernel, shifts=shifts, strips=cod...  2.52 us
  transfers between devices with their start and end apart: 15, of which 10 were waited for; matrix products, arithmetic and copies ran while one was open for 5% of the time, Pallas kernels for 23%

profile of v1, /device:TPU:1, one launch (start us, length us, event | category | flops | bytes accessed | tf_op | source)
XLA Modules:
  0.0 90.5 jit_solution(576029605806760798)
XLA Ops:
  0.0 0.7 multiply_add_fusion.code_ref
  0.7 4.2 %collective-permute-start.2 = (s32[16]{0:T(128)S(1)}, s32[16]{0:T(128)S(1)}, u32[]{:S(2)}, u32[]{:S(2)}) collective-permute-start(s32[16]{0:T(128)S(1)} %multiply_add_fusion.code_ref), channel_id=1, source_target_pairs={{0,12},{4,0},{8,4},{12,8},{1,13},{5,1},{9,5},{13,9},{2,14},{6,2},{... | collective-permute-start | bytes 200 | tf_op jit(solution)/shard_map/ppermute | solution.py:490
  4.8 0.0 collective-permute-start.1
  4.8 0.5 collective-permute-start
  5.3 0.8 slice.15
  6.0 0.8 rev.3
  6.8 1.3 %pad_convert_fusion.rows_ref = f32[14,128]{1,0:T(8,128)} fusion(bf16[14,21]{1,0:T(8,128)(2,1)} %param.15), kind=kLoop, calls=%fused_computation.3 | loop fusion | flops 1792 | bytes 7756 | tf_op jit(solution)/shard_map/jit(_pad)/pad | solution.py:69
  8.1 0.1 pad_slice_fusion
  8.2 0.6 pad_add_fusion.me_ref
  8.8 0.1 slice.14
  8.9 0.1 collective-permute-done.refs_0_
  9.0 0.4 copy-done.8
  9.4 0.1 copy-done.9
  9.5 0.5 copy-done.10
  10.0 2.5 %select.3 = (bf16[8,80,128]{2,1,0:T(8,128)(2,1)}, bf16[8,80,128]{2,1,0:T(8,128)(2,1)}, bf16[8,80,128]{2,1,0:T(8,128)(2,1)}) custom-call(s32[3]{0:T(128)} %pad_add_fusion.me_ref, s32[16]{0:T(128)} %copy-done.10, s32[16]{0:T(128)} %copy-done.9, s32[16]{0:T(128)} %copy-done.8, bf16[16,80,128]{2,1,0:T(8,128)(2,1)} %plates.1), custom_call_target="tpu_custom_call" | custom-call | tf_op jit(solution)/shard_map/select/pallas_call | solution.py:95
  12.5 1.9 %collective-permute-start.5 = (bf16[8,80,128]{2,1,0:T(8,128)(2,1)}, bf16[8,80,128]{2,1,0:T(8,128)(2,1)S(1)}, u32[]{:S(2)}, u32[]{:S(2)}) collective-permute-start(bf16[8,80,128]{2,1,0:T(8,128)(2,1)} %get-tuple-element.27), channel_id=1, source_target_pairs={{0,8},{4,12},{8,0},{12,4},{1,9},{5,13},{9,1},{13,5},{2,10},{6,14},... | collective-permute-start | bytes 491528 | tf_op jit(solution)/shard_map/ppermute | solution.py:490
  14.4 0.7 pad_maximum_fusion.cols_ref
  15.1 1.8 %tables.1 = (bf16[672,80]{1,0:T(8,128)(2,1)}, bf16[14,128,128]{2,1,0:T(8,128)(2,1)}) custom-call(f32[14,128]{1,0:T(8,128)} %pad_convert_fusion.rows_ref, f32[14,128]{1,0:T(8,128)} %pad_maximum_fusion.cols_ref), custom_call_target="tpu_custom_call" | custom-call | tf_op jit(solution)/shard_map/tables/pallas_call | solution.py:51
  16.8 2.4 %collective-permute-start.4 = (bf16[8,80,128]{2,1,0:T(8,128)(2,1)}, bf16[8,80,128]{2,1,0:T(8,128)(2,1)S(1)}, u32[]{:S(2)}, u32[]{:S(2)}) collective-permute-start(bf16[8,80,128]{2,1,0:T(8,128)(2,1)} %get-tuple-element.25), channel_id=1, source_target_pairs={{0,12},{4,0},{8,4},{12,8},{1,13},{5,1},{9,5},{13,9},{2,14},{6,2},{... | collective-permute-start | bytes 491528 | tf_op jit(solution)/shard_map/ppermute | solution.py:490
  19.2 5.2 %moments.4 = (bf16[8,768,128]{2,1,0:T(8,128)(2,1)}, f32[1,48,128]{2,1,0:T(8,128)}) custom-call(s32[3]{0:T(128)} %pad_add_fusion.me_ref, s32[16]{0:T(128)} %copy-done.7, s32[16]{0:T(128)} %row_ref.9, s32[16]{0:T(128)} %good_ref.9, bf16[16,80,128]{2,1,0:T(8,128)(2,1)} %plates.1, bf16[16,48,128]{2,1,0:T(8,128)(2,1)} %science.7, ...), custom_call_target="tpu_custom_call" | custom-call | flops 1000000000 | bytes 1048576 | tf_op jit(solution)/shard_map/moments/pallas_call | solution.py:265
  24.4 2.7 %collective-permute-start.3 = (bf16[8,80,128]{2,1,0:T(8,128)(2,1)S(1)}, bf16[8,80,128]{2,1,0:T(8,128)(2,1)S(1)}, u32[]{:S(2)}, u32[]{:S(2)}) collective-permute-start(bf16[8,80,128]{2,1,0:T(8,128)(2,1)S(1)} %copy-done.11), channel_id=1, source_target_pairs={{0,4},{4,8},{8,12},{12,0},{1,5},{5,9},{9,13},{13,1},{2,6},{6,10},{... | collective-permute-start | bytes 491528 | tf_op jit(solution)/shard_map/ppermute | solution.py:490
  27.1 0.7 copy-done.13
  27.8 5.2 %moments.6 = (bf16[8,768,128]{2,1,0:T(8,128)(2,1)}, f32[1,48,128]{2,1,0:T(8,128)}) custom-call(s32[3]{0:T(128)} %pad_add_fusion.me_ref, s32[16]{0:T(128)} %copy-done.7, s32[16]{0:T(128)} %row_ref.9, s32[16]{0:T(128)} %good_ref.9, bf16[8,80,128]{2,1,0:T(8,128)(2,1)} %copy-done.13, bf16[16,48,128]{2,1,0:T(8,128)(2,1)} %science.7, ...), custom_call_target="tpu_custom_call" | custom-call | flops 1000000000 | bytes 1048576 | tf_op jit(solution)/shard_map/moments/pallas_call | solution.py:265
  33.0 0.7 copy-done.14
  33.6 8.7 %moments.5 = (bf16[8,768,128]{2,1,0:T(8,128)(2,1)}, f32[1,48,128]{2,1,0:T(8,128)}) custom-call(s32[3]{0:T(128)} %pad_add_fusion.me_ref, s32[16]{0:T(128)} %copy-done.7, s32[16]{0:T(128)} %row_ref.9, s32[16]{0:T(128)} %good_ref.9, bf16[8,80,128]{2,1,0:T(8,128)(2,1)} %copy-done.14, bf16[16,48,128]{2,1,0:T(8,128)(2,1)} %science.7, ...), custom_call_target="tpu_custom_call" | custom-call | flops 1000000000 | bytes 1048576 | tf_op jit(solution)/shard_map/moments/pallas_call | solution.py:265
  42.4 0.7 copy-done.12
  43.0 4.6 %moments.7 = (bf16[8,768,128]{2,1,0:T(8,128)(2,1)}, f32[1,48,128]{2,1,0:T(8,128)}, f32[1,48,128]{2,1,0:T(8,128)}, f32[1,48,128]{2,1,0:T(8,128)}, f32[1,48,128]{2,1,0:T(8,128)}) custom-call(s32[3]{0:T(128)} %pad_add_fusion.me_ref, s32[16]{0:T(128)} %copy-done.7, s32[16]{0:T(128)} %row_ref.9, s32[16]{0:T(128)} %good_ref.9, bf16[8,80,128]{2,1,0:T(8,128)(2,1)} %copy-done.12, ...), custom_call_target="tpu_custom_call" | custom-call | flops 1000000000 | bytes 1048576 | tf_op jit(solution)/shard_map/moments/pallas_call | solution.py:265
  47.7 3.2 %collective-permute-start.6 = (f32[1,48,128]{2,1,0:T(8,128)}, f32[1,48,128]{2,1,0:T(8,128)S(1)}, u32[]{:S(2)}, u32[]{:S(2)}) collective-permute-start(f32[1,48,128]{2,1,0:T(8,128)} %get-tuple-element.30), channel_id=1, source_target_pairs={{0,1},{1,2},{2,3},{3,0},{4,5},{5,6},{6,7},{7,4},{8,9},{9,10},{10,1... | collective-permute-start | bytes 73736 | tf_op jit(solution)/shard_map/ppermute | solution.py:490
  50.8 0.3 collective-permute-start.7
  51.1 0.2 collective-permute-start.8
  51.3 0.7 collective-permute-done.6
  52.0 1.7 %collective-permute-done.7 = f32[1,48,128]{2,1,0:T(8,128)S(1)} collective-permute-done((f32[1,48,128]{2,1,0:T(8,128)}, f32[1,48,128]{2,1,0:T(8,128)S(1)}, u32[]{:S(2)}, u32[]{:S(2)}) %collective-permute-start.7) | collective-permute-done | bytes 24608 | tf_op jit(solution)/shard_map/ppermute | solution.py:490
  53.7 0.8 collective-permute-done.8
  54.6 0.7 add_add_fusion.refs_0_
  55.3 2.1 %collective-permute-start.11 = (f32[1,48,128]{2,1,0:T(8,128)S(1)}, f32[1,48,128]{2,1,0:T(8,128)S(1)}, u32[]{:S(2)}, u32[]{:S(2)}) collective-permute-start(f32[1,48,128]{2,1,0:T(8,128)S(1)} %add_add_fusion.refs_0_), channel_id=1, source_target_pairs={{0,12},{4,0},{8,4},{12,8},{1,13},{5,1},{9,5},{13,9},{2,14},{6,2},{... | collective-permute-start | bytes 73736 | tf_op jit(solution)/shard_map/ppermute | solution.py:490
  57.4 0.4 collective-permute-start.9
  57.8 0.6 collective-permute-done.11.refs_3_
  58.4 2.6 %collective-permute-done.10.refs_2_ = f32[1,48,128]{2,1,0:T(8,128)S(1)} collective-permute-done((f32[1,48,128]{2,1,0:T(8,128)S(1)}, f32[1,48,128]{2,1,0:T(8,128)S(1)}, u32[]{:S(2)}, u32[]{:S(2)}) %collective-permute-start.10) | collective-permute-done | bytes 24608 | tf_op jit(solution)/shard_map/ppermute | solution.py:490
  61.0 0.9 collective-permute-done.9.refs_1_
  61.9 0.6 copy-done.3
  62.5 13.7 %solve.1.refs_0_ = f32[1,8,128]{2,1,0:T(8,128)} custom-call(s32[14]{0:T(128)} %order_ref.1, f32[1,48,128]{2,1,0:T(8,128)} %copy-done, f32[1,48,128]{2,1,0:T(8,128)} %copy-done.3, f32[1,48,128]{2,1,0:T(8,128)} %copy-done.2, f32[1,48,128]{2,1,0:T(8,128)} %copy-done.1), custom_call_target="tpu_custom_call" | custom-call | tf_op jit(solution)/shard_map/solve/pallas_call | solution.py:364
  76.2 2.0 %collective-permute-start.14 = (f32[1,8,128]{2,1,0:T(8,128)}, f32[1,8,128]{2,1,0:T(8,128)S(1)}, u32[]{:S(2)}, u32[]{:S(2)}) collective-permute-start(f32[1,8,128]{2,1,0:T(8,128)} %solve.1.refs_0_), channel_id=1, source_target_pairs={{0,1},{1,2},{2,3},{3,0},{4,5},{5,6},{6,7},{7,4},{8,9},{9,10},{10,1... | collective-permute-start | bytes 12296 | tf_op jit(solution)/shard_map/ppermute | solution.py:490
  78.2 0.6 collective-permute-start.13
  78.9 0.3 collective-permute-done.14.refs_3_
  79.2 1.8 %collective-permute-done.13.refs_2_ = f32[1,8,128]{2,1,0:T(8,128)S(1)} collective-permute-done((f32[1,8,128]{2,1,0:T(8,128)}, f32[1,8,128]{2,1,0:T(8,128)S(1)}, u32[]{:S(2)}, u32[]{:S(2)}) %collective-permute-start.13) | collective-permute-done | bytes 4128 | tf_op jit(solution)/shard_map/ppermute | solution.py:490
  81.0 1.1 %collective-permute-done.12.refs_1_ = f32[1,8,128]{2,1,0:T(8,128)S(1)} collective-permute-done((f32[1,8,128]{2,1,0:T(8,128)}, f32[1,8,128]{2,1,0:T(8,128)S(1)}, u32[]{:S(2)}, u32[]{:S(2)}) %collective-permute-start.12) | collective-permute-done | bytes 4128 | tf_op jit(solution)/shard_map/ppermute | solution.py:490
  82.1 0.6 copy-done.6
  82.7 7.8 %difference.1 = bf16[16,48,128]{2,1,0:T(8,128)(2,1)} custom-call(s32[3]{0:T(128)} %pad_add_fusion.me_ref, s32[16]{0:T(128)} %copy-done.7, s32[16]{0:T(128)} %row_ref.9, s32[16]{0:T(128)} %good_ref.9, f32[1,8,128]{2,1,0:T(8,128)} %solve.1.refs_0_, f32[1,8,128]{2,1,0:T(8,128)} %copy-done.6, f32[1,8,128]{2,1,0:T(8,128)} %copy-done.5, f32[1,8,128]{2,1,0:T(8,128)} %copy-done.4, ...), custom_call_target="tpu_custom_call" | custom-call | tf_op jit(solution)/shard_map/difference/pallas_call | solution.py:464
  (29 shorter events, 0.1 us)
Async XLA Ops:
  0.7 18.5 %copy-start.7 = (s32[16]{0:T(128)}, s32[16]{0:T(128)S(1)}, u32[]{:S(2)}) copy-start(s32[16]{0:T(128)S(1)} %multiply_add_fusion.code_ref) | copy-start | bytes 196
  0.7 8.2 %collective-permute-start.2 = (s32[16]{0:T(128)S(1)}, s32[16]{0:T(128)S(1)}, u32[]{:S(2)}, u32[]{:S(2)}) collective-permute-start(s32[16]{0:T(128)S(1)} %multiply_add_fusion.code_ref), channel_id=1, source_target_pairs={{0,12},{4,0},{8,4},{12,8},{1,13},{5,1},{9,5},{13,9},{2,14},{6,2},{... | collective-permute-start | bytes 200 | tf_op jit(solution)/shard_map/ppermute | solution.py:490
  4.8 4.0 %collective-permute-start.1 = (s32[16]{0:T(128)S(1)}, s32[16]{0:T(128)S(1)}, u32[]{:S(2)}, u32[]{:S(2)}) collective-permute-start(s32[16]{0:T(128)S(1)} %multiply_add_fusion.code_ref), channel_id=1, source_target_pairs={{0,8},{4,12},{8,0},{12,4},{1,9},{5,13},{9,1},{13,5},{2,10},{6,14},... | collective-permute-start | bytes 200 | tf_op jit(solution)/shard_map/ppermute | solution.py:490
  4.8 4.2 %collective-permute-start = (s32[16]{0:T(128)S(1)}, s32[16]{0:T(128)S(1)}, u32[]{:S(2)}, u32[]{:S(2)}) collective-permute-start(s32[16]{0:T(128)S(1)} %multiply_add_fusion.code_ref), channel_id=1, source_target_pairs={{0,4},{4,8},{8,12},{12,0},{1,5},{5,9},{9,13},{13,1},{2,6},{6,10},{... | collective-permute-start | bytes 200 | tf_op jit(solution)/shard_map/ppermute | solution.py:490
  8.9 0.5 copy-start.8
  8.9 0.6 copy-start.9
  9.5 0.5 copy-start.10
  12.5 14.6 %collective-permute-start.5 = (bf16[8,80,128]{2,1,0:T(8,128)(2,1)}, bf16[8,80,128]{2,1,0:T(8,128)(2,1)S(1)}, u32[]{:S(2)}, u32[]{:S(2)}) collective-permute-start(bf16[8,80,128]{2,1,0:T(8,128)(2,1)} %get-tuple-element.27), channel_id=1, source_target_pairs={{0,8},{4,12},{8,0},{12,4},{1,9},{5,13},{9,1},{13,5},{2,10},{6,14},... | collective-permute-start | bytes 491528 | tf_op jit(solution)/shard_map/ppermute | solution.py:490
  16.8 16.1 %collective-permute-start.4 = (bf16[8,80,128]{2,1,0:T(8,128)(2,1)}, bf16[8,80,128]{2,1,0:T(8,128)(2,1)S(1)}, u32[]{:S(2)}, u32[]{:S(2)}) collective-permute-start(bf16[8,80,128]{2,1,0:T(8,128)(2,1)} %get-tuple-element.25), channel_id=1, source_target_pairs={{0,12},{4,0},{8,4},{12,8},{1,13},{5,1},{9,5},{13,9},{2,14},{6,2},{... | collective-permute-start | bytes 491528 | tf_op jit(solution)/shard_map/ppermute | solution.py:490
  19.2 5.2 %copy-start.11 = (bf16[8,80,128]{2,1,0:T(8,128)(2,1)S(1)}, bf16[8,80,128]{2,1,0:T(8,128)(2,1)}, u32[]{:S(2)}) copy-start(bf16[8,80,128]{2,1,0:T(8,128)(2,1)} %get-tuple-element.21) | copy-start | bytes 491524
  24.4 17.9 %collective-permute-start.3 = (bf16[8,80,128]{2,1,0:T(8,128)(2,1)S(1)}, bf16[8,80,128]{2,1,0:T(8,128)(2,1)S(1)}, u32[]{:S(2)}, u32[]{:S(2)}) collective-permute-start(bf16[8,80,128]{2,1,0:T(8,128)(2,1)S(1)} %copy-done.11), channel_id=1, source_target_pairs={{0,4},{4,8},{8,12},{12,0},{1,5},{5,9},{9,13},{13,1},{2,6},{6,10},{... | collective-permute-start | bytes 491528 | tf_op jit(solution)/shard_map/ppermute | solution.py:490
  27.1 0.7 copy-start.13
  33.0 0.7 copy-start.14
  42.4 0.7 copy-start.12
  47.7 4.3 %collective-permute-start.6 = (f32[1,48,128]{2,1,0:T(8,128)}, f32[1,48,128]{2,1,0:T(8,128)S(1)}, u32[]{:S(2)}, u32[]{:S(2)}) collective-permute-start(f32[1,48,128]{2,1,0:T(8,128)} %get-tuple-element.30), channel_id=1, source_target_pairs={{0,1},{1,2},{2,3},{3,0},{4,5},{5,6},{6,7},{7,4},{8,9},{9,10},{10,1... | collective-permute-start | bytes 73736 | tf_op jit(solution)/shard_map/ppermute | solution.py:490
  50.8 2.9 %collective-permute-start.7 = (f32[1,48,128]{2,1,0:T(8,128)}, f32[1,48,128]{2,1,0:T(8,128)S(1)}, u32[]{:S(2)}, u32[]{:S(2)}) collective-permute-start(f32[1,48,128]{2,1,0:T(8,128)} %get-tuple-element.31), channel_id=1, source_target_pairs={{0,2},{1,3},{2,0},{3,1},{4,6},{5,7},{6,4},{7,5},{8,10},{9,11},{10,... | collective-permute-start | bytes 73736 | tf_op jit(solution)/shard_map/ppermute | solution.py:490
  51.1 3.5 %collective-permute-start.8 = (f32[1,48,128]{2,1,0:T(8,128)}, f32[1,48,128]{2,1,0:T(8,128)S(1)}, u32[]{:S(2)}, u32[]{:S(2)}) collective-permute-start(f32[1,48,128]{2,1,0:T(8,128)} %get-tuple-element.32), channel_id=1, source_target_pairs={{0,3},{1,0},{2,1},{3,2},{4,7},{5,4},{6,5},{7,6},{8,11},{9,8},{10,9... | collective-permute-start | bytes 73736 | tf_op jit(solution)/shard_map/ppermute | solution.py:490
  55.3 6.6 %copy-start = (f32[1,48,128]{2,1,0:T(8,128)}, f32[1,48,128]{2,1,0:T(8,128)S(1)}, u32[]{:S(2)}) copy-start(f32[1,48,128]{2,1,0:T(8,128)S(1)} %add_add_fusion.refs_0_) | copy-start | bytes 73732
  55.3 3.0 %collective-permute-start.11 = (f32[1,48,128]{2,1,0:T(8,128)S(1)}, f32[1,48,128]{2,1,0:T(8,128)S(1)}, u32[]{:S(2)}, u32[]{:S(2)}) collective-permute-start(f32[1,48,128]{2,1,0:T(8,128)S(1)} %add_add_fusion.refs_0_), channel_id=1, source_target_pairs={{0,12},{4,0},{8,4},{12,8},{1,13},{5,1},{9,5},{13,9},{2,14},{6,2},{... | collective-permute-start | bytes 73736 | tf_op jit(solution)/shard_map/ppermute | solution.py:490
  57.4 3.6 %collective-permute-start.10 = (f32[1,48,128]{2,1,0:T(8,128)S(1)}, f32[1,48,128]{2,1,0:T(8,128)S(1)}, u32[]{:S(2)}, u32[]{:S(2)}) collective-permute-start(f32[1,48,128]{2,1,0:T(8,128)S(1)} %add_add_fusion.refs_0_), channel_id=1, source_target_pairs={{0,8},{4,12},{8,0},{12,4},{1,9},{5,13},{9,1},{13,5},{2,10},{6,14},... | collective-permute-start | bytes 73736 | tf_op jit(solution)/shard_map/ppermute | solution.py:490
  57.4 4.5 %collective-permute-start.9 = (f32[1,48,128]{2,1,0:T(8,128)S(1)}, f32[1,48,128]{2,1,0:T(8,128)S(1)}, u32[]{:S(2)}, u32[]{:S(2)}) collective-permute-start(f32[1,48,128]{2,1,0:T(8,128)S(1)} %add_add_fusion.refs_0_), channel_id=1, source_target_pairs={{0,4},{4,8},{8,12},{12,0},{1,5},{5,9},{9,13},{13,1},{2,6},{6,10},{... | collective-permute-start | bytes 73736 | tf_op jit(solution)/shard_map/ppermute | solution.py:490
  58.4 3.5 %copy-start.1 = (f32[1,48,128]{2,1,0:T(8,128)}, f32[1,48,128]{2,1,0:T(8,128)S(1)}, u32[]{:S(2)}) copy-start(f32[1,48,128]{2,1,0:T(8,128)S(1)} %collective-permute-done.11.refs_3_) | copy-start | bytes 73732
  61.0 0.9 copy-start.2
  61.9 0.6 copy-start.3
  76.2 3.0 %collective-permute-start.14 = (f32[1,8,128]{2,1,0:T(8,128)}, f32[1,8,128]{2,1,0:T(8,128)S(1)}, u32[]{:S(2)}, u32[]{:S(2)}) collective-permute-start(f32[1,8,128]{2,1,0:T(8,128)} %solve.1.refs_0_), channel_id=1, source_target_pairs={{0,1},{1,2},{2,3},{3,0},{4,5},{5,6},{6,7},{7,4},{8,9},{9,10},{10,1... | collective-permute-start | bytes 12296 | tf_op jit(solution)/shard_map/ppermute | solution.py:490
  78.2 2.7 %collective-permute-start.13 = (f32[1,8,128]{2,1,0:T(8,128)}, f32[1,8,128]{2,1,0:T(8,128)S(1)}, u32[]{:S(2)}, u32[]{:S(2)}) collective-permute-start(f32[1,8,128]{2,1,0:T(8,128)} %solve.1.refs_0_), channel_id=1, source_target_pairs={{0,2},{1,3},{2,0},{3,1},{4,6},{5,7},{6,4},{7,5},{8,10},{9,11},{10,... | collective-permute-start | bytes 12296 | tf_op jit(solution)/shard_map/ppermute | solution.py:490
  78.9 3.2 %collective-permute-start.12 = (f32[1,8,128]{2,1,0:T(8,128)}, f32[1,8,128]{2,1,0:T(8,128)S(1)}, u32[]{:S(2)}, u32[]{:S(2)}) collective-permute-start(f32[1,8,128]{2,1,0:T(8,128)} %solve.1.refs_0_), channel_id=1, source_target_pairs={{0,3},{1,0},{2,1},{3,2},{4,7},{5,4},{6,5},{7,6},{8,11},{9,8},{10,9... | collective-permute-start | bytes 12296 | tf_op jit(solution)/shard_map/ppermute | solution.py:490
  79.2 2.9 %copy-start.4 = (f32[1,8,128]{2,1,0:T(8,128)}, f32[1,8,128]{2,1,0:T(8,128)S(1)}, u32[]{:S(2)}) copy-start(f32[1,8,128]{2,1,0:T(8,128)S(1)} %collective-permute-done.14.refs_3_) | copy-start | bytes 12292
  81.0 1.1 %copy-start.5 = (f32[1,8,128]{2,1,0:T(8,128)}, f32[1,8,128]{2,1,0:T(8,128)S(1)}, u32[]{:S(2)}) copy-start(f32[1,8,128]{2,1,0:T(8,128)S(1)} %collective-permute-done.13.refs_2_) | copy-start | bytes 12292
  82.1 0.6 copy-start.6

commit v2 on v1

--- a/solution.py
+++ b/solution.py
@@ -12,6 +12,7 @@
 TERMS = ((0, 0), (2, 0), (0, 2), (1, 0), (0, 1), (1, 1))
 LEFT = 3
 BATCH = 4
+PAIR = 2
 VMEM = pl.BlockSpec(memory_space=pltpu.VMEM)
 SMEM = pl.BlockSpec(memory_space=pltpu.SMEM)
 F32, BF16, I32 = jnp.float32, jnp.bfloat16, jnp.int32
@@ -26,8 +27,8 @@
     raise ValueError(want)
 
 
-def params():
-    return pltpu.CompilerParams(vmem_limit_bytes=56 * 1024 * 1024)
+def params(mebibytes):
+    return pltpu.CompilerParams(vmem_limit_bytes=mebibytes * 1024 * 1024)
 
 
 def tables_kernel(rows_ref, cols_ref, row_out, col_out, *, kernels, taps, rows, tile_rows, columns):
@@ -63,7 +64,7 @@
         ),
         in_specs=[VMEM, VMEM],
         out_specs=(VMEM, VMEM),
-        compiler_params=params(),
+        compiler_params=params(8),
         name="tables",
     )(
         jnp.pad(basis_rows.astype(F32), pad),
@@ -97,7 +98,7 @@
         out_shape=[jax.ShapeDtypeStruct((capacity, tile_rows, columns), BF16)] * shifts,
         in_specs=[SMEM] + [SMEM] * shifts + [VMEM],
         out_specs=[VMEM] * shifts,
-        compiler_params=params(),
+        compiler_params=params(8),
         name="select",
     )(me, *codes, template)
 
@@ -159,36 +160,41 @@
     for b in range(BATCH):
         p32[pl.ds(b * span + kernels, rows, stride=planes), :] = jnp.ones((rows, columns), F32)
     across = jnp.concatenate([across_rows(columns)] * (planes // 8), axis=0)
-    across2 = across * across
+    across = across.astype(BF16)
     step_rows = 8
 
-    def gram(b, strip, slot):
-        offset = row_ref[strip]
-        good = good_ref[strip]
-        total = jnp.zeros((LEFT * planes, unknowns), F32)
+    def gram(first_b, chosen, goods, slots):
+        offsets = [row_ref[strip] for strip in chosen]
+        totals = [jnp.zeros((unknowns, LEFT * planes), F32) for _ in chosen]
         for chunk in range(rows // step_rows):
-            pieces = [[] for _ in TERMS]
-            for r in range(chunk * step_rows, (chunk + 1) * step_rows):
-                at = r * planes
-                rounded = p32[b * span + at : b * span + at + planes, :].astype(BF16)
-                planes_out[slot, at : at + planes, :] = rounded
-                value = rounded.astype(F32)
-                v = (2 * (offset + r) + 1).astype(F32) * (1.0 / PATCH_ROWS) - 1.0
-                value = value * jnp.where(r < good, 1.0, 0.0)
-                with_u = value * across
-                pieces[0].append(value.astype(BF16))
-                pieces[1].append((value * (v * v)).astype(BF16))
-                pieces[2].append((value * across2).astype(BF16))
-                pieces[3].append((value * v).astype(BF16))
-                pieces[4].append(with_u.astype(BF16))
-                pieces[5].append((with_u * v).astype(BF16))
-            wide = [jnp.concatenate(part, axis=1) for part in pieces]
-            right = jnp.concatenate(wide, axis=0)
-            left = jnp.concatenate(wide[:LEFT], axis=0)
-            total = total + lax.dot_general(
-                left, right, (((1,), (1,)), ((), ())), preferred_element_type=F32
-            )
-        return total
+            operands = []
+            for i in range(len(chosen)):
+                pieces = [[] for _ in TERMS]
+                for r in range(chunk * step_rows, (chunk + 1) * step_rows):
+                    at = r * planes
+                    base = (first_b + i) * span + at
+                    value = p32[base : base + planes, :].astype(BF16)
+                    planes_out[slots[i], at : at + planes, :] = value
+                    v = (2 * (offsets[i] + r) + 1).astype(F32) * (1.0 / PATCH_ROWS) - 1.0
+                    value = value * jnp.where(r < goods[i], 1.0, 0.0).astype(BF16)
+                    with_v = value.astype(F32) * v
+                    with_u = value * across
+                    once = with_v.astype(BF16)
+                    pieces[0].append(value)
+                    pieces[1].append((with_v * v).astype(BF16))
+                    pieces[2].append(with_u * across)
+                    pieces[3].append(once)
+                    pieces[4].append(with_u)
+                    pieces[5].append(once * across)
+                wide = [jnp.concatenate(part, axis=1) for part in pieces]
+                operands.append(
+                    (jnp.concatenate(wide, axis=0), jnp.concatenate(wide[:LEFT], axis=0))
+                )
+            for i, (every, left) in enumerate(operands):
+                totals[i] = totals[i] + lax.dot_general(
+                    every, left, (((1,), (1,)), ((), ())), preferred_element_type=F32
+                )
+        return functools.reduce(lambda a, b: a + b, totals)
 
     def group(g, carry):
         patch = me + (first + g)
@@ -220,13 +226,19 @@
                 p32[pl.ds(b * span + planes - 1, rows, stride=planes), :] = science[
                     chosen[b]
                 ].astype(F32)
-            for b in range(BATCH):
-
-                @pl.when(slots[b] < count)
-                def _(b=b):
-                    total = gram(b, chosen[b], g * capacity + slots[b])
-                    sums[first + g, :, :unknowns] += total
-
+            total = jnp.zeros((unknowns, LEFT * planes), F32)
+            for b in range(0, BATCH, PAIR):
+                these = slice(b, b + PAIR)
+                goods = [
+                    jnp.where(slot < count, good_ref[strip], 0)
+                    for slot, strip in zip(slots[these], chosen[these])
+                ]
+                total = total + gram(
+                    b, chosen[these], goods, [g * capacity + slot for slot in slots[these]]
+                )
+            half = LEFT * planes
+            sums[first + g, :, :half] += total[:half]
+            sums[first + g, :, half : 2 * half] += total[half:]
             return carry
 
         lax.fori_loop(0, (count + BATCH - 1) // BATCH, batch, 0)
@@ -284,7 +296,7 @@
             pltpu.SMEM((strips,), I32),
             pltpu.VMEM((max(patches, ccds),) + sum_shape, F32),
         ],
-        compiler_params=params(),
+        compiler_params=params(20),
         cost_estimate=pl.CostEstimate(
             flops=int(4e9) * groups // patches, bytes_accessed=1 << 20, transcendentals=0
         ),
@@ -315,18 +327,20 @@
     active_col = activity(sub)
     lane16 = lane[:planes]
     row8 = lax.broadcasted_iota(I32, (8, 128), 0)
-    for k in range(share):
-        moments = parts[0][k]
+    for q in range(share):
+        moments = parts[0][q]
         for ref in parts[1:]:
-            moments = moments + ref[k]
+            moments = moments + ref[q]
         rows = []
         for a in range(terms):
             row = jnp.zeros((planes, 128), F32)
             for b in range(terms):
                 left, right = block_of(a, b)
-                piece = moments[left * planes : (left + 1) * planes]
-                if b != right:
-                    piece = pltpu.roll(piece, ((b - right) * planes) % 128, 1)
+                at = right % LEFT * planes
+                place = right // LEFT * LEFT + left
+                piece = moments[at : at + planes]
+                if b != place:
+                    piece = pltpu.roll(piece, ((b - place) * planes) % 128, 1)
                 row = jnp.where(lane16 // planes == b, piece, row)
             rows.append(row)
         paired = jnp.concatenate(rows, axis=0)
@@ -335,19 +349,33 @@
         system = jnp.where(lane == sub, masked + (1.0 + RIDGE * masked), masked)
         system = jnp.where(lane == size, active_col * target, system)
         blocks = [system[8 * m : 8 * m + 8] for m in range(size // 8)]
-        for x in range(size):
-            if x % planes > kernels:
-                continue
-            at, inner = divmod(x, 8)
-            row = jnp.broadcast_to(blocks[at][inner : inner + 1], (8, 128))
-            pivot = jnp.broadcast_to(row[:, x : x + 1], (8, 128))
-            scaled = row * (1.0 / pivot)
+        for at in range(size // 8):
+            wanted = [i for i in range(8) if (8 * at + i) % planes <= kernels]
+            columns = [
+                {i: jnp.broadcast_to(block[:, 8 * at + i : 8 * at + i + 1], (8, 128)) for i in wanted}
+                for block in blocks
+            ]
+            inner, here = columns[at], blocks[at]
+            for i in wanted:
+                scale = 1.0 / jnp.broadcast_to(inner[i][i : i + 1], (8, 128))
+                line = jnp.broadcast_to(here[i : i + 1], (8, 128)) * scale
+                here = jnp.where(row8 == i, line, here - inner[i] * line)
+                for k in wanted:
+                    if k > i:
+                        entry = jnp.broadcast_to(inner[k][i : i + 1], (8, 128)) * scale
+                        inner[k] = jnp.where(row8 == i, entry, inner[k] - inner[i] * entry)
+            lines = {i: jnp.broadcast_to(here[i : i + 1], (8, 128)) for i in wanted}
             for m in range(size // 8):
-                column = jnp.broadcast_to(blocks[m][:, x : x + 1], (8, 128))
-                new = blocks[m] - column * scaled
                 if m == at:
-                    new = jnp.where(row8 == inner, scaled, new)
-                blocks[m] = new
+                    blocks[m] = here
+                    continue
+                terms_here = [columns[m][i] * lines[i] for i in wanted]
+                while len(terms_here) > 1:
+                    terms_here = [
+                        functools.reduce(lambda a, b: a + b, terms_here[q : q + 2])
+                        for q in range(0, len(terms_here), 2)
+                    ]
+                blocks[m] = blocks[m] - terms_here[0]
         answer = jnp.concatenate(blocks, axis=0)
         answer = jnp.broadcast_to(answer[:, size : size + 1], (size, 128))
         answer = jnp.where(sub % planes == lane % planes, answer, 0.0)
@@ -356,7 +384,7 @@
             for t in range(terms)
         ]
         lines.append(jnp.zeros((8 - terms, 128), F32))
-        out[k] = jnp.concatenate(lines, axis=0)
+        out[q] = jnp.concatenate(lines, axis=0)
 
 
 def solve(order, parts, kernels, planes):
@@ -366,7 +394,7 @@
         out_shape=jax.ShapeDtypeStruct((share, 8, 128), F32),
         in_specs=[SMEM] + [VMEM] * len(parts),
         out_specs=VMEM,
-        compiler_params=params(),
+        compiler_params=params(4),
         name="solve",
     )(order, *parts)
 
@@ -399,16 +427,14 @@
     across2 = across * across
     width = tall * planes
     lane = lax.broadcasted_iota(I32, (tall, width), 1)
-    sub = lax.broadcasted_iota(I32, (tall, width), 0)
-    diagonal = lane // planes == sub
+    diagonal = lane // planes == lax.broadcasted_iota(I32, (tall, width), 0)
     is_science = diagonal & (lane % planes == planes - 1)
-    sub_out = lax.broadcasted_iota(I32, (tall, columns), 0)
+    sub = lax.broadcasted_iota(I32, (tall, columns), 0)
 
     def pieces(value):
         high = value.astype(BF16)
         rest = value - high.astype(F32)
-        middle = rest.astype(BF16)
-        return high, middle, (rest - middle.astype(F32)).astype(BF16)
+        return high, rest.astype(BF16)
 
     for (first, groups), stack in zip(calls, stacks):
 
@@ -417,39 +443,37 @@
             patch = jnp.where(patch >= patches, patch - patches, patch)
             count = list_group(code_ref, listing, patch, tiles, strips)
             block = table[patch]
-            coef = [
-                jnp.broadcast_to(
-                    jnp.concatenate([block[t : t + 1]] * (width // 128), axis=1), (tall, width)
-                )
-                for t in range(len(TERMS))
-            ]
-
-            def strip_step(j, carry):
-                strip = listing[j]
-                offset, good = row_ref[strip], good_ref[strip]
-                for h in range(rows // tall):
-                    v = (2 * (offset + h * tall + sub) + 1).astype(F32) / PATCH_ROWS - 1.0
-                    plain = coef[0] + v * (coef[3] + v * coef[1])
-                    once = coef[4] + v * coef[5]
-                    twice = coef[2]
-                    plain = jnp.where(diagonal, -plain, 0.0)
-                    plain = jnp.where(is_science, 1.0, plain)
-                    once = jnp.where(diagonal, -once, 0.0)
-                    twice = jnp.where(diagonal, -twice, 0.0)
-                    lhs = jnp.concatenate([*pieces(plain), *pieces(once), *pieces(twice)], axis=0)
-                    rhs = stack[g * capacity + j, h * width : (h + 1) * width, :]
-                    got = jnp.dot(lhs, rhs, preferred_element_type=F32)
-                    part = [got[i * tall : (i + 1) * tall] for i in range(9)]
-                    value = (
-                        (part[0] + (part[1] + part[2]))
-                        + across * (part[3] + (part[4] + part[5]))
-                        + across2 * (part[6] + (part[7] + part[8]))
-                    )
-                    value = jnp.where(h * tall + sub_out < good, value, 0.0)
-                    out[strip, h * tall : (h + 1) * tall, :] = value.astype(BF16)
+            coef = []
+            for t in range(len(TERMS)):
+                line = jnp.concatenate([block[t : t + 1]] * (width // 128), axis=1)
+                coef.append(jnp.where(diagonal, -jnp.broadcast_to(line, (tall, width)), 0.0))
+            coef[0] = jnp.where(is_science, 1.0, coef[0])
+            twice = pieces(coef[2])
+
+            def strip_step(t, carry):
+                for j in range(PAIR):
+                    j = jnp.minimum(t * PAIR + j, count - 1)
+                    strip = listing[j]
+                    offset, good = row_ref[strip], good_ref[strip]
+                    for h in range(rows // tall):
+                        v = (2 * (offset + h * tall + sub) + 1).astype(F32) / PATCH_ROWS - 1.0
+                        v = jnp.concatenate([v] * (width // 128), axis=1)
+                        plain = coef[0] + v * (coef[3] + v * coef[1])
+                        once = coef[4] + v * coef[5]
+                        lhs = jnp.concatenate([*pieces(plain), *pieces(once), *twice], axis=0)
+                        rhs = stack[g * capacity + j, h * width : (h + 1) * width, :]
+                        got = jnp.dot(lhs, rhs, preferred_element_type=F32)
+                        part = [got[i * tall : (i + 1) * tall] for i in range(6)]
+                        value = (
+                            (part[0] + part[1])
+                            + across * (part[2] + part[3])
+                            + across2 * (part[4] + part[5])
+                        )
+                        value = jnp.where(h * tall + sub < good, value, 0.0)
+                        out[strip, h * tall : (h + 1) * tall, :] = value.astype(BF16)
                 return carry
 
-            lax.fori_loop(0, count, strip_step, 0)
+            lax.fori_loop(0, (count + PAIR - 1) // PAIR, strip_step, 0)
             return carry
 
         if groups == 1:
@@ -480,7 +504,7 @@
             pltpu.VMEM((share * ccds, 8, 128), F32),
             pltpu.SMEM((strips,), I32),
         ],
-        compiler_params=params(),
+        compiler_params=params(20),
         name="difference",
     )(*scalars, *coefs, *stacks)
 

time: 92 us -> 68 us (0.74); the launches traced: 90.5 us -> 68 us
  Pallas kernels: 49.5 us -> 28.6 us
  other arithmetic: 3.99 us -> 1.53 us
    pallas_call x1, Pallas kernels: 13.7 us -> 4.6 us  [solve(): pl.pallas_call(functools.partial(solve_kernel, kernels=kernels, planes=pl...]
    pallas_call x4, Pallas kernels: 23.8 us -> 18.3 us  [moments_call(): pl.pallas_call(functools.partial(moments_kernel, first=first, groups=grou...]
    pallas_call x1, Pallas kernels: 7.77 us -> 4.16 us  [difference(): pl.pallas_call(functools.partial(difference_kernel, calls=calls, capacity...]
    pallas_call x1, Pallas kernels: 1.77 us -> 0.23 us  [make_tables(): pl.pallas_call(functools.partial(tables_kernel, kernels=kernels, taps=tap...]
    pallas_call x1, Pallas kernels: 2.52 us -> 1.31 us  [select_tiles(): pl.pallas_call(functools.partial(select_kernel, shifts=shifts, strips=cod...]
    unnamed x30 -> x18, local copies, waits for them, and re-layouts: 4.13 us -> 4.2 us
  transfers between devices with their start and end apart: 15 -> 15, of which waited for: 10 -> 11; matrix products, arithmetic and copies ran while one was open for 5% -> 4% of each run, Pallas kernels for 23% -> 22%
where the time goes in v2:
time: 68 us
  Pallas kernels  28.6 us (42%)
  starting transfers between devices  20.2 us (30%)
  waiting for transfers between devices  11.6 us (17%)
  local copies, waits for them, and re-layouts  5.87 us (9%)
  other arithmetic  1.53 us (2%)
    ppermute x15, starting transfers between devices, shifted(): lax.ppermute(value, axis, [(i, (i + shift) % size) for i in range(size)])  20.2 us
    pallas_call x4, Pallas kernels, moments_call(): pl.pallas_call(functools.partial(moments_kernel, first=first, groups=grou...  18.3 us
    ppermute x15, waiting for transfers between devices, shifted(): lax.ppermute(value, axis, [(i, (i + shift) % size) for i in range(size)])  11.6 us
    pallas_call x1, Pallas kernels, solve(): pl.pallas_call(functools.partial(solve_kernel, kernels=kernels, planes=pl...  4.6 us
    unnamed x18, local copies, waits for them, and re-layouts  4.2 us
    pallas_call x1, Pallas kernels, difference(): pl.pallas_call(functools.partial(difference_kernel, calls=calls, capacity...  4.16 us
  transfers between devices with their start and end apart: 15, of which 11 were waited for; matrix products, arithmetic and copies ran while one was open for 4% of the time, Pallas kernels for 22%

profile of v2, /device:TPU:1, one launch (start us, length us, event | category | flops | bytes accessed | tf_op | source)
XLA Modules:
  0.0 68.0 jit_solution(11547069361920881597)
XLA Ops:
  0.0 0.7 multiply_add_fusion.code_ref
  0.7 4.2 %collective-permute-start.2 = (s32[16]{0:T(128)S(1)}, s32[16]{0:T(128)S(1)}, u32[]{:S(2)}, u32[]{:S(2)}) collective-permute-start(s32[16]{0:T(128)S(1)} %multiply_add_fusion.code_ref), channel_id=1, source_target_pairs={{0,12},{4,0},{8,4},{12,8},{1,13},{5,1},{9,5},{13,9},{2,14},{6,2},{... | collective-permute-start | bytes 200 | tf_op jit(solution)/shard_map/ppermute | solution.py:514
  4.8 0.0 collective-permute-start.1
  4.8 0.5 collective-permute-start
  5.3 0.8 %slice.15 = f32[14,10]{1,0:T(8,128)S(1)} slice(bf16[14,21]{1,0:T(8,128)(2,1)} %param.16), slice={[0:14], [11:21]} | slice | bytes 1120 | tf_op jit(solution)/shard_map/jit(_roll_static)/slice | solution.py:71
  6.0 0.8 %rev.3 = f32[14,21]{1,0:T(8,128)S(1)} reverse(bf16[14,21]{1,0:T(8,128)(2,1)} %param.16), dimensions={1} | reverse | bytes 1764 | tf_op jit(solution)/shard_map/rev | solution.py:71
  6.8 0.7 %pad_convert_fusion.rows_ref = f32[14,128]{1,0:T(8,128)S(1)} fusion(bf16[14,21]{1,0:T(8,128)(2,1)} %param.15), kind=kLoop, calls=%fused_computation.3 | loop fusion | flops 1792 | bytes 7756 | tf_op jit(solution)/shard_map/jit(_pad)/pad | solution.py:70
  7.5 0.1 pad_slice_fusion
  7.6 0.1 pad_add_fusion.me_ref
  7.6 0.1 slice.14
  7.7 0.4 collective-permute-done.1.refs_1_
  8.1 0.9 %collective-permute-done.refs_0_ = s32[16]{0:T(128)S(1)} collective-permute-done((s32[16]{0:T(128)S(1)}, s32[16]{0:T(128)S(1)}, u32[]{:S(2)}, u32[]{:S(2)}) %collective-permute-start) | collective-permute-done | bytes 96 | tf_op jit(solution)/shard_map/ppermute | solution.py:514
  9.0 1.0 %copy-done = bf16[16,80,128]{2,1,0:T(8,128)(2,1)S(1)} copy-done((bf16[16,80,128]{2,1,0:T(8,128)(2,1)S(1)}, bf16[16,80,128]{2,1,0:T(8,128)(2,1)}, u32[]{:S(2)}) %copy-start) | copy-done | bytes 327704
  10.0 1.3 %select.3 = (bf16[8,80,128]{2,1,0:T(8,128)(2,1)S(1)}, bf16[8,80,128]{2,1,0:T(8,128)(2,1)S(1)}, bf16[8,80,128]{2,1,0:T(8,128)(2,1)S(1)}) custom-call(s32[3]{0:T(128)S(1)} %pad_add_fusion.me_ref, s32[16]{0:T(128)S(1)} %collective-permute-done.refs_0_, s32[16]{0:T(128)S(1)} %collective-permute-done.1.refs_1_, s32[16]{0:T(128)S(1)} %collective-permute-done.2.refs_2_, ...), custom_call_target="tpu_custom_call" | custom-call | tf_op jit(solution)/shard_map/select/pallas_call | solution.py:96
  11.3 0.7 %collective-permute-start.5 = (bf16[8,80,128]{2,1,0:T(8,128)(2,1)S(1)}, bf16[8,80,128]{2,1,0:T(8,128)(2,1)S(1)}, u32[]{:S(2)}, u32[]{:S(2)}) collective-permute-start(bf16[8,80,128]{2,1,0:T(8,128)(2,1)S(1)} %get-tuple-element.27), channel_id=1, source_target_pairs={{0,8},{4,12},{8,0},{12,4},{1,9},{5,13},{9,1},{13,5},{2,10},{6,14},... | collective-permute-start | bytes 491528 | tf_op jit(solution)/shard_map/ppermute | solution.py:514
  12.0 0.1 pad_maximum_fusion.cols_ref
  12.1 0.2 tables.1
  12.3 2.4 %collective-permute-start.4 = (bf16[8,80,128]{2,1,0:T(8,128)(2,1)S(1)}, bf16[8,80,128]{2,1,0:T(8,128)(2,1)S(1)}, u32[]{:S(2)}, u32[]{:S(2)}) collective-permute-start(bf16[8,80,128]{2,1,0:T(8,128)(2,1)S(1)} %get-tuple-element.25), channel_id=1, source_target_pairs={{0,12},{4,0},{8,4},{12,8},{1,13},{5,1},{9,5},{13,9},{2,14},{6,2},{... | collective-permute-start | bytes 491528 | tf_op jit(solution)/shard_map/ppermute | solution.py:514
  14.7 1.0 %copy-done.1 = bf16[16,80,128]{2,1,0:T(8,128)(2,1)S(1)} copy-done((bf16[16,80,128]{2,1,0:T(8,128)(2,1)S(1)}, bf16[16,80,128]{2,1,0:T(8,128)(2,1)}, u32[]{:S(2)}) %copy-start.1) | copy-done | bytes 327704
  15.7 0.7 copy-done.3
  16.4 0.7 copy-done.5
  17.0 0.9 %copy-done.7 = bf16[16,48,128]{2,1,0:T(8,128)(2,1)S(1)} copy-done((bf16[16,48,128]{2,1,0:T(8,128)(2,1)S(1)}, bf16[16,48,128]{2,1,0:T(8,128)(2,1)}, u32[]{:S(2)}) %copy-start.7) | copy-done | bytes 196632
  17.9 3.8 %moments.4 = (bf16[8,768,128]{2,1,0:T(8,128)(2,1)S(1)}, f32[1,48,128]{2,1,0:T(8,128)S(1)}) custom-call(s32[3]{0:T(128)S(1)} %pad_add_fusion.me_ref, s32[16]{0:T(128)S(1)} %multiply_add_fusion.code_ref, s32[16]{0:T(128)S(1)} %copy-done.3, s32[16]{0:T(128)S(1)} %copy-done.5, bf16[16,80,128]{2,1,0:T(8,128)(2,1)S(1)} %copy-done.1, ...), custom_call_target="tpu_custom_call" | custom-call | flops 1000000000 | bytes 1048576 | tf_op jit(solution)/shard_map/moments/pallas_call | solution.py:277
  21.8 0.0 copy-start.8
  21.8 2.2 %collective-permute-start.3 = (bf16[8,80,128]{2,1,0:T(8,128)(2,1)S(1)}, bf16[8,80,128]{2,1,0:T(8,128)(2,1)S(1)}, u32[]{:S(2)}, u32[]{:S(2)}) collective-permute-start(bf16[8,80,128]{2,1,0:T(8,128)(2,1)S(1)} %get-tuple-element.21), channel_id=1, source_target_pairs={{0,4},{4,8},{8,12},{12,0},{1,5},{5,9},{9,13},{13,1},{2,6},{6,10},{... | collective-permute-start | bytes 491528 | tf_op jit(solution)/shard_map/ppermute | solution.py:514
  24.0 3.8 %moments.6 = (bf16[8,768,128]{2,1,0:T(8,128)(2,1)S(1)}, f32[1,48,128]{2,1,0:T(8,128)S(1)}) custom-call(s32[3]{0:T(128)S(1)} %pad_add_fusion.me_ref, s32[16]{0:T(128)S(1)} %multiply_add_fusion.code_ref, s32[16]{0:T(128)S(1)} %copy-done.3, s32[16]{0:T(128)S(1)} %copy-done.6, bf16[8,80,128]{2,1,0:T(8,128)(2,1)S(1)} %collective-permute-done.5.plates, ...), custom_call_target="tpu_custom_call" | custom-call | flops 1000000000 | bytes 1048576 | tf_op jit(solution)/shard_map/moments/pallas_call | solution.py:277
  27.8 0.0 copy-start.4
  27.8 6.8 %moments.5 = (bf16[8,768,128]{2,1,0:T(8,128)(2,1)S(1)}, f32[1,48,128]{2,1,0:T(8,128)S(1)}) custom-call(s32[3]{0:T(128)S(1)} %pad_add_fusion.me_ref, s32[16]{0:T(128)S(1)} %multiply_add_fusion.code_ref, s32[16]{0:T(128)S(1)} %copy-done.3, s32[16]{0:T(128)S(1)} %copy-done.6, bf16[8,80,128]{2,1,0:T(8,128)(2,1)S(1)} %collective-permute-done.4.plates, ...), custom_call_target="tpu_custom_call" | custom-call | flops 1000000000 | bytes 1048576 | tf_op jit(solution)/shard_map/moments/pallas_call | solution.py:277
  34.7 0.0 copy-start.2
  34.7 3.8 %moments.7 = (bf16[8,768,128]{2,1,0:T(8,128)(2,1)S(1)}, f32[1,48,128]{2,1,0:T(8,128)S(1)}, f32[1,48,128]{2,1,0:T(8,128)S(1)}, f32[1,48,128]{2,1,0:T(8,128)S(1)}, f32[1,48,128]{2,1,0:T(8,128)S(1)}) custom-call(s32[3]{0:T(128)S(1)} %pad_add_fusion.me_ref, s32[16]{0:T(128)S(1)} %multiply_add_fusion.code_ref, s32[16]{0:T(128)S(1)} %copy-done.4, ...), custom_call_target="tpu_custom_call" | custom-call | flops 1000000000 | bytes 1048576 | tf_op jit(solution)/shard_map/moments/pallas_call | solution.py:277
  38.6 4.3 %collective-permute-start.6 = (f32[1,48,128]{2,1,0:T(8,128)S(1)}, f32[1,48,128]{2,1,0:T(8,128)S(1)}, u32[]{:S(2)}, u32[]{:S(2)}) collective-permute-start(f32[1,48,128]{2,1,0:T(8,128)S(1)} %get-tuple-element.30), channel_id=1, source_target_pairs={{0,1},{1,2},{2,3},{3,0},{4,5},{5,6},{6,7},{7,4},{8,9},{9,10},{10,1... | collective-permute-start | bytes 73736 | tf_op jit(solution)/shard_map/ppermute | solution.py:514
  42.9 0.3 collective-permute-start.7
  43.1 0.2 collective-permute-start.8
  43.3 0.5 collective-permute-done.6
  43.8 1.7 %collective-permute-done.7 = f32[1,48,128]{2,1,0:T(8,128)S(1)} collective-permute-done((f32[1,48,128]{2,1,0:T(8,128)S(1)}, f32[1,48,128]{2,1,0:T(8,128)S(1)}, u32[]{:S(2)}, u32[]{:S(2)}) %collective-permute-start.7) | collective-permute-done | bytes 24608 | tf_op jit(solution)/shard_map/ppermute | solution.py:514
  45.5 0.8 %collective-permute-done.8 = f32[1,48,128]{2,1,0:T(8,128)S(1)} collective-permute-done((f32[1,48,128]{2,1,0:T(8,128)S(1)}, f32[1,48,128]{2,1,0:T(8,128)S(1)}, u32[]{:S(2)}, u32[]{:S(2)}) %collective-permute-start.8) | collective-permute-done | bytes 24608 | tf_op jit(solution)/shard_map/ppermute | solution.py:514
  46.4 2.9 %collective-permute-start.11 = (f32[1,48,128]{2,1,0:T(8,128)S(1)}, f32[1,48,128]{2,1,0:T(8,128)S(1)}, u32[]{:S(2)}, u32[]{:S(2)}) collective-permute-start(f32[1,48,128]{2,1,0:T(8,128)S(1)} %add_add_fusion.refs_0_), channel_id=1, source_target_pairs={{0,12},{4,0},{8,4},{12,8},{1,13},{5,1},{9,5},{13,9},{2,14},{6,2},{... | collective-permute-start | bytes 73736 | tf_op jit(solution)/shard_map/ppermute | solution.py:514
  49.3 0.4 collective-permute-start.9
  49.6 0.7 collective-permute-done.11.refs_3_
  50.3 3.1 %collective-permute-done.10.refs_2_ = f32[1,48,128]{2,1,0:T(8,128)S(1)} collective-permute-done((f32[1,48,128]{2,1,0:T(8,128)S(1)}, f32[1,48,128]{2,1,0:T(8,128)S(1)}, u32[]{:S(2)}, u32[]{:S(2)}) %collective-permute-start.10) | collective-permute-done | bytes 24608 | tf_op jit(solution)/shard_map/ppermute | solution.py:514
  53.4 0.9 %collective-permute-done.9.refs_1_ = f32[1,48,128]{2,1,0:T(8,128)S(1)} collective-permute-done((f32[1,48,128]{2,1,0:T(8,128)S(1)}, f32[1,48,128]{2,1,0:T(8,128)S(1)}, u32[]{:S(2)}, u32[]{:S(2)}) %collective-permute-start.9) | collective-permute-done | bytes 24608 | tf_op jit(solution)/shard_map/ppermute | solution.py:514
  54.3 4.6 %solve.1.refs_0_ = f32[1,8,128]{2,1,0:T(8,128)S(1)} custom-call(s32[14]{0:T(128)S(1)} %copy-done.2, f32[1,48,128]{2,1,0:T(8,128)S(1)} %add_add_fusion.refs_0_, f32[1,48,128]{2,1,0:T(8,128)S(1)} %collective-permute-done.9.refs_1_, f32[1,48,128]{2,1,0:T(8,128)S(1)} %collective-permute-done.10.refs_2_, f32[1,48,128]{2,1,0:T(8,128)S(1)} %collective-permute-done.11.refs_3_), custom_call_target="tpu_custom_call" | custom-call | tf_op jit(solution)/shard_map/solve/pallas_call | solution.py:392
  58.9 1.8 %collective-permute-start.14 = (f32[1,8,128]{2,1,0:T(8,128)S(1)}, f32[1,8,128]{2,1,0:T(8,128)S(1)}, u32[]{:S(2)}, u32[]{:S(2)}) collective-permute-start(f32[1,8,128]{2,1,0:T(8,128)S(1)} %solve.1.refs_0_), channel_id=1, source_target_pairs={{0,1},{1,2},{2,3},{3,0},{4,5},{5,6},{6,7},{7,4},{8,9},{9,10},{10,1... | collective-permute-start | bytes 12296 | tf_op jit(solution)/shard_map/ppermute | solution.py:514
  60.7 0.5 collective-permute-start.12
  61.2 0.3 collective-permute-done.14.refs_3_
  61.5 1.7 %collective-permute-done.13.refs_2_ = f32[1,8,128]{2,1,0:T(8,128)S(1)} collective-permute-done((f32[1,8,128]{2,1,0:T(8,128)S(1)}, f32[1,8,128]{2,1,0:T(8,128)S(1)}, u32[]{:S(2)}, u32[]{:S(2)}) %collective-permute-start.13) | collective-permute-done | bytes 4128 | tf_op jit(solution)/shard_map/ppermute | solution.py:514
  63.2 0.6 collective-permute-done.12.refs_1_
  63.8 4.2 %difference.1 = bf16[16,48,128]{2,1,0:T(8,128)(2,1)} custom-call(s32[3]{0:T(128)S(1)} %pad_add_fusion.me_ref, s32[16]{0:T(128)S(1)} %multiply_add_fusion.code_ref, s32[16]{0:T(128)S(1)} %copy-done.4, s32[16]{0:T(128)S(1)} %copy-done.6, f32[1,8,128]{2,1,0:T(8,128)S(1)} %solve.1.refs_0_, f32[1,8,128]{2,1,0:T(8,128)S(1)} %collective-permute-done.12.refs_1_, ...), custom_call_target="tpu_custom_call" | custom-call | tf_op jit(solution)/shard_map/difference/pallas_call | solution.py:488
  (17 shorter events, 0.0 us)
Async XLA Ops:
  0.7 7.0 %collective-permute-start.2 = (s32[16]{0:T(128)S(1)}, s32[16]{0:T(128)S(1)}, u32[]{:S(2)}, u32[]{:S(2)}) collective-permute-start(s32[16]{0:T(128)S(1)} %multiply_add_fusion.code_ref), channel_id=1, source_target_pairs={{0,12},{4,0},{8,4},{12,8},{1,13},{5,1},{9,5},{13,9},{2,14},{6,2},{... | collective-permute-start | bytes 200 | tf_op jit(solution)/shard_map/ppermute | solution.py:514
  4.8 3.3 %collective-permute-start.1 = (s32[16]{0:T(128)S(1)}, s32[16]{0:T(128)S(1)}, u32[]{:S(2)}, u32[]{:S(2)}) collective-permute-start(s32[16]{0:T(128)S(1)} %multiply_add_fusion.code_ref), channel_id=1, source_target_pairs={{0,8},{4,12},{8,0},{12,4},{1,9},{5,13},{9,1},{13,5},{2,10},{6,14},... | collective-permute-start | bytes 200 | tf_op jit(solution)/shard_map/ppermute | solution.py:514
  4.8 4.2 %collective-permute-start = (s32[16]{0:T(128)S(1)}, s32[16]{0:T(128)S(1)}, u32[]{:S(2)}, u32[]{:S(2)}) collective-permute-start(s32[16]{0:T(128)S(1)} %multiply_add_fusion.code_ref), channel_id=1, source_target_pairs={{0,4},{4,8},{8,12},{12,0},{1,5},{5,9},{9,13},{13,1},{2,6},{6,10},{... | collective-permute-start | bytes 200 | tf_op jit(solution)/shard_map/ppermute | solution.py:514
  9.0 1.0 %copy-start = (bf16[16,80,128]{2,1,0:T(8,128)(2,1)S(1)}, bf16[16,80,128]{2,1,0:T(8,128)(2,1)}, u32[]{:S(2)}) copy-start(bf16[16,80,128]{2,1,0:T(8,128)(2,1)} %plates.1) | copy-start | bytes 983044
  11.3 12.7 %collective-permute-start.5 = (bf16[8,80,128]{2,1,0:T(8,128)(2,1)S(1)}, bf16[8,80,128]{2,1,0:T(8,128)(2,1)S(1)}, u32[]{:S(2)}, u32[]{:S(2)}) collective-permute-start(bf16[8,80,128]{2,1,0:T(8,128)(2,1)S(1)} %get-tuple-element.27), channel_id=1, source_target_pairs={{0,8},{4,12},{8,0},{12,4},{1,9},{5,13},{9,1},{13,5},{2,10},{6,14},... | collective-permute-start | bytes 491528 | tf_op jit(solution)/shard_map/ppermute | solution.py:514
  12.3 15.5 %collective-permute-start.4 = (bf16[8,80,128]{2,1,0:T(8,128)(2,1)S(1)}, bf16[8,80,128]{2,1,0:T(8,128)(2,1)S(1)}, u32[]{:S(2)}, u32[]{:S(2)}) collective-permute-start(bf16[8,80,128]{2,1,0:T(8,128)(2,1)S(1)} %get-tuple-element.25), channel_id=1, source_target_pairs={{0,12},{4,0},{8,4},{12,8},{1,13},{5,1},{9,5},{13,9},{2,14},{6,2},{... | collective-permute-start | bytes 491528 | tf_op jit(solution)/shard_map/ppermute | solution.py:514
  14.7 1.0 %copy-start.1 = (bf16[16,80,128]{2,1,0:T(8,128)(2,1)S(1)}, bf16[16,80,128]{2,1,0:T(8,128)(2,1)}, u32[]{:S(2)}) copy-start(bf16[16,80,128]{2,1,0:T(8,128)(2,1)} %plates.1) | copy-start | bytes 983044
  15.7 0.7 copy-start.3
  16.4 0.7 copy-start.5
  17.0 0.9 %copy-start.7 = (bf16[16,48,128]{2,1,0:T(8,128)(2,1)S(1)}, bf16[16,48,128]{2,1,0:T(8,128)(2,1)}, u32[]{:S(2)}) copy-start(bf16[16,48,128]{2,1,0:T(8,128)(2,1)} %science.7) | copy-start | bytes 589828
  17.9 6.0 %copy-start.6 = (s32[16]{0:T(128)S(1)}, s32[16]{0:T(128)}, u32[]{:S(2)}) copy-start(s32[16]{0:T(128)} %good_ref.9) | copy-start | bytes 196
  21.8 6.0 %copy-start.8 = (bf16[16,48,128]{2,1,0:T(8,128)(2,1)S(1)}, bf16[16,48,128]{2,1,0:T(8,128)(2,1)}, u32[]{:S(2)}) copy-start(bf16[16,48,128]{2,1,0:T(8,128)(2,1)} %science.7) | copy-start | bytes 589828
  21.8 12.9 %collective-permute-start.3 = (bf16[8,80,128]{2,1,0:T(8,128)(2,1)S(1)}, bf16[8,80,128]{2,1,0:T(8,128)(2,1)S(1)}, u32[]{:S(2)}, u32[]{:S(2)}) collective-permute-start(bf16[8,80,128]{2,1,0:T(8,128)(2,1)S(1)} %get-tuple-element.21), channel_id=1, source_target_pairs={{0,4},{4,8},{8,12},{12,0},{1,5},{5,9},{9,13},{13,1},{2,6},{6,10},{... | collective-permute-start | bytes 491528 | tf_op jit(solution)/shard_map/ppermute | solution.py:514
  27.8 6.9 %copy-start.4 = (s32[16]{0:T(128)S(1)}, s32[16]{0:T(128)}, u32[]{:S(2)}) copy-start(s32[16]{0:T(128)} %row_ref.9) | copy-start | bytes 196
  34.7 19.6 %copy-start.2 = (s32[14]{0:T(128)S(1)}, s32[14]{0:T(128)}, u32[]{:S(2)}) copy-start(s32[14]{0:T(128)} %order_ref.1) | copy-start | bytes 172
  38.6 5.3 %collective-permute-start.6 = (f32[1,48,128]{2,1,0:T(8,128)S(1)}, f32[1,48,128]{2,1,0:T(8,128)S(1)}, u32[]{:S(2)}, u32[]{:S(2)}) collective-permute-start(f32[1,48,128]{2,1,0:T(8,128)S(1)} %get-tuple-element.30), channel_id=1, source_target_pairs={{0,1},{1,2},{2,3},{3,0},{4,5},{5,6},{6,7},{7,4},{8,9},{9,10},{10,1... | collective-permute-start | bytes 73736 | tf_op jit(solution)/shard_map/ppermute | solution.py:514
  42.9 2.7 %collective-permute-start.7 = (f32[1,48,128]{2,1,0:T(8,128)S(1)}, f32[1,48,128]{2,1,0:T(8,128)S(1)}, u32[]{:S(2)}, u32[]{:S(2)}) collective-permute-start(f32[1,48,128]{2,1,0:T(8,128)S(1)} %get-tuple-element.31), channel_id=1, source_target_pairs={{0,2},{1,3},{2,0},{3,1},{4,6},{5,7},{6,4},{7,5},{8,10},{9,11},{10,... | collective-permute-start | bytes 73736 | tf_op jit(solution)/shard_map/ppermute | solution.py:514
  43.1 3.3 %collective-permute-start.8 = (f32[1,48,128]{2,1,0:T(8,128)S(1)}, f32[1,48,128]{2,1,0:T(8,128)S(1)}, u32[]{:S(2)}, u32[]{:S(2)}) collective-permute-start(f32[1,48,128]{2,1,0:T(8,128)S(1)} %get-tuple-element.32), channel_id=1, source_target_pairs={{0,3},{1,0},{2,1},{3,2},{4,7},{5,4},{6,5},{7,6},{8,11},{9,8},{10,9... | collective-permute-start | bytes 73736 | tf_op jit(solution)/shard_map/ppermute | solution.py:514
  46.4 3.9 %collective-permute-start.11 = (f32[1,48,128]{2,1,0:T(8,128)S(1)}, f32[1,48,128]{2,1,0:T(8,128)S(1)}, u32[]{:S(2)}, u32[]{:S(2)}) collective-permute-start(f32[1,48,128]{2,1,0:T(8,128)S(1)} %add_add_fusion.refs_0_), channel_id=1, source_target_pairs={{0,12},{4,0},{8,4},{12,8},{1,13},{5,1},{9,5},{13,9},{2,14},{6,2},{... | collective-permute-start | bytes 73736 | tf_op jit(solution)/shard_map/ppermute | solution.py:514
  49.2 4.1 %collective-permute-start.10 = (f32[1,48,128]{2,1,0:T(8,128)S(1)}, f32[1,48,128]{2,1,0:T(8,128)S(1)}, u32[]{:S(2)}, u32[]{:S(2)}) collective-permute-start(f32[1,48,128]{2,1,0:T(8,128)S(1)} %add_add_fusion.refs_0_), channel_id=1, source_target_pairs={{0,8},{4,12},{8,0},{12,4},{1,9},{5,13},{9,1},{13,5},{2,10},{6,14},... | collective-permute-start | bytes 73736 | tf_op jit(solution)/shard_map/ppermute | solution.py:514
  49.3 5.0 %collective-permute-start.9 = (f32[1,48,128]{2,1,0:T(8,128)S(1)}, f32[1,48,128]{2,1,0:T(8,128)S(1)}, u32[]{:S(2)}, u32[]{:S(2)}) collective-permute-start(f32[1,48,128]{2,1,0:T(8,128)S(1)} %add_add_fusion.refs_0_), channel_id=1, source_target_pairs={{0,4},{4,8},{8,12},{12,0},{1,5},{5,9},{9,13},{13,1},{2,6},{6,10},{... | collective-permute-start | bytes 73736 | tf_op jit(solution)/shard_map/ppermute | solution.py:514
  58.9 2.6 %collective-permute-start.14 = (f32[1,8,128]{2,1,0:T(8,128)S(1)}, f32[1,8,128]{2,1,0:T(8,128)S(1)}, u32[]{:S(2)}, u32[]{:S(2)}) collective-permute-start(f32[1,8,128]{2,1,0:T(8,128)S(1)} %solve.1.refs_0_), channel_id=1, source_target_pairs={{0,1},{1,2},{2,3},{3,0},{4,5},{5,6},{6,7},{7,4},{8,9},{9,10},{10,1... | collective-permute-start | bytes 12296 | tf_op jit(solution)/shard_map/ppermute | solution.py:514
  60.7 2.5 %collective-permute-start.13 = (f32[1,8,128]{2,1,0:T(8,128)S(1)}, f32[1,8,128]{2,1,0:T(8,128)S(1)}, u32[]{:S(2)}, u32[]{:S(2)}) collective-permute-start(f32[1,8,128]{2,1,0:T(8,128)S(1)} %solve.1.refs_0_), channel_id=1, source_target_pairs={{0,2},{1,3},{2,0},{3,1},{4,6},{5,7},{6,4},{7,5},{8,10},{9,11},{10,... | collective-permute-start | bytes 12296 | tf_op jit(solution)/shard_map/ppermute | solution.py:514
  60.7 3.1 %collective-permute-start.12 = (f32[1,8,128]{2,1,0:T(8,128)S(1)}, f32[1,8,128]{2,1,0:T(8,128)S(1)}, u32[]{:S(2)}, u32[]{:S(2)}) collective-permute-start(f32[1,8,128]{2,1,0:T(8,128)S(1)} %solve.1.refs_0_), channel_id=1, source_target_pairs={{0,3},{1,0},{2,1},{3,2},{4,7},{5,4},{6,5},{7,6},{8,11},{9,8},{10,9... | collective-permute-start | bytes 12296 | tf_op jit(solution)/shard_map/ppermute | solution.py:514

commit v3 on v2

v3 whole, which is shorter than its diff:
```python
import functools

import jax
import jax.numpy as jnp
from jax import lax
from jax.experimental import pallas as pl
from jax.experimental.pallas import tpu as pltpu
from jax.sharding import PartitionSpec as P

PATCH_ROWS = 4000
RIDGE = 0.01
TERMS = ((0, 0), (2, 0), (0, 2), (1, 0), (0, 1), (1, 1))
LEFT = 3
BATCH = 4
PAIR = 2
VMEM = pl.BlockSpec(memory_space=pltpu.VMEM)
SMEM = pl.BlockSpec(memory_space=pltpu.SMEM)
CODE, ROW, GOOD, PATCH, ME, CCD = range(6)
OWN, REST, GROUP, START = range(4)
F32, BF16, I32 = jnp.float32, jnp.bfloat16, jnp.int32


def block_of(a, b):
    want = (TERMS[a][0] + TERMS[b][0], TERMS[a][1] + TERMS[b][1])
    for left in range(LEFT):
        for right in range(len(TERMS)):
            if (TERMS[left][0] + TERMS[right][0], TERMS[left][1] + TERMS[right][1]) == want:
                return left, right
    raise ValueError(want)


def params(mebibytes):
    return pltpu.CompilerParams(vmem_limit_bytes=mebibytes * 1024 * 1024)


def prepare_kernel(
    rows_ref,
    cols_ref,
    template,
    science,
    row_out,
    col_out,
    template_out,
    science_out,
    taps_held,
):
    kernels, taps = rows_ref.shape
    rows, columns = science.shape[1:]
    reach = template_out.shape[1]
    middle = taps // 2
    lag = (template.shape[1] - rows) // 2 - middle
    template_out[...] = template[:, lag : lag + reach, :]
    science_out[...] = science[...]
    taps_held[...] = jnp.zeros_like(taps_held)
    taps_held[0, :kernels, :taps] = rows_ref[...].astype(F32)
    taps_held[1, :kernels, :taps] = cols_ref[...].astype(F32)
    k = lax.broadcasted_iota(I32, (columns, columns), 0)
    lane = lax.broadcasted_iota(I32, (columns, columns), 1)
    moved_to = (k < taps) & ((k + lane == middle) | (k + lane == middle + columns))
    placed = jnp.dot(
        taps_held[1].astype(BF16),
        jnp.where(moved_to, 1.0, 0.0).astype(BF16),
        preferred_element_type=F32,
    )
    band = (k - lane <= middle) & (lane - k <= middle)
    for n in range(kernels):
        taps_n = jnp.broadcast_to(taps_held[0, n : n + 1, :], (rows, columns))
        moved = pltpu.roll(taps_n, 0, 1, stride=1, stride_axis=0)
        row_out[n * rows : (n + 1) * rows, :] = moved[:, :reach].astype(BF16)
        taps_n = jnp.broadcast_to(placed[n : n + 1, :], (columns, columns))
        moved = pltpu.roll(taps_n, 0, 1, stride=1, stride_axis=0)
        col_out[n] = jnp.where(band, moved, 0.0).astype(BF16)


def prepare(basis_rows, basis_cols, template, science):
    rows, columns = science.shape[1:]
    tiles, tile_rows = template.shape[:2]
    kernels, taps = basis_rows.shape
    reach = min(-(-(rows + taps - 1) // 8) * 8, (tile_rows + rows) // 2 + taps // 2)
    held_rows = -(-kernels // 16) * 16
    return pl.pallas_call(
        prepare_kernel,
        out_shape=(
            jax.ShapeDtypeStruct((kernels * rows, reach), BF16),
            jax.ShapeDtypeStruct((kernels, columns, columns), BF16),
            jax.ShapeDtypeStruct((tiles, reach, columns), BF16),
            jax.ShapeDtypeStruct(science.shape, BF16),
        ),
        in_specs=[VMEM] * 4,
        out_specs=[VMEM] * 4,
        scratch_shapes=[pltpu.VMEM((2, held_rows, columns), F32)],
        compiler_params=params(8),
        name="prepare",
    )(basis_rows, basis_cols, template, science)


def select_kernel(facts_ref, *refs, shifts, strips, tiles, capacity):
    others, template, outs = refs[:shifts], refs[shifts], refs[shifts + 1 : -1]
    listing = refs[-1]
    low = facts_ref[ME, 0] * tiles
    for other, out in zip(others, outs):
        for j in range(capacity):
            listing[j] = 0
        count = jnp.int32(0)
        for s in range(strips):
            tile = other[s] - low
            hit = (tile >= 0) & (tile < tiles)
            listing[count] = jnp.where(hit, tile, 0)
            count = count + hit.astype(I32)
        for j in range(capacity):
            out[j] = template[listing[j]]


def select_tiles(facts, others, template, capacity):
    shifts = len(others)
    strips = facts.shape[1]
    tiles, tile_rows, columns = template.shape
    return pl.pallas_call(
        functools.partial(
            select_kernel, shifts=shifts, strips=strips, tiles=tiles, capacity=capacity
        ),
        out_shape=[jax.ShapeDtypeStruct((capacity, tile_rows, columns), BF16)] * shifts,
        in_specs=[SMEM] * (1 + shifts) + [VMEM],
        out_specs=[VMEM] * shifts,
        scratch_shapes=[pltpu.SMEM((strips + capacity,), I32)],
        compiler_params=params(8),
        name="select",
    )(facts, *others, template)


def across_rows(columns):
    c = lax.broadcasted_iota(I32, (8, columns), 1)
    return (2 * c + 1).astype(F32) / columns - 1.0


def place(facts_ref, patch, patches):
    d = patch - facts_ref[ME, 0]
    return jnp.where(d < 0, d + patches, d)


def patch_at(facts_ref, e, k, ccds, patches):
    owner = facts_ref[CCD, 0] + e
    owner = jnp.where(owner >= ccds, owner - ccds, owner)
    return jnp.minimum(k * ccds + owner, patches - 1)


def write_lists(facts_ref, lists, patches, strips):
    me = facts_ref[ME, 0]
    groups = []
    for s in range(strips):
        d = facts_ref[PATCH, s] - me
        groups.append(jnp.where(d < 0, d + patches, d))

    def gather(d, row, count):
        for s in range(strips):
            lists[row, count] = s
            if row == REST:
                lists[GROUP, count] = d
            count = count + (groups[s] == d).astype(I32)
        return count

    def step(d, count):
        lists[START, d] = count
        return gather(d, REST, count)

    last = lists.shape[1] - 1
    lists[OWN, last] = gather(0, OWN, jnp.int32(0))
    lists[REST, last] = lax.fori_loop(1, patches, step, jnp.int32(0))


def moments_kernel(facts_ref, *refs, own, sizes):
    capacity, patches, ccds, share, tiles, kernels, planes = sizes
    if own:
        science, row_table, col_table, plates, lists, planes_out, sums, p32, running = refs
    else:
        lists, science, row_table, col_table, before, *arrived = refs[: -4 - ccds]
        planes_out, outs = refs[-4 - ccds], refs[-3 - ccds : -3]
        p32, running, plates = refs[-3:]
    strips, rows, columns = science.shape
    span = rows * planes
    unknowns = len(TERMS) * planes
    if kernels + 2 < planes:
        p32[...] = jnp.zeros_like(p32)
    across = jnp.concatenate([across_rows(columns)] * (planes // 8), axis=0)
    across = across.astype(BF16)
    step_rows = 8

    def gram(first_b, chosen, slots):
        offsets = [facts_ref[ROW, strip] for strip in chosen]
        totals = [jnp.zeros((unknowns, LEFT * planes), F32) for _ in chosen]
        row_iota = lax.broadcasted_iota(I32, (rows, columns), 0)
        heights = [
            (2 * (offset + row_iota) + 1).astype(F32) / PATCH_ROWS - 1.0 for offset in offsets
        ]
        for chunk in range(rows // step_rows):
            operands = []
            for i in range(len(chosen)):
                pieces = [[] for _ in TERMS]
                for r in range(chunk * step_rows, (chunk + 1) * step_rows):
                    at = r * planes
                    base = (first_b + i) * span + at
                    value = p32[base : base + planes, :].astype(BF16)
                    planes_out[slots[i], at : at + planes, :] = value
                    v = jnp.concatenate([jnp.broadcast_to(heights[i][r : r + 1], (8, columns))] * (planes // 8), axis=0)
                    with_v = value.astype(F32) * v
                    with_u = value * across
                    once = with_v.astype(BF16)
                    pieces[0].append(value)
                    pieces[1].append((with_v * v).astype(BF16))
                    pieces[2].append(with_u * across)
                    pieces[3].append(once)
                    pieces[4].append(with_u)
                    pieces[5].append(once * across)
                wide = [jnp.concatenate(part, axis=1) for part in pieces]
                operands.append(
                    (jnp.concatenate(wide, axis=0), jnp.concatenate(wide[:LEFT], axis=0))
                )
            for i, (every, left) in enumerate(operands):
                totals[i] = totals[i] + lax.dot_general(
                    every, left, (((1,), (1,)), ((), ())), preferred_element_type=F32
                )
        return totals

    if own:
        write_lists(facts_ref, lists, patches, strips)
    else:
        for d in range(1, patches):
            start = lists[START, d]
            source, base = (arrived[0], (d - 1) * capacity) if len(arrived) == 1 else (arrived[d - 1], 0)
            for i in range(capacity):
                plates[start + i] = source[base + i]
    row = OWN if own else REST
    count = lists[row, lists.shape[1] - 1]
    half = LEFT * planes
    running[...] = jnp.zeros_like(running)

    def batch(t, carry):
        slots = [t * BATCH + b for b in range(BATCH)]
        at = [jnp.minimum(slot, count - 1) for slot in slots]
        chosen = [lists[row, x] for x in at]
        if own:
            low = facts_ref[ME, 0] * tiles
            groups = [0] * BATCH
            stack = [plates[facts_ref[CODE, s] - low] for s in chosen]
        else:
            groups = [lists[GROUP, x] for x in at]
            stack = [plates[x] for x in at]
        smoothed = jnp.dot(
            row_table[...], jnp.concatenate(stack, axis=1), preferred_element_type=F32
        ).astype(BF16)
        usable = [
            jnp.where(
                lax.broadcasted_iota(I32, (rows, columns), 0)
                < jnp.where(slot < count, facts_ref[GOOD, strip], 0),
                1.0,
                0.0,
            )
            for slot, strip in zip(slots, chosen)
        ]
        for n in range(kernels):
            part = smoothed[n * rows : (n + 1) * rows]
            lhs = jnp.concatenate(
                [part[:, b * columns : (b + 1) * columns] for b in range(BATCH)], axis=0
            )
            convolved = jnp.dot(lhs, col_table[n], preferred_element_type=F32)
            for b in range(BATCH):
                p32[pl.ds(b * span + n, rows, stride=planes), :] = (
                    convolved[b * rows : (b + 1) * rows] * usable[b]
                )
        for b in range(BATCH):
            p32[pl.ds(b * span + kernels, rows, stride=planes), :] = usable[b]
            p32[pl.ds(b * span + planes - 1, rows, stride=planes), :] = (
                science[chosen[b]].astype(F32) * usable[b]
            )
        for b in range(0, BATCH, PAIR):

            @pl.when(slots[b] < count)
            def _(b=b):
                totals = gram(b, chosen[b : b + PAIR], slots[b : b + PAIR])
                for d, total in zip(groups[b : b + PAIR], totals):
                    running[d, :, :half] += total

        return carry

    lax.fori_loop(0, (count + BATCH - 1) // BATCH, batch, 0)

    def packed(total):
        return total[:half] + pltpu.roll(total[half:], half, 1)

    if own:
        sums[...] = packed(running[0])
        return
    running[0, :half] = before[...]
    for d in range(1, patches):
        running[d, :half] = packed(running[d])
    for e in range(ccds):
        for k in range(share):
            d = place(facts_ref, patch_at(facts_ref, e, k, ccds, patches), patches)
            outs[e][k] = running[d, :half]


def moments_call(facts, lists, science, tables, before, plates, sizes):
    capacity, patches, ccds, share, tiles, kernels, planes = sizes
    strips, rows, columns = science.shape
    own = before is None
    held = -(-strips // BATCH) * BATCH
    one_sum = (LEFT * planes, 128)
    scratch = [
        pltpu.VMEM((BATCH * rows * planes, columns), F32),
        pltpu.VMEM((1 if own else patches, len(TERMS) * planes, 128), F32),
    ]
    if own:
        held = min(held, -(-capacity // BATCH) * BATCH)
        arguments = [facts, science, *tables, *plates]
        outs = [jax.ShapeDtypeStruct((4, max(strips, patches) + 2), I32)]
        sums = [jax.ShapeDtypeStruct(one_sum, F32)]
    else:
        arguments = [facts, lists, science, *tables, before, *plates]
        outs = []
        sums = [jax.ShapeDtypeStruct((share,) + one_sum, F32)] * ccds
        scratch.append(pltpu.VMEM((strips + capacity,) + plates[0].shape[1:], BF16))
    scalars = 1 if own else 2
    return pl.pallas_call(
        functools.partial(moments_kernel, own=own, sizes=sizes),
        out_shape=outs + [jax.ShapeDtypeStruct((held, rows * planes, columns), BF16)] + sums,
        in_specs=[SMEM] * scalars + [VMEM] * (len(arguments) - scalars),
        out_specs=[SMEM] * len(outs) + [VMEM] * (1 + len(sums)),
        scratch_shapes=scratch,
        compiler_params=params(20),
        cost_estimate=pl.CostEstimate(flops=1 << 20, bytes_accessed=1 << 10, transcendentals=0),
        name="moments",
    )(*arguments)


def solve_kernel(order_ref, *refs, kernels, planes):
    parts, out = refs[:-1], refs[-1]
    terms = len(TERMS)
    size = terms * planes
    lane = lax.broadcasted_iota(I32, (size, 128), 1)
    sub = lax.broadcasted_iota(I32, (size, 128), 0)

    def activity(index):
        plane, term = index % planes, index // planes
        order = jnp.zeros_like(index)
        for i in range(kernels):
            order = jnp.where(plane == i, order_ref[i], order)
        degree = jnp.zeros_like(index)
        for t, powers in enumerate(TERMS):
            degree = jnp.where(term == t, powers[0] + powers[1], degree)
        wanted = (plane == kernels) | ((plane < kernels) & (degree <= order))
        return jnp.where(wanted & (index < size), 1.0, 0.0)

    active_row = activity(lane[:8])
    active_row = jnp.concatenate([active_row] * (size // 8), axis=0)
    active_col = activity(sub)
    lane16 = lane[:planes]
    row8 = lax.broadcasted_iota(I32, (8, 128), 0)
    for q in range(out.shape[0]):
        moments = parts[0][q]
        for ref in parts[1:]:
            moments = moments + ref[q]
        rows = []
        for a in range(terms):
            row = jnp.zeros((planes, 128), F32)
            for b in range(terms):
                left, right = block_of(a, b)
                at = right % LEFT * planes
                place = right // LEFT * LEFT + left
                piece = moments[at : at + planes]
                if b != place:
                    piece = pltpu.roll(piece, ((b - place) * planes) % 128, 1)
                row = jnp.where(lane16 // planes == b, piece, row)
            rows.append(row)
        paired = jnp.concatenate(rows, axis=0)
        target = pltpu.roll(paired, size - (planes - 1), 1)
        masked = active_row * active_col * paired
        system = jnp.where(lane == sub, masked + (1.0 + RIDGE * masked), masked)
        system = jnp.where(lane == size, active_col * target, system)
        blocks = [system[8 * m : 8 * m + 8] for m in range(size // 8)]
        for at in range(size // 8):
            wanted = [i for i in range(8) if (8 * at + i) % planes <= kernels]
            columns = [
                {i: jnp.broadcast_to(block[:, 8 * at + i : 8 * at + i + 1], (8, 128)) for i in wanted}
                for block in blocks
            ]
            inner, here = columns[at], blocks[at]
            for i in wanted:
                scale = 1.0 / jnp.broadcast_to(inner[i][i : i + 1], (8, 128))
                line = jnp.broadcast_to(here[i : i + 1], (8, 128)) * scale
                here = jnp.where(row8 == i, line, here - inner[i] * line)
                for k in wanted:
                    if k > i:
                        entry = jnp.broadcast_to(inner[k][i : i + 1], (8, 128)) * scale
                        inner[k] = jnp.where(row8 == i, entry, inner[k] - inner[i] * entry)
            lines = {i: jnp.broadcast_to(here[i : i + 1], (8, 128)) for i in wanted}
            for m in range(size // 8):
                if m == at:
                    blocks[m] = here
                    continue
                terms_here = [columns[m][i] * lines[i] for i in wanted]
                while len(terms_here) > 1:
                    terms_here = [
                        functools.reduce(lambda a, b: a + b, terms_here[q : q + 2])
                        for q in range(0, len(terms_here), 2)
                    ]
                blocks[m] = blocks[m] - terms_here[0]
        answer = jnp.concatenate(blocks, axis=0)
        answer = jnp.broadcast_to(answer[:, size : size + 1], (size, 128))
        answer = jnp.where(sub % planes == lane % planes, answer, 0.0)
        lines = [
            jnp.sum(answer[t * planes : (t + 1) * planes], axis=0, keepdims=True)
            for t in range(terms)
        ]
        lines.append(jnp.zeros((8 - terms, 128), F32))
        out[q] = jnp.concatenate(lines, axis=0)


def solve(order, parts, kernels, planes):
    return pl.pallas_call(
        functools.partial(solve_kernel, kernels=kernels, planes=planes),
        out_shape=jax.ShapeDtypeStruct((parts[0].shape[0], 8, 128), F32),
        in_specs=[SMEM] + [VMEM] * len(parts),
        out_specs=VMEM,
        compiler_params=params(4),
        name="solve",
    )(order, *parts)


def difference_kernel(facts_ref, lists, *refs, sizes, tall):
    capacity, patches, ccds, share, tiles, kernels, planes = sizes
    coefs, stacks = refs[:ccds], refs[ccds : ccds + 2]
    out, table = refs[ccds + 2 :]
    strips, rows, columns = out.shape
    across = jnp.concatenate([across_rows(columns)] * (tall // 8), axis=0)
    across2 = across * across
    width = tall * planes
    lane = lax.broadcasted_iota(I32, (tall, width), 1)
    diagonal = lane // planes == lax.broadcasted_iota(I32, (tall, width), 0)
    is_science = diagonal & (lane % planes == planes - 1)
    sub = lax.broadcasted_iota(I32, (tall, columns), 0)

    def pieces(value):
        high = value.astype(BF16)
        rest = value - high.astype(F32)
        return high, rest.astype(BF16)

    for e in range(ccds):
        for k in range(share):
            d = place(facts_ref, patch_at(facts_ref, e, k, ccds, patches), patches)
            block = coefs[e][k]
            for t in range(len(TERMS)):
                line = jnp.concatenate([block[t : t + 1]] * (width // 128), axis=1)
                value = jnp.where(diagonal, -jnp.broadcast_to(line, (tall, width)), 0.0)
                table[d, t] = jnp.where(is_science, 1.0, value) if t == 0 else value

    for row, stack in zip((OWN, REST), stacks):
        count = lists[row, lists.shape[1] - 1]

        def step(t, carry, row=row, stack=stack, count=count):
            for i in range(PAIR):
                j = jnp.minimum(t * PAIR + i, count - 1)
                strip = lists[row, j]
                d = 0 if row == OWN else lists[GROUP, j]
                coef = [table[d, t] for t in range(len(TERMS))]
                twice = pieces(coef[2])
                offset, good = facts_ref[ROW, strip], facts_ref[GOOD, strip]
                for h in range(rows // tall):
                    v = (2 * (offset + h * tall + sub) + 1).astype(F32) / PATCH_ROWS - 1.0
                    v = jnp.concatenate([v] * (width // 128), axis=1)
                    plain = coef[0] + v * (coef[3] + v * coef[1])
                    once = coef[4] + v * coef[5]
                    lhs = jnp.concatenate([*pieces(plain), *pieces(once), *twice], axis=0)
                    rhs = stack[j, h * width : (h + 1) * width, :]
                    got = jnp.dot(lhs, rhs, preferred_element_type=F32)
                    part = [got[x * tall : (x + 1) * tall] for x in range(6)]
                    value = (
                        (part[0] + part[1])
                        + across * (part[2] + part[3])
                        + across2 * (part[4] + part[5])
                    )
                    value = jnp.where(h * tall + sub < good, value, 0.0)
                    out[strip, h * tall : (h + 1) * tall, :] = value.astype(BF16)
            return carry

        lax.fori_loop(0, (count + PAIR - 1) // PAIR, step, 0)


def difference(facts, lists, coefs, stacks, shape, sizes):
    patches, planes, tall = sizes[1], sizes[-1], 16
    return pl.pallas_call(
        functools.partial(difference_kernel, sizes=sizes, tall=tall),
        out_shape=jax.ShapeDtypeStruct(shape, BF16),
        in_specs=[SMEM] * 2 + [VMEM] * (len(coefs) + len(stacks)),
        out_specs=VMEM,
        scratch_shapes=[pltpu.VMEM((patches, len(TERMS), tall, tall * planes), F32)],
        compiler_params=params(20),
        name="difference",
    )(facts, lists, *coefs, *stacks)


def shifted(value, axis, shift):
    size = lax.axis_size(axis)
    return lax.ppermute(value, axis, [(i, (i + shift) % size) for i in range(size)])


def body(
    science,
    strip_patch,
    strip_tile,
    strip_row,
    row_count,
    template,
    basis_rows,
    basis_cols,
    basis_order,
):
    patches, ccds = lax.axis_size("patch"), lax.axis_size("ccd")
    strips = science.shape[0]
    tiles = template.shape[0]
    kernels = basis_rows.shape[0]
    planes = -(-(kernels + 2) // 16) * 16
    capacity = max(2, 2 * strips // patches)
    share = -(-patches // ccds)
    sizes = (capacity, patches, ccds, share, tiles, kernels, planes)
    code = strip_patch * tiles + strip_tile
    others = [shifted(code, "patch", d) for d in range(1, patches)]
    facts = jnp.stack(
        [code, strip_row, row_count, strip_patch]
        + [jnp.full_like(code, lax.axis_index(axis)) for axis in ("patch", "ccd")]
    )
    *tables, template, science = prepare(basis_rows, basis_cols, template, science)
    chosen = select_tiles(facts, others, template, capacity)
    plates = [shifted(tile, "patch", patches - d) for d, tile in enumerate(chosen, 1)]
    if patches > 8:
        plates = [jnp.concatenate(plates, axis=0)]
    lists, own_planes, before = moments_call(facts, None, science, tables, None, [template], sizes)
    planes_left, *scattered = moments_call(facts, lists, science, tables, before, plates, sizes)
    mine = scattered[0]
    for e in range(1, ccds):
        mine = mine + shifted(scattered[e], "ccd", e)
    parts = [mine] + [shifted(mine, "patch", d) for d in range(1, patches)]
    coefficients = solve(basis_order, parts, kernels, planes)
    coefs = [coefficients] + [shifted(coefficients, "ccd", ccds - e) for e in range(1, ccds)]
    return difference(facts, lists, coefs, [own_planes, planes_left], science.shape, sizes)


def solution(mesh):
    spread = P(("groups", "patch", "ccd"))
    return jax.shard_map(
        body,
        mesh=mesh,
        in_specs=(spread,) * 6 + (P(), P(), P()),
        out_specs=spread,
        check_vma=False,
    )
```

time: 68 us -> 62.4 us (0.918)
  Pallas kernels: 28.6 us -> 21.5 us
  waiting for transfers between devices: 11.6 us -> 15 us
  local copies, waits for them, and re-layouts: 5.87 us -> 3.99 us
  other arithmetic: 1.53 us -> 0.7 us
    pallas_call x7 -> x5, Pallas kernels: 24 us -> 16.9 us  [the longest x2 12.4 us: moments_call(): pl.pallas_call(functools.partial(moments_kernel, own=own, sizes=sizes), o...]
    ppermute x15, waiting for transfers between devices: 11.6 us -> 15 us  [shifted(): lax.ppermute(value, axis, [(i, (i + shift) % size) for i in range(size)])]
    unnamed x18 -> x10, local copies, waits for them, and re-layouts: 4.2 us -> 3.27 us
    slice x3 -> x0, local copies, waits for them, and re-layouts: 0.9 us -> none  [make_tables(): jnp.roll(jnp.pad(basis_cols.astype(F32)[:, ::-1], pad), -(taps // 2), axi...]
    rev x1 -> x0, local copies, waits for them, and re-layouts: 0.76 us -> none  [make_tables(): basis_cols.astype(F32)[:, ::-1]]
    another operation x0 -> x3, local copies, waits for them, and re-layouts: none -> 0.72 us  [body(): jnp.stack([code, strip_row, row_count, strip_patch] + [jnp.full_like(code...]
    pad x1 -> x0, other arithmetic: 0.69 us -> none  [make_tables(): jnp.pad(basis_rows.astype(F32), pad)]
  transfers between devices with their start and end apart: 15 -> 15, of which waited for: 11 -> 8; matrix products, arithmetic and copies ran while one was open for 4% -> 1% of each run, Pallas kernels for 22% -> 11%
where the time goes in v3:
time: 62.4 us; the launch traced here: 62.2 us
  Pallas kernels  21.5 us (34%)
  starting transfers between devices  20.8 us (33%)
  waiting for transfers between devices  15 us (24%)
  local copies, waits for them, and re-layouts  3.99 us (6%)
  other arithmetic  0.7 us (1%)
    ppermute x15, starting transfers between devices, shifted(): lax.ppermute(value, axis, [(i, (i + shift) % size) for i in range(size)])  20.8 us
    ppermute x15, waiting for transfers between devices, shifted(): lax.ppermute(value, axis, [(i, (i + shift) % size) for i in range(size)])  15 us
    pallas_call x2, Pallas kernels, moments_call(): pl.pallas_call(functools.partial(moments_kernel, own=own, sizes=sizes), o...  12.4 us
    pallas_call x1, Pallas kernels, solve(): pl.pallas_call(functools.partial(solve_kernel, kernels=kernels, planes=pl...  4.6 us
    pallas_call x1, Pallas kernels, difference(): pl.pallas_call(functools.partial(difference_kernel, sizes=sizes, tall=tal...  3.3 us
    unnamed x10, local copies, waits for them, and re-layouts  3.27 us
  transfers between devices with their start and end apart: 15, of which 8 were waited for; matrix products, arithmetic and copies ran while one was open for 1% of the time, Pallas kernels for 11%

profile of v3, /device:TPU:1, one launch (start us, length us, event | category | flops | bytes accessed | tf_op | source)
XLA Modules:
  0.0 62.2 jit_solution(14252399913628213910)
XLA Ops:
  0.0 0.0 copy-start.4
  0.0 0.7 %multiply_add_fusion = s32[16]{0:T(128)S(1)} fusion(s32[16]{0:T(128)} %param.11, s32[16]{0:T(128)} %param.10), kind=kLoop, calls=%fused_computation.1 | loop fusion | flops 32 | bytes 192 | tf_op jit(solution)/shard_map/add | solution.py:525
  0.7 4.2 %collective-permute-start.2 = (s32[16]{0:T(128)S(1)}, s32[16]{0:T(128)S(1)}, u32[]{:S(2)}, u32[]{:S(2)}) collective-permute-start(s32[16]{0:T(128)S(1)} %multiply_add_fusion), channel_id=1, source_target_pairs={{0,12},{4,0},{8,4},{12,8},{1,13},{5,1},{9,5},{13,9},{2,14},{6,2},{... | collective-permute-start | bytes 200 | tf_op jit(solution)/shard_map/ppermute | solution.py:503
  4.8 0.0 collective-permute-start.1
  4.8 0.5 collective-permute-start
  5.3 0.0 copy-start
  5.3 1.0 %copy-done = bf16[16,80,128]{2,1,0:T(8,128)(2,1)S(1)} copy-done((bf16[16,80,128]{2,1,0:T(8,128)(2,1)S(1)}, bf16[16,80,128]{2,1,0:T(8,128)(2,1)}, u32[]{:S(2)}) %copy-start) | copy-done | bytes 327704
  6.3 0.0 copy-start.1
  6.3 0.9 %copy-done.1 = bf16[16,48,128]{2,1,0:T(8,128)(2,1)S(1)} copy-done((bf16[16,48,128]{2,1,0:T(8,128)(2,1)S(1)}, bf16[16,48,128]{2,1,0:T(8,128)(2,1)}, u32[]{:S(2)}) %copy-start.1) | copy-done | bytes 196632
  7.2 0.0 copy-start.2
  7.2 0.7 %copy-done.2 = bf16[14,21]{1,0:T(8,128)(2,1)S(1)} copy-done((bf16[14,21]{1,0:T(8,128)(2,1)S(1)}, bf16[14,21]{1,0:T(8,128)(2,1)}, u32[]{:S(2)}) %copy-start.2) | copy-done | bytes 612
  7.9 0.0 copy-start.3
  7.9 0.7 %copy-done.3 = bf16[14,21]{1,0:T(8,128)(2,1)S(1)} copy-done((bf16[14,21]{1,0:T(8,128)(2,1)S(1)}, bf16[14,21]{1,0:T(8,128)(2,1)}, u32[]{:S(2)}) %copy-start.3) | copy-done | bytes 612
  8.6 0.4 prepare.1
  9.1 0.7 %stack.19.facts_ref = s32[6,16]{1,0:T(8,128)S(1)} concatenate(s32[1,16]{1,0:T(1,128)S(1)} %bitcast.7, s32[1,16]{1,0:T(1,128)} %bitcast.5, s32[1,16]{1,0:T(1,128)} %bitcast.6, s32[1,16]{1,0:T(1,128)} %bitcast.4, s32[1,16]{1,0:T(1,128)S(1)} %stack_broadcast_in_dim.6, s32[1,16]{1,0:T(1,128)S(1)} %stack_broadcast_in_dim.7), dimensions={0} | concatenate | bytes 768 | tf_op jit(solution)/shard_map/stack | solution.py:527
  9.8 0.0 collective-permute-done.2.refs_2_
  9.8 0.0 collective-permute-done.1.refs_1_
  9.8 0.0 collective-permute-done.refs_0_
  9.8 0.8 %select.1 = (bf16[8,72,128]{2,1,0:T(8,128)(2,1)S(1)}, bf16[8,72,128]{2,1,0:T(8,128)(2,1)S(1)}, bf16[8,72,128]{2,1,0:T(8,128)(2,1)S(1)}) custom-call(s32[6,16]{1,0:T(8,128)S(1)} %stack.19.facts_ref, s32[16]{0:T(128)S(1)} %collective-permute-done.refs_0_, s32[16]{0:T(128)S(1)} %collective-permute-done.1.refs_1_, s32[16]{0:T(128)S(1)} %collective-permute-done.2.refs_2_, ...), custom_call_target="tpu_custom_call" | custom-call | tf_op jit(solution)/shard_map/select/pallas_call | solution.py:118
  10.6 2.9 %collective-permute-start.3 = (bf16[8,72,128]{2,1,0:T(8,128)(2,1)S(1)}, bf16[8,72,128]{2,1,0:T(8,128)(2,1)S(1)}, u32[]{:S(2)}, u32[]{:S(2)}) collective-permute-start(bf16[8,72,128]{2,1,0:T(8,128)(2,1)S(1)} %get-tuple-element.26), channel_id=1, source_target_pairs={{0,12},{4,0},{8,4},{12,8},{1,13},{5,1},{9,5},{13,9},{2,14},{6,2},{... | collective-permute-start | bytes 442376 | tf_op jit(solution)/shard_map/ppermute | solution.py:503
  13.5 0.6 collective-permute-start.4
  14.0 0.0 collective-permute-start.5
  14.0 6.6 %moments.2 = (s32[4,18]{1,0:T(4,128)S(1)}, bf16[8,768,128]{2,1,0:T(8,128)(2,1)S(1)}, f32[48,128]{1,0:T(8,128)S(1)}) custom-call(s32[6,16]{1,0:T(8,128)S(1)} %stack.19.facts_ref, bf16[16,48,128]{2,1,0:T(8,128)(2,1)S(1)} %get-tuple-element.20.refs_0_.refs_1_, bf16[672,72]{1,0:T(8,128)(2,1)S(1)} %get-tuple-element.21.refs_1_.refs_2_, ...), custom_call_target="tpu_custom_call" | custom-call | flops 1048576 | bytes 1024 | tf_op jit(solution)/shard_map/moments/pallas_call | solution.py:323
  20.6 0.0 collective-permute-done.3.refs_5_
  20.6 5.4 %collective-permute-done.4.refs_6_ = bf16[8,72,128]{2,1,0:T(8,128)(2,1)S(1)} collective-permute-done((bf16[8,72,128]{2,1,0:T(8,128)(2,1)S(1)}, bf16[8,72,128]{2,1,0:T(8,128)(2,1)S(1)}, u32[]{:S(2)}, u32[]{:S(2)}) %collective-permute-start.4) | collective-permute-done | bytes 147488 | tf_op jit(solution)/shard_map/ppermute | solution.py:503
  26.0 0.0 collective-permute-done.5.refs_7_
  26.0 5.8 %moments.3 = (bf16[16,768,128]{2,1,0:T(8,128)(2,1)S(1)}, f32[1,48,128]{2,1,0:T(8,128)S(1)}, f32[1,48,128]{2,1,0:T(8,128)S(1)}, f32[1,48,128]{2,1,0:T(8,128)S(1)}, f32[1,48,128]{2,1,0:T(8,128)S(1)}) custom-call(s32[6,16]{1,0:T(8,128)S(1)} %stack.19.facts_ref, s32[4,18]{1,0:T(4,128)S(1)} %get-tuple-element.24.refs_0_.lists, ...), custom_call_target="tpu_custom_call" | custom-call | flops 1048576 | bytes 1024 | tf_op jit(solution)/shard_map/moments/pallas_call | solution.py:323
  31.8 3.5 %collective-permute-start.6 = (f32[1,48,128]{2,1,0:T(8,128)S(1)}, f32[1,48,128]{2,1,0:T(8,128)S(1)}, u32[]{:S(2)}, u32[]{:S(2)}) collective-permute-start(f32[1,48,128]{2,1,0:T(8,128)S(1)} %get-tuple-element.30), channel_id=1, source_target_pairs={{0,1},{1,2},{2,3},{3,0},{4,5},{5,6},{6,7},{7,4},{8,9},{9,10},{10,1... | collective-permute-start | bytes 73736 | tf_op jit(solution)/shard_map/ppermute | solution.py:503
  35.3 0.2 collective-permute-start.7
  35.5 0.2 collective-permute-start.8
  35.8 0.5 collective-permute-done.6
  36.2 1.7 %collective-permute-done.7 = f32[1,48,128]{2,1,0:T(8,128)S(1)} collective-permute-done((f32[1,48,128]{2,1,0:T(8,128)S(1)}, f32[1,48,128]{2,1,0:T(8,128)S(1)}, u32[]{:S(2)}, u32[]{:S(2)}) %collective-permute-start.7) | collective-permute-done | bytes 24608 | tf_op jit(solution)/shard_map/ppermute | solution.py:503
  38.0 0.8 %collective-permute-done.8 = f32[1,48,128]{2,1,0:T(8,128)S(1)} collective-permute-done((f32[1,48,128]{2,1,0:T(8,128)S(1)}, f32[1,48,128]{2,1,0:T(8,128)S(1)}, u32[]{:S(2)}, u32[]{:S(2)}) %collective-permute-start.8) | collective-permute-done | bytes 24608 | tf_op jit(solution)/shard_map/ppermute | solution.py:503
  38.8 4.0 %collective-permute-start.11 = (f32[1,48,128]{2,1,0:T(8,128)S(1)}, f32[1,48,128]{2,1,0:T(8,128)S(1)}, u32[]{:S(2)}, u32[]{:S(2)}) collective-permute-start(f32[1,48,128]{2,1,0:T(8,128)S(1)} %add_add_fusion.refs_0_), channel_id=1, source_target_pairs={{0,12},{4,0},{8,4},{12,8},{1,13},{5,1},{9,5},{13,9},{2,14},{6,2},{... | collective-permute-start | bytes 73736 | tf_op jit(solution)/shard_map/ppermute | solution.py:503
  42.8 1.6 %collective-permute-start.10 = (f32[1,48,128]{2,1,0:T(8,128)S(1)}, f32[1,48,128]{2,1,0:T(8,128)S(1)}, u32[]{:S(2)}, u32[]{:S(2)}) collective-permute-start(f32[1,48,128]{2,1,0:T(8,128)S(1)} %add_add_fusion.refs_0_), channel_id=1, source_target_pairs={{0,8},{4,12},{8,0},{12,4},{1,9},{5,13},{9,1},{13,5},{2,10},{6,14},... | collective-permute-start | bytes 73736 | tf_op jit(solution)/shard_map/ppermute | solution.py:503
  44.4 1.4 %collective-permute-start.9 = (f32[1,48,128]{2,1,0:T(8,128)S(1)}, f32[1,48,128]{2,1,0:T(8,128)S(1)}, u32[]{:S(2)}, u32[]{:S(2)}) collective-permute-start(f32[1,48,128]{2,1,0:T(8,128)S(1)} %add_add_fusion.refs_0_), channel_id=1, source_target_pairs={{0,4},{4,8},{8,12},{12,0},{1,5},{5,9},{9,13},{13,1},{2,6},{6,10},{... | collective-permute-start | bytes 73736 | tf_op jit(solution)/shard_map/ppermute | solution.py:503
  45.8 0.0 collective-permute-done.11.refs_3_
  45.8 1.3 %collective-permute-done.10.refs_2_ = f32[1,48,128]{2,1,0:T(8,128)S(1)} collective-permute-done((f32[1,48,128]{2,1,0:T(8,128)S(1)}, f32[1,48,128]{2,1,0:T(8,128)S(1)}, u32[]{:S(2)}, u32[]{:S(2)}) %collective-permute-start.10) | collective-permute-done | bytes 24608 | tf_op jit(solution)/shard_map/ppermute | solution.py:503
  47.0 2.3 %collective-permute-done.9.refs_1_ = f32[1,48,128]{2,1,0:T(8,128)S(1)} collective-permute-done((f32[1,48,128]{2,1,0:T(8,128)S(1)}, f32[1,48,128]{2,1,0:T(8,128)S(1)}, u32[]{:S(2)}, u32[]{:S(2)}) %collective-permute-start.9) | collective-permute-done | bytes 24608 | tf_op jit(solution)/shard_map/ppermute | solution.py:503
  49.4 0.0 copy-done.4
  49.4 4.6 %solve.1.refs_0_ = f32[1,8,128]{2,1,0:T(8,128)S(1)} custom-call(s32[14]{0:T(128)S(1)} %copy-done.4, f32[1,48,128]{2,1,0:T(8,128)S(1)} %add_add_fusion.refs_0_, f32[1,48,128]{2,1,0:T(8,128)S(1)} %collective-permute-done.9.refs_1_, f32[1,48,128]{2,1,0:T(8,128)S(1)} %collective-permute-done.10.refs_2_, f32[1,48,128]{2,1,0:T(8,128)S(1)} %collective-permute-done.11.refs_3_), custom_call_target="tpu_custom_call" | custom-call | tf_op jit(solution)/shard_map/solve/pallas_call | solution.py:419
  54.0 1.0 %collective-permute-start.14 = (f32[1,8,128]{2,1,0:T(8,128)S(1)}, f32[1,8,128]{2,1,0:T(8,128)S(1)}, u32[]{:S(2)}, u32[]{:S(2)}) collective-permute-start(f32[1,8,128]{2,1,0:T(8,128)S(1)} %solve.1.refs_0_), channel_id=1, source_target_pairs={{0,1},{1,2},{2,3},{3,0},{4,5},{5,6},{6,7},{7,4},{8,9},{9,10},{10,1... | collective-permute-start | bytes 12296 | tf_op jit(solution)/shard_map/ppermute | solution.py:503
  55.0 0.9 %collective-permute-start.13 = (f32[1,8,128]{2,1,0:T(8,128)S(1)}, f32[1,8,128]{2,1,0:T(8,128)S(1)}, u32[]{:S(2)}, u32[]{:S(2)}) collective-permute-start(f32[1,8,128]{2,1,0:T(8,128)S(1)} %solve.1.refs_0_), channel_id=1, source_target_pairs={{0,2},{1,3},{2,0},{3,1},{4,6},{5,7},{6,4},{7,5},{8,10},{9,11},{10,... | collective-permute-start | bytes 12296 | tf_op jit(solution)/shard_map/ppermute | solution.py:503
  55.8 0.0 collective-permute-start.12
  55.8 0.0 collective-permute-done.14.refs_3_
  55.8 1.6 %collective-permute-done.13.refs_2_ = f32[1,8,128]{2,1,0:T(8,128)S(1)} collective-permute-done((f32[1,8,128]{2,1,0:T(8,128)S(1)}, f32[1,8,128]{2,1,0:T(8,128)S(1)}, u32[]{:S(2)}, u32[]{:S(2)}) %collective-permute-start.13) | collective-permute-done | bytes 4128 | tf_op jit(solution)/shard_map/ppermute | solution.py:503
  57.4 1.4 %collective-permute-done.12.refs_1_ = f32[1,8,128]{2,1,0:T(8,128)S(1)} collective-permute-done((f32[1,8,128]{2,1,0:T(8,128)S(1)}, f32[1,8,128]{2,1,0:T(8,128)S(1)}, u32[]{:S(2)}, u32[]{:S(2)}) %collective-permute-start.12) | collective-permute-done | bytes 4128 | tf_op jit(solution)/shard_map/ppermute | solution.py:503
  58.9 3.3 %difference.1 = bf16[16,48,128]{2,1,0:T(8,128)(2,1)} custom-call(s32[6,16]{1,0:T(8,128)S(1)} %stack.19.facts_ref, s32[4,18]{1,0:T(4,128)S(1)} %get-tuple-element.24.refs_0_.lists, f32[1,8,128]{2,1,0:T(8,128)S(1)} %solve.1.refs_0_, f32[1,8,128]{2,1,0:T(8,128)S(1)} %collective-permute-done.12.refs_1_, f32[1,8,128]{2,1,0:T(8,128)S(1)} %collective-permute-done.13.refs_2_, ...), custom_call_target="tpu_custom_call" | custom-call | tf_op jit(solution)/shard_map/difference/pallas_call | solution.py:490
  (3 shorter events, 0.0 us)
Async XLA Ops:
  0.0 49.4 %copy-start.4 = (s32[14]{0:T(128)S(1)}, s32[14]{0:T(128)}, u32[]{:S(2)}) copy-start(s32[14]{0:T(128)} %order_ref.1) | copy-start | bytes 172
  0.7 9.1 %collective-permute-start.2 = (s32[16]{0:T(128)S(1)}, s32[16]{0:T(128)S(1)}, u32[]{:S(2)}, u32[]{:S(2)}) collective-permute-start(s32[16]{0:T(128)S(1)} %multiply_add_fusion), channel_id=1, source_target_pairs={{0,12},{4,0},{8,4},{12,8},{1,13},{5,1},{9,5},{13,9},{2,14},{6,2},{... | collective-permute-start | bytes 200 | tf_op jit(solution)/shard_map/ppermute | solution.py:503
  4.8 4.9 %collective-permute-start.1 = (s32[16]{0:T(128)S(1)}, s32[16]{0:T(128)S(1)}, u32[]{:S(2)}, u32[]{:S(2)}) collective-permute-start(s32[16]{0:T(128)S(1)} %multiply_add_fusion), channel_id=1, source_target_pairs={{0,8},{4,12},{8,0},{12,4},{1,9},{5,13},{9,1},{13,5},{2,10},{6,14},... | collective-permute-start | bytes 200 | tf_op jit(solution)/shard_map/ppermute | solution.py:503
  4.8 4.9 %collective-permute-start = (s32[16]{0:T(128)S(1)}, s32[16]{0:T(128)S(1)}, u32[]{:S(2)}, u32[]{:S(2)}) collective-permute-start(s32[16]{0:T(128)S(1)} %multiply_add_fusion), channel_id=1, source_target_pairs={{0,4},{4,8},{8,12},{12,0},{1,5},{5,9},{9,13},{13,1},{2,6},{6,10},{... | collective-permute-start | bytes 200 | tf_op jit(solution)/shard_map/ppermute | solution.py:503
  5.3 1.0 %copy-start = (bf16[16,80,128]{2,1,0:T(8,128)(2,1)S(1)}, bf16[16,80,128]{2,1,0:T(8,128)(2,1)}, u32[]{:S(2)}) copy-start(bf16[16,80,128]{2,1,0:T(8,128)(2,1)} %template.1) | copy-start | bytes 983044
  6.3 0.9 %copy-start.1 = (bf16[16,48,128]{2,1,0:T(8,128)(2,1)S(1)}, bf16[16,48,128]{2,1,0:T(8,128)(2,1)}, u32[]{:S(2)}) copy-start(bf16[16,48,128]{2,1,0:T(8,128)(2,1)} %science.1) | copy-start | bytes 589828
  7.2 0.7 %copy-start.2 = (bf16[14,21]{1,0:T(8,128)(2,1)S(1)}, bf16[14,21]{1,0:T(8,128)(2,1)}, u32[]{:S(2)}) copy-start(bf16[14,21]{1,0:T(8,128)(2,1)} %rows_ref.1) | copy-start | bytes 1768
  7.9 0.7 %copy-start.3 = (bf16[14,21]{1,0:T(8,128)(2,1)S(1)}, bf16[14,21]{1,0:T(8,128)(2,1)}, u32[]{:S(2)}) copy-start(bf16[14,21]{1,0:T(8,128)(2,1)} %cols_ref.1) | copy-start | bytes 1768
  10.6 10.0 %collective-permute-start.3 = (bf16[8,72,128]{2,1,0:T(8,128)(2,1)S(1)}, bf16[8,72,128]{2,1,0:T(8,128)(2,1)S(1)}, u32[]{:S(2)}, u32[]{:S(2)}) collective-permute-start(bf16[8,72,128]{2,1,0:T(8,128)(2,1)S(1)} %get-tuple-element.26), channel_id=1, source_target_pairs={{0,12},{4,0},{8,4},{12,8},{1,13},{5,1},{9,5},{13,9},{2,14},{6,2},{... | collective-permute-start | bytes 442376 | tf_op jit(solution)/shard_map/ppermute | solution.py:503
  13.5 12.5 %collective-permute-start.4 = (bf16[8,72,128]{2,1,0:T(8,128)(2,1)S(1)}, bf16[8,72,128]{2,1,0:T(8,128)(2,1)S(1)}, u32[]{:S(2)}, u32[]{:S(2)}) collective-permute-start(bf16[8,72,128]{2,1,0:T(8,128)(2,1)S(1)} %get-tuple-element.27), channel_id=1, source_target_pairs={{0,8},{4,12},{8,0},{12,4},{1,9},{5,13},{9,1},{13,5},{2,10},{6,14},... | collective-permute-start | bytes 442376 | tf_op jit(solution)/shard_map/ppermute | solution.py:503
  14.0 12.0 %collective-permute-start.5 = (bf16[8,72,128]{2,1,0:T(8,128)(2,1)S(1)}, bf16[8,72,128]{2,1,0:T(8,128)(2,1)S(1)}, u32[]{:S(2)}, u32[]{:S(2)}) collective-permute-start(bf16[8,72,128]{2,1,0:T(8,128)(2,1)S(1)} %get-tuple-element.28), channel_id=1, source_target_pairs={{0,4},{4,8},{8,12},{12,0},{1,5},{5,9},{9,13},{13,1},{2,6},{6,10},{... | collective-permute-start | bytes 442376 | tf_op jit(solution)/shard_map/ppermute | solution.py:503
  31.8 4.4 %collective-permute-start.6 = (f32[1,48,128]{2,1,0:T(8,128)S(1)}, f32[1,48,128]{2,1,0:T(8,128)S(1)}, u32[]{:S(2)}, u32[]{:S(2)}) collective-permute-start(f32[1,48,128]{2,1,0:T(8,128)S(1)} %get-tuple-element.30), channel_id=1, source_target_pairs={{0,1},{1,2},{2,3},{3,0},{4,5},{5,6},{6,7},{7,4},{8,9},{9,10},{10,1... | collective-permute-start | bytes 73736 | tf_op jit(solution)/shard_map/ppermute | solution.py:503
  35.3 2.7 %collective-permute-start.7 = (f32[1,48,128]{2,1,0:T(8,128)S(1)}, f32[1,48,128]{2,1,0:T(8,128)S(1)}, u32[]{:S(2)}, u32[]{:S(2)}) collective-permute-start(f32[1,48,128]{2,1,0:T(8,128)S(1)} %get-tuple-element.31), channel_id=1, source_target_pairs={{0,2},{1,3},{2,0},{3,1},{4,6},{5,7},{6,4},{7,5},{8,10},{9,11},{10,... | collective-permute-start | bytes 73736 | tf_op jit(solution)/shard_map/ppermute | solution.py:503
  35.5 3.3 %collective-permute-start.8 = (f32[1,48,128]{2,1,0:T(8,128)S(1)}, f32[1,48,128]{2,1,0:T(8,128)S(1)}, u32[]{:S(2)}, u32[]{:S(2)}) collective-permute-start(f32[1,48,128]{2,1,0:T(8,128)S(1)} %get-tuple-element.32), channel_id=1, source_target_pairs={{0,3},{1,0},{2,1},{3,2},{4,7},{5,4},{6,5},{7,6},{8,11},{9,8},{10,9... | collective-permute-start | bytes 73736 | tf_op jit(solution)/shard_map/ppermute | solution.py:503
  38.8 7.0 %collective-permute-start.11 = (f32[1,48,128]{2,1,0:T(8,128)S(1)}, f32[1,48,128]{2,1,0:T(8,128)S(1)}, u32[]{:S(2)}, u32[]{:S(2)}) collective-permute-start(f32[1,48,128]{2,1,0:T(8,128)S(1)} %add_add_fusion.refs_0_), channel_id=1, source_target_pairs={{0,12},{4,0},{8,4},{12,8},{1,13},{5,1},{9,5},{13,9},{2,14},{6,2},{... | collective-permute-start | bytes 73736 | tf_op jit(solution)/shard_map/ppermute | solution.py:503
  42.8 4.2 %collective-permute-start.10 = (f32[1,48,128]{2,1,0:T(8,128)S(1)}, f32[1,48,128]{2,1,0:T(8,128)S(1)}, u32[]{:S(2)}, u32[]{:S(2)}) collective-permute-start(f32[1,48,128]{2,1,0:T(8,128)S(1)} %add_add_fusion.refs_0_), channel_id=1, source_target_pairs={{0,8},{4,12},{8,0},{12,4},{1,9},{5,13},{9,1},{13,5},{2,10},{6,14},... | collective-permute-start | bytes 73736 | tf_op jit(solution)/shard_map/ppermute | solution.py:503
  44.4 5.0 %collective-permute-start.9 = (f32[1,48,128]{2,1,0:T(8,128)S(1)}, f32[1,48,128]{2,1,0:T(8,128)S(1)}, u32[]{:S(2)}, u32[]{:S(2)}) collective-permute-start(f32[1,48,128]{2,1,0:T(8,128)S(1)} %add_add_fusion.refs_0_), channel_id=1, source_target_pairs={{0,4},{4,8},{8,12},{12,0},{1,5},{5,9},{9,13},{13,1},{2,6},{6,10},{... | collective-permute-start | bytes 73736 | tf_op jit(solution)/shard_map/ppermute | solution.py:503
  54.0 1.9 %collective-permute-start.14 = (f32[1,8,128]{2,1,0:T(8,128)S(1)}, f32[1,8,128]{2,1,0:T(8,128)S(1)}, u32[]{:S(2)}, u32[]{:S(2)}) collective-permute-start(f32[1,8,128]{2,1,0:T(8,128)S(1)} %solve.1.refs_0_), channel_id=1, source_target_pairs={{0,1},{1,2},{2,3},{3,0},{4,5},{5,6},{6,7},{7,4},{8,9},{9,10},{10,1... | collective-permute-start | bytes 12296 | tf_op jit(solution)/shard_map/ppermute | solution.py:503
  55.0 2.5 %collective-permute-start.13 = (f32[1,8,128]{2,1,0:T(8,128)S(1)}, f32[1,8,128]{2,1,0:T(8,128)S(1)}, u32[]{:S(2)}, u32[]{:S(2)}) collective-permute-start(f32[1,8,128]{2,1,0:T(8,128)S(1)} %solve.1.refs_0_), channel_id=1, source_target_pairs={{0,2},{1,3},{2,0},{3,1},{4,6},{5,7},{6,4},{7,5},{8,10},{9,11},{10,... | collective-permute-start | bytes 12296 | tf_op jit(solution)/shard_map/ppermute | solution.py:503
  55.8 3.0 %collective-permute-start.12 = (f32[1,8,128]{2,1,0:T(8,128)S(1)}, f32[1,8,128]{2,1,0:T(8,128)S(1)}, u32[]{:S(2)}, u32[]{:S(2)}) collective-permute-start(f32[1,8,128]{2,1,0:T(8,128)S(1)} %solve.1.refs_0_), channel_id=1, source_target_pairs={{0,3},{1,0},{2,1},{3,2},{4,7},{5,4},{6,5},{7,6},{8,11},{9,8},{10,9... | collective-permute-start | bytes 12296 | tf_op jit(solution)/shard_map/ppermute | solution.py:503

commit v4 on v3

--- a/solution.py
+++ b/solution.py
@@ -13,6 +13,7 @@
 LEFT = 3
 BATCH = 4
 PAIR = 2
+FOUR = 4
 VMEM = pl.BlockSpec(memory_space=pltpu.VMEM)
 SMEM = pl.BlockSpec(memory_space=pltpu.SMEM)
 CODE, ROW, GOOD, PATCH, ME, CCD = range(6)
@@ -34,26 +35,21 @@
 
 
 def prepare_kernel(
-    rows_ref,
-    cols_ref,
+    taps_ref,
     template,
-    science,
     row_out,
     col_out,
     template_out,
-    science_out,
     taps_held,
 ):
-    kernels, taps = rows_ref.shape
-    rows, columns = science.shape[1:]
+    kernels, taps = taps_ref.shape[1:]
+    rows, columns = row_out.shape[0] // kernels, template.shape[2]
     reach = template_out.shape[1]
     middle = taps // 2
     lag = (template.shape[1] - rows) // 2 - middle
     template_out[...] = template[:, lag : lag + reach, :]
-    science_out[...] = science[...]
     taps_held[...] = jnp.zeros_like(taps_held)
-    taps_held[0, :kernels, :taps] = rows_ref[...].astype(F32)
-    taps_held[1, :kernels, :taps] = cols_ref[...].astype(F32)
+    taps_held[:, :kernels, :taps] = taps_ref[...]
     k = lax.broadcasted_iota(I32, (columns, columns), 0)
     lane = lax.broadcasted_iota(I32, (columns, columns), 1)
     moved_to = (k < taps) & ((k + lane == middle) | (k + lane == middle + columns))
@@ -72,9 +68,8 @@
         col_out[n] = jnp.where(band, moved, 0.0).astype(BF16)
 
 
-def prepare(basis_rows, basis_cols, template, science):
-    rows, columns = science.shape[1:]
-    tiles, tile_rows = template.shape[:2]
+def prepare(basis_rows, basis_cols, template, rows):
+    tiles, tile_rows, columns = template.shape
     kernels, taps = basis_rows.shape
     reach = min(-(-(rows + taps - 1) // 8) * 8, (tile_rows + rows) // 2 + taps // 2)
     held_rows = -(-kernels // 16) * 16
@@ -84,26 +79,24 @@
             jax.ShapeDtypeStruct((kernels * rows, reach), BF16),
             jax.ShapeDtypeStruct((kernels, columns, columns), BF16),
             jax.ShapeDtypeStruct((tiles, reach, columns), BF16),
-            jax.ShapeDtypeStruct(science.shape, BF16),
         ),
-        in_specs=[VMEM] * 4,
-        out_specs=[VMEM] * 4,
+        in_specs=[VMEM] * 2,
+        out_specs=[VMEM] * 3,
         scratch_shapes=[pltpu.VMEM((2, held_rows, columns), F32)],
         compiler_params=params(8),
         name="prepare",
-    )(basis_rows, basis_cols, template, science)
-
-
-def select_kernel(facts_ref, *refs, shifts, strips, tiles, capacity):
+    )(jnp.stack([basis_rows, basis_cols]).astype(F32), template)
+
+
+def select_kernel(*refs, shifts, strips, tiles, capacity):
     others, template, outs = refs[:shifts], refs[shifts], refs[shifts + 1 : -1]
     listing = refs[-1]
-    low = facts_ref[ME, 0] * tiles
     for other, out in zip(others, outs):
         for j in range(capacity):
             listing[j] = 0
         count = jnp.int32(0)
         for s in range(strips):
-            tile = other[s] - low
+            tile = other[s]
             hit = (tile >= 0) & (tile < tiles)
             listing[count] = jnp.where(hit, tile, 0)
             count = count + hit.astype(I32)
@@ -111,21 +104,21 @@
             out[j] = template[listing[j]]
 
 
-def select_tiles(facts, others, template, capacity):
+def select_tiles(others, template, capacity):
     shifts = len(others)
-    strips = facts.shape[1]
+    strips = others[0].shape[0]
     tiles, tile_rows, columns = template.shape
     return pl.pallas_call(
         functools.partial(
             select_kernel, shifts=shifts, strips=strips, tiles=tiles, capacity=capacity
         ),
         out_shape=[jax.ShapeDtypeStruct((capacity, tile_rows, columns), BF16)] * shifts,
-        in_specs=[SMEM] * (1 + shifts) + [VMEM],
+        in_specs=[SMEM] * shifts + [VMEM],
         out_specs=[VMEM] * shifts,
         scratch_shapes=[pltpu.SMEM((strips + capacity,), I32)],
         compiler_params=params(8),
         name="select",
-    )(facts, *others, template)
+    )(*others, template)
 
 
 def across_rows(columns):
@@ -171,7 +164,7 @@
 def moments_kernel(facts_ref, *refs, own, sizes):
     capacity, patches, ccds, share, tiles, kernels, planes = sizes
     if own:
-        science, row_table, col_table, plates, lists, planes_out, sums, p32, running = refs
+        science, row_table, col_table, plates, lists, science_out, planes_out, sums, p32, running = refs
     else:
         lists, science, row_table, col_table, before, *arrived = refs[: -4 - ccds]
         planes_out, outs = refs[-4 - ccds], refs[-3 - ccds : -3]
@@ -223,6 +216,7 @@
 
     if own:
         write_lists(facts_ref, lists, patches, strips)
+        science_out[...] = science[...]
     else:
         for d in range(1, patches):
             start = lists[START, d]
@@ -313,18 +307,19 @@
         held = min(held, -(-capacity // BATCH) * BATCH)
         arguments = [facts, science, *tables, *plates]
         outs = [jax.ShapeDtypeStruct((4, max(strips, patches) + 2), I32)]
+        passed = [jax.ShapeDtypeStruct(science.shape, BF16)]
         sums = [jax.ShapeDtypeStruct(one_sum, F32)]
     else:
         arguments = [facts, lists, science, *tables, before, *plates]
-        outs = []
+        outs, passed = [], []
         sums = [jax.ShapeDtypeStruct((share,) + one_sum, F32)] * ccds
         scratch.append(pltpu.VMEM((strips + capacity,) + plates[0].shape[1:], BF16))
     scalars = 1 if own else 2
     return pl.pallas_call(
         functools.partial(moments_kernel, own=own, sizes=sizes),
-        out_shape=outs + [jax.ShapeDtypeStruct((held, rows * planes, columns), BF16)] + sums,
+        out_shape=outs + passed + [jax.ShapeDtypeStruct((held, rows * planes, columns), BF16)] + sums,
         in_specs=[SMEM] * scalars + [VMEM] * (len(arguments) - scalars),
-        out_specs=[SMEM] * len(outs) + [VMEM] * (1 + len(sums)),
+        out_specs=[SMEM] * len(outs) + [VMEM] * (len(passed) + 1 + len(sums)),
         scratch_shapes=scratch,
         compiler_params=params(20),
         cost_estimate=pl.CostEstimate(flops=1 << 20, bytes_accessed=1 << 10, transcendentals=0),
@@ -385,7 +380,10 @@
             ]
             inner, here = columns[at], blocks[at]
             for i in wanted:
-                scale = 1.0 / jnp.broadcast_to(inner[i][i : i + 1], (8, 128))
+                pivot = jnp.broadcast_to(inner[i][i : i + 1], (8, 128))
+                scale = pl.reciprocal(pivot, approx=True)
+                scale = scale * (2.0 - pivot * scale)
+                scale = scale * (2.0 - pivot * scale)
                 line = jnp.broadcast_to(here[i : i + 1], (8, 128)) * scale
                 here = jnp.where(row8 == i, line, here - inner[i] * line)
                 for k in wanted:
@@ -457,8 +455,8 @@
         count = lists[row, lists.shape[1] - 1]
 
         def step(t, carry, row=row, stack=stack, count=count):
-            for i in range(PAIR):
-                j = jnp.minimum(t * PAIR + i, count - 1)
+            for i in range(FOUR):
+                j = jnp.minimum(t * FOUR + i, count - 1)
                 strip = lists[row, j]
                 d = 0 if row == OWN else lists[GROUP, j]
                 coef = [table[d, t] for t in range(len(TERMS))]
@@ -482,7 +480,7 @@
                     out[strip, h * tall : (h + 1) * tall, :] = value.astype(BF16)
             return carry
 
-        lax.fori_loop(0, (count + PAIR - 1) // PAIR, step, 0)
+        lax.fori_loop(0, (count + FOUR - 1) // FOUR, step, 0)
 
 
 def difference(facts, lists, coefs, stacks, shape, sizes):
@@ -523,17 +521,21 @@
     share = -(-patches // ccds)
     sizes = (capacity, patches, ccds, share, tiles, kernels, planes)
     code = strip_patch * tiles + strip_tile
-    others = [shifted(code, "patch", d) for d in range(1, patches)]
+    me = lax.axis_index("patch")
+    others = []
+    for d in range(1, patches):
+        owner = jnp.where(me + d >= patches, me + d - patches, me + d)
+        others.append(shifted(code - owner * tiles, "patch", d))
     facts = jnp.stack(
         [code, strip_row, row_count, strip_patch]
         + [jnp.full_like(code, lax.axis_index(axis)) for axis in ("patch", "ccd")]
     )
-    *tables, template, science = prepare(basis_rows, basis_cols, template, science)
-    chosen = select_tiles(facts, others, template, capacity)
+    *tables, template = prepare(basis_rows, basis_cols, template, science.shape[1])
+    chosen = select_tiles(others, template, capacity)
     plates = [shifted(tile, "patch", patches - d) for d, tile in enumerate(chosen, 1)]
     if patches > 8:
         plates = [jnp.concatenate(plates, axis=0)]
-    lists, own_planes, before = moments_call(facts, None, science, tables, None, [template], sizes)
+    lists, science, own_planes, before = moments_call(facts, None, science, tables, None, [template], sizes)
     planes_left, *scattered = moments_call(facts, lists, science, tables, before, plates, sizes)
     mine = scattered[0]
     for e in range(1, ccds):

time: 62.4 us -> 60 us (0.962); the launches traced: 62.2 us -> 59.1 us
  starting transfers between devices: 20.8 us -> 18.8 us
  local copies, waits for them, and re-layouts: 3.99 us -> 2.61 us
  other arithmetic: 0.7 us -> 1.41 us
    ppermute x15, starting transfers between devices: 20.8 us -> 18.8 us  [shifted(): lax.ppermute(value, axis, [(i, (i + shift) % size) for i in range(size)])]
    unnamed x10 -> x6, local copies, waits for them, and re-layouts: 3.27 us -> 1.9 us
    pallas_call x2, Pallas kernels: 12.4 us -> 13.4 us  [moments_call(): pl.pallas_call(functools.partial(moments_kernel, own=own, sizes=sizes), o...]
    convert_element_type x0 -> x1, other arithmetic: none -> 0.71 us  [prepare(): jnp.stack([basis_rows, basis_cols]).astype(F32)]
    sub x0 -> x2, other arithmetic: none -> 0.69 us  [body(): others.append(shifted(code - owner * tiles, 'patch', d))]
    add x1 -> x0, other arithmetic: 0.69 us -> none  [body(): code = strip_patch * tiles + strip_tile]
  transfers between devices with their start and end apart: 15 -> 15, of which waited for: 8 -> 9; matrix products, arithmetic and copies ran while one was open for 1% -> 2% of each run, Pallas kernels for 11% -> 11%
where the time goes in v4:
time: 60 us; the launch traced here: 59.1 us
  Pallas kernels  21.5 us (36%)
  starting transfers between devices  18.8 us (31%)
  waiting for transfers between devices  14.6 us (24%)
  local copies, waits for them, and re-layouts  2.61 us (4%)
  other arithmetic  1.41 us (2%)
    ppermute x15, starting transfers between devices, shifted(): lax.ppermute(value, axis, [(i, (i + shift) % size) for i in range(size)])  18.8 us
    ppermute x15, waiting for transfers between devices, shifted(): lax.ppermute(value, axis, [(i, (i + shift) % size) for i in range(size)])  14.6 us
    pallas_call x2, Pallas kernels, moments_call(): pl.pallas_call(functools.partial(moments_kernel, own=own, sizes=sizes), o...  13.4 us
    pallas_call x1, Pallas kernels, solve(): pl.pallas_call(functools.partial(solve_kernel, kernels=kernels, planes=pl...  4 us
    pallas_call x1, Pallas kernels, difference(): pl.pallas_call(functools.partial(difference_kernel, sizes=sizes, tall=tal...  2.96 us
    unnamed x6, local copies, waits for them, and re-layouts  1.9 us
  transfers between devices with their start and end apart: 15, of which 9 were waited for; matrix products, arithmetic and copies ran while one was open for 2% of the time, Pallas kernels for 11%

profile of v4, /device:TPU:1, one launch (start us, length us, event | category | flops | bytes accessed | tf_op | source)
XLA Modules:
  0.0 59.1 jit_solution(7908153257565555459)
XLA Ops:
  0.0 0.0 copy-start.2
  0.0 0.7 %broadcast_subtract_fusion = (s32[16]{0:T(128)S(1)}, s32[16]{0:T(128)S(1)}) fusion(s32[]{:T(128)S(6)} %mul.15, s32[16]{0:T(128)} %param.11, s32[16]{0:T(128)} %param.10), kind=kLoop, calls=%fused_computation.3 | loop fusion | flops 48 | bytes 260 | tf_op jit(solution)/shard_map/sub | solution.py:528
  0.7 3.1 %collective-permute-start.1 = (s32[16]{0:T(128)S(1)}, s32[16]{0:T(128)S(1)}, u32[]{:S(2)}, u32[]{:S(2)}) collective-permute-start(s32[16]{0:T(128)S(1)} %get-tuple-element.37), channel_id=1, source_target_pairs={{0,8},{4,12},{8,0},{12,4},{1,9},{5,13},{9,1},{13,5},{2,10},{6,14},... | collective-permute-start | bytes 200 | tf_op jit(solution)/shard_map/ppermute | solution.py:501
  3.8 1.3 %collective-permute-start = (s32[16]{0:T(128)S(1)}, s32[16]{0:T(128)S(1)}, u32[]{:S(2)}, u32[]{:S(2)}) collective-permute-start(s32[16]{0:T(128)S(1)} %get-tuple-element.38), channel_id=1, source_target_pairs={{0,4},{4,8},{8,12},{12,0},{1,5},{5,9},{9,13},{13,1},{2,6},{6,10},{... | collective-permute-start | bytes 200 | tf_op jit(solution)/shard_map/ppermute | solution.py:501
  5.1 2.0 %collective-permute-start.2 = (s32[16]{0:T(128)S(1)}, s32[16]{0:T(128)S(1)}, u32[]{:S(2)}, u32[]{:S(2)}) collective-permute-start(s32[16]{0:T(128)S(1)} %get-tuple-element.35), channel_id=1, source_target_pairs={{0,12},{4,0},{8,4},{12,8},{1,13},{5,1},{9,5},{13,9},{2,14},{6,2},{... | collective-permute-start | bytes 200 | tf_op jit(solution)/shard_map/ppermute | solution.py:501
  7.1 0.7 %maximum_convert_fusion.taps_ref = f32[2,14,21]{2,1,0:T(8,128)S(1)} fusion(bf16[1,14,21]{2,1,0:T(8,128)(2,1)} %bitcast.7, bf16[1,14,21]{2,1,0:T(8,128)(2,1)} %bitcast.8), kind=kLoop, calls=%fused_computation.1 | loop fusion | flops 1176 | bytes 3528 | tf_op jit(solution)/shard_map/convert_element_type | solution.py:88
  7.8 0.0 copy-start
  7.8 1.0 %copy-done = bf16[16,80,128]{2,1,0:T(8,128)(2,1)S(1)} copy-done((bf16[16,80,128]{2,1,0:T(8,128)(2,1)S(1)}, bf16[16,80,128]{2,1,0:T(8,128)(2,1)}, u32[]{:S(2)}) %copy-start) | copy-done | bytes 327704
  8.8 0.4 prepare.1
  9.2 0.0 collective-permute-done.1.refs_1_
  9.2 0.0 collective-permute-done.refs_0_
  9.3 0.0 collective-permute-done.2.refs_2_
  9.3 0.7 %select.1 = (bf16[8,72,128]{2,1,0:T(8,128)(2,1)S(1)}, bf16[8,72,128]{2,1,0:T(8,128)(2,1)S(1)}, bf16[8,72,128]{2,1,0:T(8,128)(2,1)S(1)}) custom-call(s32[16]{0:T(128)S(1)} %collective-permute-done.refs_0_, s32[16]{0:T(128)S(1)} %collective-permute-done.1.refs_1_, s32[16]{0:T(128)S(1)} %collective-permute-done.2.refs_2_, ...), custom_call_target="tpu_custom_call" | custom-call | tf_op jit(solution)/shard_map/select/pallas_call | solution.py:111
  10.0 2.1 %collective-permute-start.3 = (bf16[8,72,128]{2,1,0:T(8,128)(2,1)S(1)}, bf16[8,72,128]{2,1,0:T(8,128)(2,1)S(1)}, u32[]{:S(2)}, u32[]{:S(2)}) collective-permute-start(bf16[8,72,128]{2,1,0:T(8,128)(2,1)S(1)} %get-tuple-element.26), channel_id=1, source_target_pairs={{0,12},{4,0},{8,4},{12,8},{1,13},{5,1},{9,5},{13,9},{2,14},{6,2},{... | collective-permute-start | bytes 442376 | tf_op jit(solution)/shard_map/ppermute | solution.py:501
  12.1 0.0 collective-permute-start.4
  12.1 0.4 collective-permute-start.5
  12.4 0.7 %stack.28.facts_ref = s32[6,16]{1,0:T(8,128)S(1)} concatenate(s32[1,16]{1,0:T(1,128)S(1)} %bitcast.6, s32[1,16]{1,0:T(1,128)} %bitcast.10, s32[1,16]{1,0:T(1,128)} %bitcast.11, s32[1,16]{1,0:T(1,128)} %bitcast.9, s32[1,16]{1,0:T(1,128)S(1)} %stack_broadcast_in_dim.6, s32[1,16]{1,0:T(1,128)S(1)} %stack_broadcast_in_dim.7), dimensions={0} | concatenate | bytes 768 | tf_op jit(solution)/shard_map/stack | solution.py:529
  13.1 0.0 copy-start.1
  13.1 0.9 %copy-done.1 = bf16[16,48,128]{2,1,0:T(8,128)(2,1)S(1)} copy-done((bf16[16,48,128]{2,1,0:T(8,128)(2,1)S(1)}, bf16[16,48,128]{2,1,0:T(8,128)(2,1)}, u32[]{:S(2)}) %copy-start.1) | copy-done | bytes 196632
  14.1 5.8 %moments.2 = (s32[4,18]{1,0:T(4,128)S(1)}, bf16[16,48,128]{2,1,0:T(8,128)(2,1)S(1)}, bf16[8,768,128]{2,1,0:T(8,128)(2,1)S(1)}, f32[48,128]{1,0:T(8,128)S(1)}) custom-call(s32[6,16]{1,0:T(8,128)S(1)} %stack.28.facts_ref, bf16[16,48,128]{2,1,0:T(8,128)(2,1)S(1)} %copy-done.1, bf16[672,72]{1,0:T(8,128)(2,1)S(1)} %get-tuple-element.20.refs_1_.refs_2_, ...), custom_call_target="tpu_custom_call" | custom-call | flops 1048576 | bytes 1024 | tf_op jit(solution)/shard_map/moments/pallas_call | solution.py:318
  19.9 0.0 collective-permute-done.3.refs_5_
  19.9 4.2 %collective-permute-done.4.refs_6_ = bf16[8,72,128]{2,1,0:T(8,128)(2,1)S(1)} collective-permute-done((bf16[8,72,128]{2,1,0:T(8,128)(2,1)S(1)}, bf16[8,72,128]{2,1,0:T(8,128)(2,1)S(1)}, u32[]{:S(2)}, u32[]{:S(2)}) %collective-permute-start.4) | collective-permute-done | bytes 147488 | tf_op jit(solution)/shard_map/ppermute | solution.py:501
  24.1 0.0 collective-permute-done.5.refs_7_
  24.1 7.6 %moments.3 = (bf16[16,768,128]{2,1,0:T(8,128)(2,1)S(1)}, f32[1,48,128]{2,1,0:T(8,128)S(1)}, f32[1,48,128]{2,1,0:T(8,128)S(1)}, f32[1,48,128]{2,1,0:T(8,128)S(1)}, f32[1,48,128]{2,1,0:T(8,128)S(1)}) custom-call(s32[6,16]{1,0:T(8,128)S(1)} %stack.28.facts_ref, s32[4,18]{1,0:T(4,128)S(1)} %get-tuple-element.23.refs_0_.lists, ...), custom_call_target="tpu_custom_call" | custom-call | flops 1048576 | bytes 1024 | tf_op jit(solution)/shard_map/moments/pallas_call | solution.py:318
  31.7 5.0 %collective-permute-start.6 = (f32[1,48,128]{2,1,0:T(8,128)S(1)}, f32[1,48,128]{2,1,0:T(8,128)S(1)}, u32[]{:S(2)}, u32[]{:S(2)}) collective-permute-start(f32[1,48,128]{2,1,0:T(8,128)S(1)} %get-tuple-element.30), channel_id=1, source_target_pairs={{0,1},{1,2},{2,3},{3,0},{4,5},{5,6},{6,7},{7,4},{8,9},{9,10},{10,1... | collective-permute-start | bytes 73736 | tf_op jit(solution)/shard_map/ppermute | solution.py:501
  36.7 0.0 collective-permute-start.7
  36.7 0.5 collective-permute-start.8
  37.2 0.5 collective-permute-done.6
  37.6 1.7 %collective-permute-done.7 = f32[1,48,128]{2,1,0:T(8,128)S(1)} collective-permute-done((f32[1,48,128]{2,1,0:T(8,128)S(1)}, f32[1,48,128]{2,1,0:T(8,128)S(1)}, u32[]{:S(2)}, u32[]{:S(2)}) %collective-permute-start.7) | collective-permute-done | bytes 24608 | tf_op jit(solution)/shard_map/ppermute | solution.py:501
  39.4 0.6 %collective-permute-done.8 = f32[1,48,128]{2,1,0:T(8,128)S(1)} collective-permute-done((f32[1,48,128]{2,1,0:T(8,128)S(1)}, f32[1,48,128]{2,1,0:T(8,128)S(1)}, u32[]{:S(2)}, u32[]{:S(2)}) %collective-permute-start.8) | collective-permute-done | bytes 24608 | tf_op jit(solution)/shard_map/ppermute | solution.py:501
  40.0 2.3 %collective-permute-start.11 = (f32[1,48,128]{2,1,0:T(8,128)S(1)}, f32[1,48,128]{2,1,0:T(8,128)S(1)}, u32[]{:S(2)}, u32[]{:S(2)}) collective-permute-start(f32[1,48,128]{2,1,0:T(8,128)S(1)} %add_add_fusion.refs_0_), channel_id=1, source_target_pairs={{0,12},{4,0},{8,4},{12,8},{1,13},{5,1},{9,5},{13,9},{2,14},{6,2},{... | collective-permute-start | bytes 73736 | tf_op jit(solution)/shard_map/ppermute | solution.py:501
  42.3 0.0 collective-permute-start.10
  42.3 0.4 collective-permute-start.9
  42.6 0.7 %collective-permute-done.11.refs_3_ = f32[1,48,128]{2,1,0:T(8,128)S(1)} collective-permute-done((f32[1,48,128]{2,1,0:T(8,128)S(1)}, f32[1,48,128]{2,1,0:T(8,128)S(1)}, u32[]{:S(2)}, u32[]{:S(2)}) %collective-permute-start.11) | collective-permute-done | bytes 24608 | tf_op jit(solution)/shard_map/ppermute | solution.py:501
  43.3 3.1 %collective-permute-done.10.refs_2_ = f32[1,48,128]{2,1,0:T(8,128)S(1)} collective-permute-done((f32[1,48,128]{2,1,0:T(8,128)S(1)}, f32[1,48,128]{2,1,0:T(8,128)S(1)}, u32[]{:S(2)}, u32[]{:S(2)}) %collective-permute-start.10) | collective-permute-done | bytes 24608 | tf_op jit(solution)/shard_map/ppermute | solution.py:501
  46.4 0.8 %collective-permute-done.9.refs_1_ = f32[1,48,128]{2,1,0:T(8,128)S(1)} collective-permute-done((f32[1,48,128]{2,1,0:T(8,128)S(1)}, f32[1,48,128]{2,1,0:T(8,128)S(1)}, u32[]{:S(2)}, u32[]{:S(2)}) %collective-permute-start.9) | collective-permute-done | bytes 24608 | tf_op jit(solution)/shard_map/ppermute | solution.py:501
  47.2 0.0 copy-done.2
  47.2 4.0 %solve.1.refs_0_ = f32[1,8,128]{2,1,0:T(8,128)S(1)} custom-call(s32[14]{0:T(128)S(1)} %copy-done.2, f32[1,48,128]{2,1,0:T(8,128)S(1)} %add_add_fusion.refs_0_, f32[1,48,128]{2,1,0:T(8,128)S(1)} %collective-permute-done.9.refs_1_, f32[1,48,128]{2,1,0:T(8,128)S(1)} %collective-permute-done.10.refs_2_, f32[1,48,128]{2,1,0:T(8,128)S(1)} %collective-permute-done.11.refs_3_), custom_call_target="tpu_custom_call" | custom-call | tf_op jit(solution)/shard_map/solve/pallas_call | solution.py:417
  51.2 1.1 %collective-permute-start.14 = (f32[1,8,128]{2,1,0:T(8,128)S(1)}, f32[1,8,128]{2,1,0:T(8,128)S(1)}, u32[]{:S(2)}, u32[]{:S(2)}) collective-permute-start(f32[1,8,128]{2,1,0:T(8,128)S(1)} %solve.1.refs_0_), channel_id=1, source_target_pairs={{0,1},{1,2},{2,3},{3,0},{4,5},{5,6},{6,7},{7,4},{8,9},{9,10},{10,1... | collective-permute-start | bytes 12296 | tf_op jit(solution)/shard_map/ppermute | solution.py:501
  52.3 0.8 %collective-permute-start.13 = (f32[1,8,128]{2,1,0:T(8,128)S(1)}, f32[1,8,128]{2,1,0:T(8,128)S(1)}, u32[]{:S(2)}, u32[]{:S(2)}) collective-permute-start(f32[1,8,128]{2,1,0:T(8,128)S(1)} %solve.1.refs_0_), channel_id=1, source_target_pairs={{0,2},{1,3},{2,0},{3,1},{4,6},{5,7},{6,4},{7,5},{8,10},{9,11},{10,... | collective-permute-start | bytes 12296 | tf_op jit(solution)/shard_map/ppermute | solution.py:501
  53.1 0.0 collective-permute-start.12
  53.1 0.0 collective-permute-done.14.refs_3_
  53.1 1.9 %collective-permute-done.13.refs_2_ = f32[1,8,128]{2,1,0:T(8,128)S(1)} collective-permute-done((f32[1,8,128]{2,1,0:T(8,128)S(1)}, f32[1,8,128]{2,1,0:T(8,128)S(1)}, u32[]{:S(2)}, u32[]{:S(2)}) %collective-permute-start.13) | collective-permute-done | bytes 4128 | tf_op jit(solution)/shard_map/ppermute | solution.py:501
  55.1 1.1 %collective-permute-done.12.refs_1_ = f32[1,8,128]{2,1,0:T(8,128)S(1)} collective-permute-done((f32[1,8,128]{2,1,0:T(8,128)S(1)}, f32[1,8,128]{2,1,0:T(8,128)S(1)}, u32[]{:S(2)}, u32[]{:S(2)}) %collective-permute-start.12) | collective-permute-done | bytes 4128 | tf_op jit(solution)/shard_map/ppermute | solution.py:501
  56.1 3.0 %difference.1 = bf16[16,48,128]{2,1,0:T(8,128)(2,1)} custom-call(s32[6,16]{1,0:T(8,128)S(1)} %stack.28.facts_ref, s32[4,18]{1,0:T(4,128)S(1)} %get-tuple-element.23.refs_0_.lists, f32[1,8,128]{2,1,0:T(8,128)S(1)} %solve.1.refs_0_, f32[1,8,128]{2,1,0:T(8,128)S(1)} %collective-permute-done.12.refs_1_, f32[1,8,128]{2,1,0:T(8,128)S(1)} %collective-permute-done.13.refs_2_, ...), custom_call_target="tpu_custom_call" | custom-call | tf_op jit(solution)/shard_map/difference/pallas_call | solution.py:488
  (4 shorter events, 0.0 us)
Async XLA Ops:
  0.0 47.2 %copy-start.2 = (s32[14]{0:T(128)S(1)}, s32[14]{0:T(128)}, u32[]{:S(2)}) copy-start(s32[14]{0:T(128)} %order_ref.1) | copy-start | bytes 172
  0.7 8.5 %collective-permute-start.1 = (s32[16]{0:T(128)S(1)}, s32[16]{0:T(128)S(1)}, u32[]{:S(2)}, u32[]{:S(2)}) collective-permute-start(s32[16]{0:T(128)S(1)} %get-tuple-element.37), channel_id=1, source_target_pairs={{0,8},{4,12},{8,0},{12,4},{1,9},{5,13},{9,1},{13,5},{2,10},{6,14},... | collective-permute-start | bytes 200 | tf_op jit(solution)/shard_map/ppermute | solution.py:501
  3.8 5.4 %collective-permute-start = (s32[16]{0:T(128)S(1)}, s32[16]{0:T(128)S(1)}, u32[]{:S(2)}, u32[]{:S(2)}) collective-permute-start(s32[16]{0:T(128)S(1)} %get-tuple-element.38), channel_id=1, source_target_pairs={{0,4},{4,8},{8,12},{12,0},{1,5},{5,9},{9,13},{13,1},{2,6},{6,10},{... | collective-permute-start | bytes 200 | tf_op jit(solution)/shard_map/ppermute | solution.py:501
  5.1 4.1 %collective-permute-start.2 = (s32[16]{0:T(128)S(1)}, s32[16]{0:T(128)S(1)}, u32[]{:S(2)}, u32[]{:S(2)}) collective-permute-start(s32[16]{0:T(128)S(1)} %get-tuple-element.35), channel_id=1, source_target_pairs={{0,12},{4,0},{8,4},{12,8},{1,13},{5,1},{9,5},{13,9},{2,14},{6,2},{... | collective-permute-start | bytes 200 | tf_op jit(solution)/shard_map/ppermute | solution.py:501
  7.8 1.0 %copy-start = (bf16[16,80,128]{2,1,0:T(8,128)(2,1)S(1)}, bf16[16,80,128]{2,1,0:T(8,128)(2,1)}, u32[]{:S(2)}) copy-start(bf16[16,80,128]{2,1,0:T(8,128)(2,1)} %template.1) | copy-start | bytes 983044
  10.0 9.9 %collective-permute-start.3 = (bf16[8,72,128]{2,1,0:T(8,128)(2,1)S(1)}, bf16[8,72,128]{2,1,0:T(8,128)(2,1)S(1)}, u32[]{:S(2)}, u32[]{:S(2)}) collective-permute-start(bf16[8,72,128]{2,1,0:T(8,128)(2,1)S(1)} %get-tuple-element.26), channel_id=1, source_target_pairs={{0,12},{4,0},{8,4},{12,8},{1,13},{5,1},{9,5},{13,9},{2,14},{6,2},{... | collective-permute-start | bytes 442376 | tf_op jit(solution)/shard_map/ppermute | solution.py:501
  12.1 12.0 %collective-permute-start.4 = (bf16[8,72,128]{2,1,0:T(8,128)(2,1)S(1)}, bf16[8,72,128]{2,1,0:T(8,128)(2,1)S(1)}, u32[]{:S(2)}, u32[]{:S(2)}) collective-permute-start(bf16[8,72,128]{2,1,0:T(8,128)(2,1)S(1)} %get-tuple-element.27), channel_id=1, source_target_pairs={{0,8},{4,12},{8,0},{12,4},{1,9},{5,13},{9,1},{13,5},{2,10},{6,14},... | collective-permute-start | bytes 442376 | tf_op jit(solution)/shard_map/ppermute | solution.py:501
  12.1 12.0 %collective-permute-start.5 = (bf16[8,72,128]{2,1,0:T(8,128)(2,1)S(1)}, bf16[8,72,128]{2,1,0:T(8,128)(2,1)S(1)}, u32[]{:S(2)}, u32[]{:S(2)}) collective-permute-start(bf16[8,72,128]{2,1,0:T(8,128)(2,1)S(1)} %get-tuple-element.28), channel_id=1, source_target_pairs={{0,4},{4,8},{8,12},{12,0},{1,5},{5,9},{9,13},{13,1},{2,6},{6,10},{... | collective-permute-start | bytes 442376 | tf_op jit(solution)/shard_map/ppermute | solution.py:501
  13.1 0.9 %copy-start.1 = (bf16[16,48,128]{2,1,0:T(8,128)(2,1)S(1)}, bf16[16,48,128]{2,1,0:T(8,128)(2,1)}, u32[]{:S(2)}) copy-start(bf16[16,48,128]{2,1,0:T(8,128)(2,1)} %refs_0_.1) | copy-start | bytes 589828
  31.7 5.9 %collective-permute-start.6 = (f32[1,48,128]{2,1,0:T(8,128)S(1)}, f32[1,48,128]{2,1,0:T(8,128)S(1)}, u32[]{:S(2)}, u32[]{:S(2)}) collective-permute-start(f32[1,48,128]{2,1,0:T(8,128)S(1)} %get-tuple-element.30), channel_id=1, source_target_pairs={{0,1},{1,2},{2,3},{3,0},{4,5},{5,6},{6,7},{7,4},{8,9},{9,10},{10,1... | collective-permute-start | bytes 73736 | tf_op jit(solution)/shard_map/ppermute | solution.py:501
  36.7 2.7 %collective-permute-start.7 = (f32[1,48,128]{2,1,0:T(8,128)S(1)}, f32[1,48,128]{2,1,0:T(8,128)S(1)}, u32[]{:S(2)}, u32[]{:S(2)}) collective-permute-start(f32[1,48,128]{2,1,0:T(8,128)S(1)} %get-tuple-element.31), channel_id=1, source_target_pairs={{0,2},{1,3},{2,0},{3,1},{4,6},{5,7},{6,4},{7,5},{8,10},{9,11},{10,... | collective-permute-start | bytes 73736 | tf_op jit(solution)/shard_map/ppermute | solution.py:501
  36.7 3.3 %collective-permute-start.8 = (f32[1,48,128]{2,1,0:T(8,128)S(1)}, f32[1,48,128]{2,1,0:T(8,128)S(1)}, u32[]{:S(2)}, u32[]{:S(2)}) collective-permute-start(f32[1,48,128]{2,1,0:T(8,128)S(1)} %get-tuple-element.32), channel_id=1, source_target_pairs={{0,3},{1,0},{2,1},{3,2},{4,7},{5,4},{6,5},{7,6},{8,11},{9,8},{10,9... | collective-permute-start | bytes 73736 | tf_op jit(solution)/shard_map/ppermute | solution.py:501
  40.0 3.3 %collective-permute-start.11 = (f32[1,48,128]{2,1,0:T(8,128)S(1)}, f32[1,48,128]{2,1,0:T(8,128)S(1)}, u32[]{:S(2)}, u32[]{:S(2)}) collective-permute-start(f32[1,48,128]{2,1,0:T(8,128)S(1)} %add_add_fusion.refs_0_), channel_id=1, source_target_pairs={{0,12},{4,0},{8,4},{12,8},{1,13},{5,1},{9,5},{13,9},{2,14},{6,2},{... | collective-permute-start | bytes 73736 | tf_op jit(solution)/shard_map/ppermute | solution.py:501
  42.3 4.1 %collective-permute-start.10 = (f32[1,48,128]{2,1,0:T(8,128)S(1)}, f32[1,48,128]{2,1,0:T(8,128)S(1)}, u32[]{:S(2)}, u32[]{:S(2)}) collective-permute-start(f32[1,48,128]{2,1,0:T(8,128)S(1)} %add_add_fusion.refs_0_), channel_id=1, source_target_pairs={{0,8},{4,12},{8,0},{12,4},{1,9},{5,13},{9,1},{13,5},{2,10},{6,14},... | collective-permute-start | bytes 73736 | tf_op jit(solution)/shard_map/ppermute | solution.py:501
  42.3 4.9 %collective-permute-start.9 = (f32[1,48,128]{2,1,0:T(8,128)S(1)}, f32[1,48,128]{2,1,0:T(8,128)S(1)}, u32[]{:S(2)}, u32[]{:S(2)}) collective-permute-start(f32[1,48,128]{2,1,0:T(8,128)S(1)} %add_add_fusion.refs_0_), channel_id=1, source_target_pairs={{0,4},{4,8},{8,12},{12,0},{1,5},{5,9},{9,13},{13,1},{2,6},{6,10},{... | collective-permute-start | bytes 73736 | tf_op jit(solution)/shard_map/ppermute | solution.py:501
  51.2 1.9 %collective-permute-start.14 = (f32[1,8,128]{2,1,0:T(8,128)S(1)}, f32[1,8,128]{2,1,0:T(8,128)S(1)}, u32[]{:S(2)}, u32[]{:S(2)}) collective-permute-start(f32[1,8,128]{2,1,0:T(8,128)S(1)} %solve.1.refs_0_), channel_id=1, source_target_pairs={{0,1},{1,2},{2,3},{3,0},{4,5},{5,6},{6,7},{7,4},{8,9},{9,10},{10,1... | collective-permute-start | bytes 12296 | tf_op jit(solution)/shard_map/ppermute | solution.py:501
  52.3 2.8 %collective-permute-start.13 = (f32[1,8,128]{2,1,0:T(8,128)S(1)}, f32[1,8,128]{2,1,0:T(8,128)S(1)}, u32[]{:S(2)}, u32[]{:S(2)}) collective-permute-start(f32[1,8,128]{2,1,0:T(8,128)S(1)} %solve.1.refs_0_), channel_id=1, source_target_pairs={{0,2},{1,3},{2,0},{3,1},{4,6},{5,7},{6,4},{7,5},{8,10},{9,11},{10,... | collective-permute-start | bytes 12296 | tf_op jit(solution)/shard_map/ppermute | solution.py:501
  53.1 3.0 %collective-permute-start.12 = (f32[1,8,128]{2,1,0:T(8,128)S(1)}, f32[1,8,128]{2,1,0:T(8,128)S(1)}, u32[]{:S(2)}, u32[]{:S(2)}) collective-permute-start(f32[1,8,128]{2,1,0:T(8,128)S(1)} %solve.1.refs_0_), channel_id=1, source_target_pairs={{0,3},{1,0},{2,1},{3,2},{4,7},{5,4},{6,5},{7,6},{8,11},{9,8},{10,9... | collective-permute-start | bytes 12296 | tf_op jit(solution)/shard_map/ppermute | solution.py:501

commit v5 on v4

--- a/solution.py
+++ b/solution.py
@@ -427,7 +427,7 @@
 def difference_kernel(facts_ref, lists, *refs, sizes, tall):
     capacity, patches, ccds, share, tiles, kernels, planes = sizes
     coefs, stacks = refs[:ccds], refs[ccds : ccds + 2]
-    out, table = refs[ccds + 2 :]
+    out, table, split = refs[ccds + 2 :]
     strips, rows, columns = out.shape
     across = jnp.concatenate([across_rows(columns)] * (tall // 8), axis=0)
     across2 = across * across
@@ -450,6 +450,8 @@
                 line = jnp.concatenate([block[t : t + 1]] * (width // 128), axis=1)
                 value = jnp.where(diagonal, -jnp.broadcast_to(line, (tall, width)), 0.0)
                 table[d, t] = jnp.where(is_science, 1.0, value) if t == 0 else value
+                if t == 2:
+                    split[d, 0], split[d, 1] = pieces(value)
 
     for row, stack in zip((OWN, REST), stacks):
         count = lists[row, lists.shape[1] - 1]
@@ -460,7 +462,7 @@
                 strip = lists[row, j]
                 d = 0 if row == OWN else lists[GROUP, j]
                 coef = [table[d, t] for t in range(len(TERMS))]
-                twice = pieces(coef[2])
+                twice = split[d, 0], split[d, 1]
                 offset, good = facts_ref[ROW, strip], facts_ref[GOOD, strip]
                 for h in range(rows // tall):
                     v = (2 * (offset + h * tall + sub) + 1).astype(F32) / PATCH_ROWS - 1.0
@@ -490,7 +492,10 @@
         out_shape=jax.ShapeDtypeStruct(shape, BF16),
         in_specs=[SMEM] * 2 + [VMEM] * (len(coefs) + len(stacks)),
         out_specs=VMEM,
-        scratch_shapes=[pltpu.VMEM((patches, len(TERMS), tall, tall * planes), F32)],
+        scratch_shapes=[
+            pltpu.VMEM((patches, len(TERMS), tall, tall * planes), F32),
+            pltpu.VMEM((patches, 2, tall, tall * planes), BF16),
+        ],
         compiler_params=params(20),
         name="difference",
     )(facts, lists, *coefs, *stacks)

time: 60 us -> 60.2 us (level); the launches traced: 59.1 us -> 60.1 us
  Pallas kernels: 21.5 us -> 22.4 us
  waiting for transfers between devices: 14.6 us -> 15.4 us
    pallas_call x2, Pallas kernels: 13.4 us -> 14.2 us  [moments_call(): pl.pallas_call(functools.partial(moments_kernel, own=own, sizes=sizes), o...]
    ppermute x15, waiting for transfers between devices: 14.6 us -> 15.4 us  [shifted(): lax.ppermute(value, axis, [(i, (i + shift) % size) for i in range(size)])]
  transfers between devices with their start and end apart: 15 -> 15, of which waited for: 9 -> 8; matrix products, arithmetic and copies ran while one was open for 2% -> 2% of each run, Pallas kernels for 11% -> 7%
where the time goes in v5:
time: 60.2 us; the launch traced here: 60.1 us
  Pallas kernels  22.4 us (37%)
  starting transfers between devices  18.3 us (30%)
  waiting for transfers between devices  15.4 us (26%)
  local copies, waits for them, and re-layouts  2.61 us (4%)
  other arithmetic  1.41 us (2%)
    ppermute x15, starting transfers between devices, shifted(): lax.ppermute(value, axis, [(i, (i + shift) % size) for i in range(size)])  18.3 us
    ppermute x15, waiting for transfers between devices, shifted(): lax.ppermute(value, axis, [(i, (i + shift) % size) for i in range(size)])  15.4 us
    pallas_call x2, Pallas kernels, moments_call(): pl.pallas_call(functools.partial(moments_kernel, own=own, sizes=sizes), o...  14.2 us
    pallas_call x1, Pallas kernels, solve(): pl.pallas_call(functools.partial(solve_kernel, kernels=kernels, planes=pl...  4 us
    pallas_call x1, Pallas kernels, difference(): pl.pallas_call(functools.partial(difference_kernel, sizes=sizes, tall=tal...  3.03 us
    unnamed x6, local copies, waits for them, and re-layouts  1.9 us
  transfers between devices with their start and end apart: 15, of which 8 were waited for; matrix products, arithmetic and copies ran while one was open for 2% of the time, Pallas kernels for 7%

profile of v5, /device:TPU:1, one launch (start us, length us, event | category | flops | bytes accessed | tf_op | source)
XLA Modules:
  0.0 60.1 jit_solution(6649194620439026890)
XLA Ops:
  0.0 0.0 copy-start.2
  0.0 0.7 %broadcast_subtract_fusion = (s32[16]{0:T(128)S(1)}, s32[16]{0:T(128)S(1)}) fusion(s32[]{:T(128)S(6)} %mul.15, s32[16]{0:T(128)} %param.11, s32[16]{0:T(128)} %param.10), kind=kLoop, calls=%fused_computation.3 | loop fusion | flops 48 | bytes 260 | tf_op jit(solution)/shard_map/sub | solution.py:533
  0.7 3.1 %collective-permute-start.1 = (s32[16]{0:T(128)S(1)}, s32[16]{0:T(128)S(1)}, u32[]{:S(2)}, u32[]{:S(2)}) collective-permute-start(s32[16]{0:T(128)S(1)} %get-tuple-element.37), channel_id=1, source_target_pairs={{0,8},{4,12},{8,0},{12,4},{1,9},{5,13},{9,1},{13,5},{2,10},{6,14},... | collective-permute-start | bytes 200 | tf_op jit(solution)/shard_map/ppermute | solution.py:506
  3.8 1.3 %collective-permute-start = (s32[16]{0:T(128)S(1)}, s32[16]{0:T(128)S(1)}, u32[]{:S(2)}, u32[]{:S(2)}) collective-permute-start(s32[16]{0:T(128)S(1)} %get-tuple-element.38), channel_id=1, source_target_pairs={{0,4},{4,8},{8,12},{12,0},{1,5},{5,9},{9,13},{13,1},{2,6},{6,10},{... | collective-permute-start | bytes 200 | tf_op jit(solution)/shard_map/ppermute | solution.py:506
  5.1 2.0 %collective-permute-start.2 = (s32[16]{0:T(128)S(1)}, s32[16]{0:T(128)S(1)}, u32[]{:S(2)}, u32[]{:S(2)}) collective-permute-start(s32[16]{0:T(128)S(1)} %get-tuple-element.35), channel_id=1, source_target_pairs={{0,12},{4,0},{8,4},{12,8},{1,13},{5,1},{9,5},{13,9},{2,14},{6,2},{... | collective-permute-start | bytes 200 | tf_op jit(solution)/shard_map/ppermute | solution.py:506
  7.1 0.7 %maximum_convert_fusion.taps_ref = f32[2,14,21]{2,1,0:T(8,128)S(1)} fusion(bf16[1,14,21]{2,1,0:T(8,128)(2,1)} %bitcast.7, bf16[1,14,21]{2,1,0:T(8,128)(2,1)} %bitcast.8), kind=kLoop, calls=%fused_computation.1 | loop fusion | flops 1176 | bytes 3528 | tf_op jit(solution)/shard_map/convert_element_type | solution.py:88
  7.8 0.0 copy-start
  7.8 1.0 %copy-done = bf16[16,80,128]{2,1,0:T(8,128)(2,1)S(1)} copy-done((bf16[16,80,128]{2,1,0:T(8,128)(2,1)S(1)}, bf16[16,80,128]{2,1,0:T(8,128)(2,1)}, u32[]{:S(2)}) %copy-start) | copy-done | bytes 327704
  8.8 0.4 prepare.1
  9.2 0.0 collective-permute-done.1.refs_1_
  9.2 0.0 collective-permute-done.refs_0_
  9.3 0.0 collective-permute-done.2.refs_2_
  9.3 0.7 %select.1 = (bf16[8,72,128]{2,1,0:T(8,128)(2,1)S(1)}, bf16[8,72,128]{2,1,0:T(8,128)(2,1)S(1)}, bf16[8,72,128]{2,1,0:T(8,128)(2,1)S(1)}) custom-call(s32[16]{0:T(128)S(1)} %collective-permute-done.refs_0_, s32[16]{0:T(128)S(1)} %collective-permute-done.1.refs_1_, s32[16]{0:T(128)S(1)} %collective-permute-done.2.refs_2_, ...), custom_call_target="tpu_custom_call" | custom-call | tf_op jit(solution)/shard_map/select/pallas_call | solution.py:111
  10.0 2.1 %collective-permute-start.3 = (bf16[8,72,128]{2,1,0:T(8,128)(2,1)S(1)}, bf16[8,72,128]{2,1,0:T(8,128)(2,1)S(1)}, u32[]{:S(2)}, u32[]{:S(2)}) collective-permute-start(bf16[8,72,128]{2,1,0:T(8,128)(2,1)S(1)} %get-tuple-element.26), channel_id=1, source_target_pairs={{0,12},{4,0},{8,4},{12,8},{1,13},{5,1},{9,5},{13,9},{2,14},{6,2},{... | collective-permute-start | bytes 442376 | tf_op jit(solution)/shard_map/ppermute | solution.py:506
  12.1 0.0 collective-permute-start.4
  12.1 0.4 collective-permute-start.5
  12.4 0.7 %stack.28.facts_ref = s32[6,16]{1,0:T(8,128)S(1)} concatenate(s32[1,16]{1,0:T(1,128)S(1)} %bitcast.6, s32[1,16]{1,0:T(1,128)} %bitcast.10, s32[1,16]{1,0:T(1,128)} %bitcast.11, s32[1,16]{1,0:T(1,128)} %bitcast.9, s32[1,16]{1,0:T(1,128)S(1)} %stack_broadcast_in_dim.6, s32[1,16]{1,0:T(1,128)S(1)} %stack_broadcast_in_dim.7), dimensions={0} | concatenate | bytes 768 | tf_op jit(solution)/shard_map/stack | solution.py:534
  13.1 0.0 copy-start.1
  13.1 0.9 %copy-done.1 = bf16[16,48,128]{2,1,0:T(8,128)(2,1)S(1)} copy-done((bf16[16,48,128]{2,1,0:T(8,128)(2,1)S(1)}, bf16[16,48,128]{2,1,0:T(8,128)(2,1)}, u32[]{:S(2)}) %copy-start.1) | copy-done | bytes 196632
  14.1 4.0 %moments.2 = (s32[4,18]{1,0:T(4,128)S(1)}, bf16[16,48,128]{2,1,0:T(8,128)(2,1)S(1)}, bf16[8,768,128]{2,1,0:T(8,128)(2,1)S(1)}, f32[48,128]{1,0:T(8,128)S(1)}) custom-call(s32[6,16]{1,0:T(8,128)S(1)} %stack.28.facts_ref, bf16[16,48,128]{2,1,0:T(8,128)(2,1)S(1)} %copy-done.1, bf16[672,72]{1,0:T(8,128)(2,1)S(1)} %get-tuple-element.20.refs_1_.refs_2_, ...), custom_call_target="tpu_custom_call" | custom-call | flops 1048576 | bytes 1024 | tf_op jit(solution)/shard_map/moments/pallas_call | solution.py:318
  18.1 0.0 collective-permute-done.3.refs_5_
  18.1 6.0 %collective-permute-done.4.refs_6_ = bf16[8,72,128]{2,1,0:T(8,128)(2,1)S(1)} collective-permute-done((bf16[8,72,128]{2,1,0:T(8,128)(2,1)S(1)}, bf16[8,72,128]{2,1,0:T(8,128)(2,1)S(1)}, u32[]{:S(2)}, u32[]{:S(2)}) %collective-permute-start.4) | collective-permute-done | bytes 147488 | tf_op jit(solution)/shard_map/ppermute | solution.py:506
  24.1 0.0 collective-permute-done.5.refs_7_
  24.1 10.1 %moments.3 = (bf16[16,768,128]{2,1,0:T(8,128)(2,1)S(1)}, f32[1,48,128]{2,1,0:T(8,128)S(1)}, f32[1,48,128]{2,1,0:T(8,128)S(1)}, f32[1,48,128]{2,1,0:T(8,128)S(1)}, f32[1,48,128]{2,1,0:T(8,128)S(1)}) custom-call(s32[6,16]{1,0:T(8,128)S(1)} %stack.28.facts_ref, s32[4,18]{1,0:T(4,128)S(1)} %get-tuple-element.23.refs_0_.lists, ...), custom_call_target="tpu_custom_call" | custom-call | flops 1048576 | bytes 1024 | tf_op jit(solution)/shard_map/moments/pallas_call | solution.py:318
  34.3 2.4 %collective-permute-start.6 = (f32[1,48,128]{2,1,0:T(8,128)S(1)}, f32[1,48,128]{2,1,0:T(8,128)S(1)}, u32[]{:S(2)}, u32[]{:S(2)}) collective-permute-start(f32[1,48,128]{2,1,0:T(8,128)S(1)} %get-tuple-element.30), channel_id=1, source_target_pairs={{0,1},{1,2},{2,3},{3,0},{4,5},{5,6},{6,7},{7,4},{8,9},{9,10},{10,1... | collective-permute-start | bytes 73736 | tf_op jit(solution)/shard_map/ppermute | solution.py:506
  36.7 1.0 %collective-permute-start.7 = (f32[1,48,128]{2,1,0:T(8,128)S(1)}, f32[1,48,128]{2,1,0:T(8,128)S(1)}, u32[]{:S(2)}, u32[]{:S(2)}) collective-permute-start(f32[1,48,128]{2,1,0:T(8,128)S(1)} %get-tuple-element.31), channel_id=1, source_target_pairs={{0,2},{1,3},{2,0},{3,1},{4,6},{5,7},{6,4},{7,5},{8,10},{9,11},{10,... | collective-permute-start | bytes 73736 | tf_op jit(solution)/shard_map/ppermute | solution.py:506
  37.7 0.0 collective-permute-start.8
  37.7 0.0 collective-permute-done.6
  37.7 2.0 %collective-permute-done.7 = f32[1,48,128]{2,1,0:T(8,128)S(1)} collective-permute-done((f32[1,48,128]{2,1,0:T(8,128)S(1)}, f32[1,48,128]{2,1,0:T(8,128)S(1)}, u32[]{:S(2)}, u32[]{:S(2)}) %collective-permute-start.7) | collective-permute-done | bytes 24608 | tf_op jit(solution)/shard_map/ppermute | solution.py:506
  39.7 1.3 %collective-permute-done.8 = f32[1,48,128]{2,1,0:T(8,128)S(1)} collective-permute-done((f32[1,48,128]{2,1,0:T(8,128)S(1)}, f32[1,48,128]{2,1,0:T(8,128)S(1)}, u32[]{:S(2)}, u32[]{:S(2)}) %collective-permute-start.8) | collective-permute-done | bytes 24608 | tf_op jit(solution)/shard_map/ppermute | solution.py:506
  41.0 0.5 collective-permute-start.11
  41.5 1.4 %collective-permute-start.10 = (f32[1,48,128]{2,1,0:T(8,128)S(1)}, f32[1,48,128]{2,1,0:T(8,128)S(1)}, u32[]{:S(2)}, u32[]{:S(2)}) collective-permute-start(f32[1,48,128]{2,1,0:T(8,128)S(1)} %add_add_fusion.refs_0_), channel_id=1, source_target_pairs={{0,8},{4,12},{8,0},{12,4},{1,9},{5,13},{9,1},{13,5},{2,10},{6,14},... | collective-permute-start | bytes 73736 | tf_op jit(solution)/shard_map/ppermute | solution.py:506
  42.8 1.4 %collective-permute-start.9 = (f32[1,48,128]{2,1,0:T(8,128)S(1)}, f32[1,48,128]{2,1,0:T(8,128)S(1)}, u32[]{:S(2)}, u32[]{:S(2)}) collective-permute-start(f32[1,48,128]{2,1,0:T(8,128)S(1)} %add_add_fusion.refs_0_), channel_id=1, source_target_pairs={{0,4},{4,8},{8,12},{12,0},{1,5},{5,9},{9,13},{13,1},{2,6},{6,10},{... | collective-permute-start | bytes 73736 | tf_op jit(solution)/shard_map/ppermute | solution.py:506
  44.2 0.0 collective-permute-done.11.refs_3_
  44.2 0.8 %collective-permute-done.10.refs_2_ = f32[1,48,128]{2,1,0:T(8,128)S(1)} collective-permute-done((f32[1,48,128]{2,1,0:T(8,128)S(1)}, f32[1,48,128]{2,1,0:T(8,128)S(1)}, u32[]{:S(2)}, u32[]{:S(2)}) %collective-permute-start.10) | collective-permute-done | bytes 24608 | tf_op jit(solution)/shard_map/ppermute | solution.py:506
  45.1 2.3 %collective-permute-done.9.refs_1_ = f32[1,48,128]{2,1,0:T(8,128)S(1)} collective-permute-done((f32[1,48,128]{2,1,0:T(8,128)S(1)}, f32[1,48,128]{2,1,0:T(8,128)S(1)}, u32[]{:S(2)}, u32[]{:S(2)}) %collective-permute-start.9) | collective-permute-done | bytes 24608 | tf_op jit(solution)/shard_map/ppermute | solution.py:506
  47.3 0.0 copy-done.2
  47.3 4.0 %solve.1.refs_0_ = f32[1,8,128]{2,1,0:T(8,128)S(1)} custom-call(s32[14]{0:T(128)S(1)} %copy-done.2, f32[1,48,128]{2,1,0:T(8,128)S(1)} %add_add_fusion.refs_0_, f32[1,48,128]{2,1,0:T(8,128)S(1)} %collective-permute-done.9.refs_1_, f32[1,48,128]{2,1,0:T(8,128)S(1)} %collective-permute-done.10.refs_2_, f32[1,48,128]{2,1,0:T(8,128)S(1)} %collective-permute-done.11.refs_3_), custom_call_target="tpu_custom_call" | custom-call | tf_op jit(solution)/shard_map/solve/pallas_call | solution.py:417
  51.3 2.1 %collective-permute-start.14 = (f32[1,8,128]{2,1,0:T(8,128)S(1)}, f32[1,8,128]{2,1,0:T(8,128)S(1)}, u32[]{:S(2)}, u32[]{:S(2)}) collective-permute-start(f32[1,8,128]{2,1,0:T(8,128)S(1)} %solve.1.refs_0_), channel_id=1, source_target_pairs={{0,1},{1,2},{2,3},{3,0},{4,5},{5,6},{6,7},{7,4},{8,9},{9,10},{10,1... | collective-permute-start | bytes 12296 | tf_op jit(solution)/shard_map/ppermute | solution.py:506
  53.5 0.6 collective-permute-start.13
  54.1 0.0 collective-permute-start.12
  54.1 0.2 collective-permute-done.14.refs_3_
  54.2 1.8 %collective-permute-done.13.refs_2_ = f32[1,8,128]{2,1,0:T(8,128)S(1)} collective-permute-done((f32[1,8,128]{2,1,0:T(8,128)S(1)}, f32[1,8,128]{2,1,0:T(8,128)S(1)}, u32[]{:S(2)}, u32[]{:S(2)}) %collective-permute-start.13) | collective-permute-done | bytes 4128 | tf_op jit(solution)/shard_map/ppermute | solution.py:506
  56.0 1.1 %collective-permute-done.12.refs_1_ = f32[1,8,128]{2,1,0:T(8,128)S(1)} collective-permute-done((f32[1,8,128]{2,1,0:T(8,128)S(1)}, f32[1,8,128]{2,1,0:T(8,128)S(1)}, u32[]{:S(2)}, u32[]{:S(2)}) %collective-permute-start.12) | collective-permute-done | bytes 4128 | tf_op jit(solution)/shard_map/ppermute | solution.py:506
  57.1 3.0 %difference.1 = bf16[16,48,128]{2,1,0:T(8,128)(2,1)} custom-call(s32[6,16]{1,0:T(8,128)S(1)} %stack.28.facts_ref, s32[4,18]{1,0:T(4,128)S(1)} %get-tuple-element.23.refs_0_.lists, f32[1,8,128]{2,1,0:T(8,128)S(1)} %solve.1.refs_0_, f32[1,8,128]{2,1,0:T(8,128)S(1)} %collective-permute-done.12.refs_1_, f32[1,8,128]{2,1,0:T(8,128)S(1)} %collective-permute-done.13.refs_2_, ...), custom_call_target="tpu_custom_call" | custom-call | tf_op jit(solution)/shard_map/difference/pallas_call | solution.py:490
  (4 shorter events, 0.0 us)
Async XLA Ops:
  0.0 47.3 %copy-start.2 = (s32[14]{0:T(128)S(1)}, s32[14]{0:T(128)}, u32[]{:S(2)}) copy-start(s32[14]{0:T(128)} %order_ref.1) | copy-start | bytes 172
  0.7 8.5 %collective-permute-start.1 = (s32[16]{0:T(128)S(1)}, s32[16]{0:T(128)S(1)}, u32[]{:S(2)}, u32[]{:S(2)}) collective-permute-start(s32[16]{0:T(128)S(1)} %get-tuple-element.37), channel_id=1, source_target_pairs={{0,8},{4,12},{8,0},{12,4},{1,9},{5,13},{9,1},{13,5},{2,10},{6,14},... | collective-permute-start | bytes 200 | tf_op jit(solution)/shard_map/ppermute | solution.py:506
  3.8 5.4 %collective-permute-start = (s32[16]{0:T(128)S(1)}, s32[16]{0:T(128)S(1)}, u32[]{:S(2)}, u32[]{:S(2)}) collective-permute-start(s32[16]{0:T(128)S(1)} %get-tuple-element.38), channel_id=1, source_target_pairs={{0,4},{4,8},{8,12},{12,0},{1,5},{5,9},{9,13},{13,1},{2,6},{6,10},{... | collective-permute-start | bytes 200 | tf_op jit(solution)/shard_map/ppermute | solution.py:506
  5.1 4.1 %collective-permute-start.2 = (s32[16]{0:T(128)S(1)}, s32[16]{0:T(128)S(1)}, u32[]{:S(2)}, u32[]{:S(2)}) collective-permute-start(s32[16]{0:T(128)S(1)} %get-tuple-element.35), channel_id=1, source_target_pairs={{0,12},{4,0},{8,4},{12,8},{1,13},{5,1},{9,5},{13,9},{2,14},{6,2},{... | collective-permute-start | bytes 200 | tf_op jit(solution)/shard_map/ppermute | solution.py:506
  7.8 1.0 %copy-start = (bf16[16,80,128]{2,1,0:T(8,128)(2,1)S(1)}, bf16[16,80,128]{2,1,0:T(8,128)(2,1)}, u32[]{:S(2)}) copy-start(bf16[16,80,128]{2,1,0:T(8,128)(2,1)} %template.1) | copy-start | bytes 983044
  10.0 8.1 %collective-permute-start.3 = (bf16[8,72,128]{2,1,0:T(8,128)(2,1)S(1)}, bf16[8,72,128]{2,1,0:T(8,128)(2,1)S(1)}, u32[]{:S(2)}, u32[]{:S(2)}) collective-permute-start(bf16[8,72,128]{2,1,0:T(8,128)(2,1)S(1)} %get-tuple-element.26), channel_id=1, source_target_pairs={{0,12},{4,0},{8,4},{12,8},{1,13},{5,1},{9,5},{13,9},{2,14},{6,2},{... | collective-permute-start | bytes 442376 | tf_op jit(solution)/shard_map/ppermute | solution.py:506
  12.1 12.0 %collective-permute-start.4 = (bf16[8,72,128]{2,1,0:T(8,128)(2,1)S(1)}, bf16[8,72,128]{2,1,0:T(8,128)(2,1)S(1)}, u32[]{:S(2)}, u32[]{:S(2)}) collective-permute-start(bf16[8,72,128]{2,1,0:T(8,128)(2,1)S(1)} %get-tuple-element.27), channel_id=1, source_target_pairs={{0,8},{4,12},{8,0},{12,4},{1,9},{5,13},{9,1},{13,5},{2,10},{6,14},... | collective-permute-start | bytes 442376 | tf_op jit(solution)/shard_map/ppermute | solution.py:506
  12.1 12.0 %collective-permute-start.5 = (bf16[8,72,128]{2,1,0:T(8,128)(2,1)S(1)}, bf16[8,72,128]{2,1,0:T(8,128)(2,1)S(1)}, u32[]{:S(2)}, u32[]{:S(2)}) collective-permute-start(bf16[8,72,128]{2,1,0:T(8,128)(2,1)S(1)} %get-tuple-element.28), channel_id=1, source_target_pairs={{0,4},{4,8},{8,12},{12,0},{1,5},{5,9},{9,13},{13,1},{2,6},{6,10},{... | collective-permute-start | bytes 442376 | tf_op jit(solution)/shard_map/ppermute | solution.py:506
  13.1 0.9 %copy-start.1 = (bf16[16,48,128]{2,1,0:T(8,128)(2,1)S(1)}, bf16[16,48,128]{2,1,0:T(8,128)(2,1)}, u32[]{:S(2)}) copy-start(bf16[16,48,128]{2,1,0:T(8,128)(2,1)} %refs_0_.1) | copy-start | bytes 589828
  34.3 3.4 %collective-permute-start.6 = (f32[1,48,128]{2,1,0:T(8,128)S(1)}, f32[1,48,128]{2,1,0:T(8,128)S(1)}, u32[]{:S(2)}, u32[]{:S(2)}) collective-permute-start(f32[1,48,128]{2,1,0:T(8,128)S(1)} %get-tuple-element.30), channel_id=1, source_target_pairs={{0,1},{1,2},{2,3},{3,0},{4,5},{5,6},{6,7},{7,4},{8,9},{9,10},{10,1... | collective-permute-start | bytes 73736 | tf_op jit(solution)/shard_map/ppermute | solution.py:506
  36.7 3.0 %collective-permute-start.7 = (f32[1,48,128]{2,1,0:T(8,128)S(1)}, f32[1,48,128]{2,1,0:T(8,128)S(1)}, u32[]{:S(2)}, u32[]{:S(2)}) collective-permute-start(f32[1,48,128]{2,1,0:T(8,128)S(1)} %get-tuple-element.31), channel_id=1, source_target_pairs={{0,2},{1,3},{2,0},{3,1},{4,6},{5,7},{6,4},{7,5},{8,10},{9,11},{10,... | collective-permute-start | bytes 73736 | tf_op jit(solution)/shard_map/ppermute | solution.py:506
  37.7 3.3 %collective-permute-start.8 = (f32[1,48,128]{2,1,0:T(8,128)S(1)}, f32[1,48,128]{2,1,0:T(8,128)S(1)}, u32[]{:S(2)}, u32[]{:S(2)}) collective-permute-start(f32[1,48,128]{2,1,0:T(8,128)S(1)} %get-tuple-element.32), channel_id=1, source_target_pairs={{0,3},{1,0},{2,1},{3,2},{4,7},{5,4},{6,5},{7,6},{8,11},{9,8},{10,9... | collective-permute-start | bytes 73736 | tf_op jit(solution)/shard_map/ppermute | solution.py:506
  41.0 3.3 %collective-permute-start.11 = (f32[1,48,128]{2,1,0:T(8,128)S(1)}, f32[1,48,128]{2,1,0:T(8,128)S(1)}, u32[]{:S(2)}, u32[]{:S(2)}) collective-permute-start(f32[1,48,128]{2,1,0:T(8,128)S(1)} %add_add_fusion.refs_0_), channel_id=1, source_target_pairs={{0,12},{4,0},{8,4},{12,8},{1,13},{5,1},{9,5},{13,9},{2,14},{6,2},{... | collective-permute-start | bytes 73736 | tf_op jit(solution)/shard_map/ppermute | solution.py:506
  41.5 3.6 %collective-permute-start.10 = (f32[1,48,128]{2,1,0:T(8,128)S(1)}, f32[1,48,128]{2,1,0:T(8,128)S(1)}, u32[]{:S(2)}, u32[]{:S(2)}) collective-permute-start(f32[1,48,128]{2,1,0:T(8,128)S(1)} %add_add_fusion.refs_0_), channel_id=1, source_target_pairs={{0,8},{4,12},{8,0},{12,4},{1,9},{5,13},{9,1},{13,5},{2,10},{6,14},... | collective-permute-start | bytes 73736 | tf_op jit(solution)/shard_map/ppermute | solution.py:506
  42.8 4.5 %collective-permute-start.9 = (f32[1,48,128]{2,1,0:T(8,128)S(1)}, f32[1,48,128]{2,1,0:T(8,128)S(1)}, u32[]{:S(2)}, u32[]{:S(2)}) collective-permute-start(f32[1,48,128]{2,1,0:T(8,128)S(1)} %add_add_fusion.refs_0_), channel_id=1, source_target_pairs={{0,4},{4,8},{8,12},{12,0},{1,5},{5,9},{9,13},{13,1},{2,6},{6,10},{... | collective-permute-start | bytes 73736 | tf_op jit(solution)/shard_map/ppermute | solution.py:506
  51.3 2.9 %collective-permute-start.14 = (f32[1,8,128]{2,1,0:T(8,128)S(1)}, f32[1,8,128]{2,1,0:T(8,128)S(1)}, u32[]{:S(2)}, u32[]{:S(2)}) collective-permute-start(f32[1,8,128]{2,1,0:T(8,128)S(1)} %solve.1.refs_0_), channel_id=1, source_target_pairs={{0,1},{1,2},{2,3},{3,0},{4,5},{5,6},{6,7},{7,4},{8,9},{9,10},{10,1... | collective-permute-start | bytes 12296 | tf_op jit(solution)/shard_map/ppermute | solution.py:506
  53.5 2.5 %collective-permute-start.13 = (f32[1,8,128]{2,1,0:T(8,128)S(1)}, f32[1,8,128]{2,1,0:T(8,128)S(1)}, u32[]{:S(2)}, u32[]{:S(2)}) collective-permute-start(f32[1,8,128]{2,1,0:T(8,128)S(1)} %solve.1.refs_0_), channel_id=1, source_target_pairs={{0,2},{1,3},{2,0},{3,1},{4,6},{5,7},{6,4},{7,5},{8,10},{9,11},{10,... | collective-permute-start | bytes 12296 | tf_op jit(solution)/shard_map/ppermute | solution.py:506
  54.1 3.0 %collective-permute-start.12 = (f32[1,8,128]{2,1,0:T(8,128)S(1)}, f32[1,8,128]{2,1,0:T(8,128)S(1)}, u32[]{:S(2)}, u32[]{:S(2)}) collective-permute-start(f32[1,8,128]{2,1,0:T(8,128)S(1)} %solve.1.refs_0_), channel_id=1, source_target_pairs={{0,3},{1,0},{2,1},{3,2},{4,7},{5,4},{6,5},{7,6},{8,11},{9,8},{10,9... | collective-permute-start | bytes 12296 | tf_op jit(solution)/shard_map/ppermute | solution.py:506
